TPU v7x, 32 devices: a whole 2x2x4 slice. The times are simulated.
32 devices in a mesh: groups: 2 (over x), store: 16 (over z, y, core), tensor: 1.
Axes of the slice: x: 2, y: 2, z: 4, core: 2. Of those that a mesh axis runs over, the one named last changes fastest.
Arguments:
- tokens: bfloat16 [24576, 8192], P(('groups', 'store'), 'tensor'), parts along dimension 0, may hold values from -6 to 6
- base_weight: bfloat16 [8192, 1024], P('tensor'), may hold values from -0.0625 to 0.0625
- shrink_factors: bfloat16 [64, 16, 8192], P(('groups', 'store'), None, 'tensor'), parts along dimension 0, may hold values from -0.0625 to 0.0625
- expand_factors: bfloat16 [64, 16, 1024], P(('groups', 'store')), parts along dimension 0, may hold values from -1.5 to 1.5
- home_rows: int32 [64], P('groups'), parts along dimension 0, may hold values from 0 to 31, as said below
- requests: int32 [32, 8], P(('groups', 'store')), parts along dimension 0, may hold values from 0 to 31, as said below
- block_slot: int32 [32, 48], P(('groups', 'store')), parts along dimension 0, may hold values from 0 to 7, never falling along the last dimension, each value on 1 to 12 neighbouring positions
Outputs:
- projected: bfloat16 [24576, 1024], P(('groups', 'store', 'tensor')), parts along dimension 0
There are 2 independent parts, one for each index of `groups`. A program takes and returns all parts, laid end to end along the dimension named above; an argument that names none is the same for every part. Nothing has to cross between parts.
Inputs may be any that keep to these rules, and one draw needn't show every extreme that they name: A permutation: adapter a is stored in row home_rows[a], on storing device home_rows[a] // 2. `requests`: the 8 adapters of one replica lie on 8 different storing devices; one storing device holds a request of every replica. `block_slot`: never falling along a replica's blocks; every slot owns 1 to 12 consecutive blocks.
All inputs are finite; a program needn't handle non-finite values.
Results may differ from a plain program's by a relative error of at most 0.001.
Values may be sent and summed in bfloat16 or wider, within the bound.
No kernel may reach another device: no remote copies, remote signals or barrier semaphores. Data moves between devices by JAX's collectives and lax.ppermute only.
A program may use at most 128 MiB of HBM per device.

v0:
```python
import jax
import jax.numpy as jnp
from jax import lax
from jax.sharding import PartitionSpec as P


def shards(tokens, base_weight, shrink_factors, expand_factors, home_rows, requests, block_slot):
    slot_count = requests.shape[1]
    rank_size = shrink_factors.shape[1]
    width_half = shrink_factors.shape[2]
    key_width = expand_factors.shape[2]
    rows_here = tokens.shape[0]
    adapter_total = home_rows.shape[0]
    wanted_ids = requests[0]
    match_table = wanted_ids[:, None] == jnp.arange(adapter_total, dtype=jnp.int32)[None, :]
    stored = jnp.sum(jnp.where(match_table, home_rows[None, :], 0), axis=1)
    piece_shrink = lax.all_gather(shrink_factors, "store", axis=0, tiled=True)
    piece_expand = lax.all_gather(expand_factors, "store", axis=0, tiled=True)
    count = piece_shrink.shape[0]
    positions = jnp.arange(count, dtype=jnp.int32)
    chooser = (stored[:, None] == positions[None, :]).astype(jnp.bfloat16)
    add_shrink = jnp.einsum(
        "sc,crd->srd", chooser, piece_shrink, preferred_element_type=jnp.float32
    )
    add_expand = jnp.einsum(
        "sc,crd->srd", chooser, piece_expand, preferred_element_type=jnp.float32
    )
    chosen_shrink = add_shrink
    chosen_expand = add_expand
    chosen_shrink = chosen_shrink.astype(jnp.bfloat16)
    chosen_expand = chosen_expand.astype(jnp.bfloat16)
    flat_shrink = chosen_shrink.reshape(slot_count * rank_size, width_half)
    flat_expand = chosen_expand.reshape(slot_count * rank_size, key_width).astype(jnp.float32)
    blocks_here = block_slot.shape[1]
    slot_of_row = jnp.broadcast_to(block_slot[0][:, None], (blocks_here, 16)).reshape(rows_here)
    column_slot = jnp.arange(slot_count * rank_size, dtype=jnp.int32) // rank_size
    row_mask = (slot_of_row[:, None] == column_slot[None, :]).astype(jnp.float32)
    shrink_part = (
        lax.dot_general(
            tokens, flat_shrink, (((1,), (1,)), ((), ())), preferred_element_type=jnp.float32
        )
        * row_mask
    )
    own_rows = rows_here // lax.axis_size("tensor")
    shrink_whole = lax.psum(shrink_part, "tensor")
    base_own = lax.psum_scatter(
        jnp.dot(tokens, base_weight, preferred_element_type=jnp.float32),
        "tensor",
        scatter_dimension=0,
        tiled=True,
    )
    own_shrink = lax.dynamic_slice_in_dim(
        shrink_whole, lax.axis_index("tensor") * own_rows, own_rows, 0
    )
    summed = base_own + jnp.dot(own_shrink, flat_expand, precision=lax.Precision.HIGHEST)
    return summed.astype(jnp.bfloat16)


def solution(mesh):
    placed = (
        P(("groups", "store"), "tensor"),
        P("tensor", None),
        P(("groups", "store"), None, "tensor"),
        P(("groups", "store"), None, None),
        P("groups"),
        P(("groups", "store"), None),
        P(("groups", "store"), None),
    )
    return jax.shard_map(
        shards,
        mesh=mesh,
        in_specs=placed,
        out_specs=P(("groups", "store", "tensor"), None),
        check_vma=False,
    )
```

profile of v0, /device:TPU:0, one launch (start us, length us, event | category | flops | bytes accessed | tf_op | source)
XLA Modules:
  0.0 170.4 jit_solution(11723882076136555303)
XLA Ops:
  6.5 0.0 all-gather.5.cloned.1.call-start
  6.5 0.7 all-gather.5.cloned.1.call-update
  7.3 0.0 all-gather.3.cloned.1.call-start
  7.3 0.7 all-gather.3.cloned.1.call-update
  8.0 0.7 broadcast_in_dim.25
  8.7 0.1 eq.43
  8.8 0.9 select_reduce_fusion
  9.7 40.5 %all-gather.5.cloned.1.call-done = bf16[32,16,1024]{2,1,0:T(8,128)(2,1)} async-done(((bf16[2,16,1024]{2,1,0:T(8,128)(2,1)}), bf16[32,16,1024]{2,1,0:T(8,128)(2,1)}) %all-gather.5.cloned.1.call-update) | async-done | bytes 1048592 | tf_op jit(solution)/shard_map/all_gather | solution.py:18
  50.2 2.4 %convolution_convert_fusion.1 = bf16[8,16,1024]{2,0,1:T(8,128)(2,1)S(1)} fusion(bf16[32,16,1024]{2,1,0:T(8,128)(2,1)} %all-gather.5.cloned.1.call-done, s32[8]{0:T(128)S(1)} %select_reduce_fusion), kind=kOutput, calls=%fused_computation.4 | convolution fusion | flops 8519936 | bytes 1310752 | tf_op jit(solution)/shard_map/sc,crd->srd/dot_general | solution.py:25
  52.6 0.9 copy.21
  53.5 72.7 %all-gather.3.cloned.1.call-done = bf16[32,16,8192]{2,1,0:T(8,128)(2,1)} async-done(((bf16[2,16,8192]{2,1,0:T(8,128)(2,1)}), bf16[32,16,8192]{2,1,0:T(8,128)(2,1)}) %all-gather.3.cloned.1.call-update) | async-done | bytes 8388624 | tf_op jit(solution)/shard_map/all_gather | solution.py:17
  126.2 0.0 copy-start
  126.2 12.5 %convolution_convert_fusion = bf16[8,16,8192]{2,0,1:T(8,128)(2,1)S(1)} fusion(bf16[32,16,8192]{2,1,0:T(8,128)(2,1)} %all-gather.3.cloned.1.call-done, s32[8]{0:T(128)S(1)} %select_reduce_fusion), kind=kOutput, calls=%fused_computation | convolution fusion | flops 68157696 | bytes 10485792 | tf_op jit(solution)/shard_map/sc,crd->srd/dot_general | solution.py:22
  138.7 1.3 copy.19
  140.0 0.0 copy-done
  140.0 4.3 %fusion.1 = f32[768,128]{0,1:T(8,128)S(1)} fusion(bf16[128,8192]{1,0:T(8,128)(2,1)S(1)} %bitcast.18, bf16[768,8192]{1,0:T(8,128)(2,1)S(1)} %copy-done, s32[768]{0:T(1024)S(1)} %eq.43, s32[128]{0:T(128)S(1)} %and_select_fusion), kind=kOutput, calls=%fused_computation.5 | convolution fusion | flops 1610809344 | bytes 15076864 | tf_op jit(solution)/shard_map/dot_general | solution.py:39
  144.3 2.4 %fusion.8 = f32[768,1024]{1,0:T(8,128)S(1)} fusion(f32[768,128]{0,1:T(8,128)S(1)} %fusion.1, bf16[128,1024]{1,0:T(8,128)(2,1)} %bitcast.19), kind=kOutput, calls=%fused_computation.17 | convolution fusion | flops 1207959552 | bytes 3801088 | tf_op jit(solution)/shard_map/dot_general | solution.py:55
  146.7 16.8 %add_convert_fusion = bf16[768,1024]{1,0:T(8,128)(2,1)} fusion(f32[768,1024]{1,0:T(8,128)S(1)} %fusion.8, bf16[768,8192]{1,0:T(8,128)(2,1)S(1)} %copy-done, bf16[8192,1024]{1,0:T(8,128)(2,1)} %param.8), kind=kOutput, calls=%fused_computation.2 | convolution fusion | flops 12886474752 | bytes 34078720 | tf_op jit(solution)/shard_map/dot_general | solution.py:47
  (1 shorter events, 0.0 us)
Async XLA Ops:
  6.5 43.7 %all-gather.5.cloned.1.call-start = ((), (), s32[]{:S(2)}) async-start(), calls=%async_computation.1 | async-start | bytes 1114112 | tf_op jit(solution)/shard_map/all_gather | solution.py:18
  7.3 118.9 %all-gather.3.cloned.1.call-start = ((), (), s32[]{:S(2)}) async-start(), calls=%async_computation | async-start | bytes 8912896 | tf_op jit(solution)/shard_map/all_gather | solution.py:17
  126.2 13.8 %copy-start = (bf16[768,8192]{1,0:T(8,128)(2,1)S(1)}, bf16[768,8192]{1,0:T(8,128)(2,1)}, u32[]{:S(2)}) copy-start(bf16[768,8192]{1,0:T(8,128)(2,1)} %param.7) | copy-start | bytes 37748740
Sparse Core Ops, SparseCore 0:
  9.5 40.6 all-gather.4
  52.4 73.8 all-gather.2
where the time goes:
time: 171 us; the launch traced here: 170 us
  waiting for transfers between devices  115 us (67%)
  matrix products  38.4 us (22%)
  between operations  13.4 us (8%)
  local copies, waits for them, and re-layouts  3 us (2%)
    all_gather x1, waiting for transfers between devices, shards(): piece_shrink = lax.all_gather(shrink_factors, 'store', axis=0, tiled=True)  72.7 us
    all_gather x1, waiting for transfers between devices, shards(): piece_expand = lax.all_gather(expand_factors, 'store', axis=0, tiled=True)  40.5 us
    dot_general x1, matrix products, shards(): jnp.dot(tokens, base_weight, preferred_element_type=jnp.float32)  16.8 us
    dot_general x1, matrix products, shards(): jnp.einsum('sc,crd->srd', chooser, piece_shrink, preferred_element_type=j...  12.5 us
    dot_general x1, matrix products, shards(): lax.dot_general(tokens, flat_shrink, (((1,), (1,)), ((), ())), preferred_...  4.29 us
  transfers between devices with their start and end apart: 2, of which 2 were waited for; matrix products, arithmetic and copies ran while one was open for 3% of the time, Pallas kernels for 0%

commit v1 on v0

v1 whole, which is shorter than its diff:
```python
import functools

import jax
import jax.numpy as jnp
from jax import lax
from jax.experimental import pallas as pl
from jax.experimental.pallas import tpu as pltpu
from jax.sharding import PartitionSpec as P


def general(tokens, base_weight, shrink_factors, expand_factors, home_rows, requests, block_slot):
    slot_count = requests.shape[1]
    rank = shrink_factors.shape[1]
    width = shrink_factors.shape[2]
    rows_here = tokens.shape[0]
    wanted = requests[0]
    adapters = jnp.arange(home_rows.shape[0], dtype=jnp.int32)
    stored = jnp.sum(jnp.where(wanted[:, None] == adapters[None, :], home_rows[None, :], 0), axis=1)
    both = jnp.concatenate([shrink_factors, expand_factors], axis=2)
    everyone = lax.all_gather(both, "store", axis=0, tiled=True)
    picked = jnp.concatenate(
        [lax.dynamic_slice_in_dim(everyone, stored[s], 1, 0) for s in range(slot_count)], axis=0
    ).reshape(slot_count * rank, -1)
    slot_of_row = jnp.broadcast_to(block_slot[0][:, None], (block_slot.shape[1], 16)).reshape(rows_here)
    column_slot = jnp.arange(slot_count * rank, dtype=jnp.int32) // rank
    mask = (slot_of_row[:, None] == column_slot[None, :]).astype(jnp.float32)
    shrink = lax.dot_general(
        tokens, picked[:, :width], (((1,), (1,)), ((), ())), preferred_element_type=jnp.float32
    )
    shrink = lax.psum_scatter(shrink * mask, "tensor", scatter_dimension=0, tiled=True)
    base = lax.psum_scatter(
        jnp.dot(tokens, base_weight, preferred_element_type=jnp.float32),
        "tensor",
        scatter_dimension=0,
        tiled=True,
    )
    expand = jnp.dot(shrink, picked[:, width:].astype(jnp.float32), precision=lax.Precision.HIGHEST)
    return (base + expand).astype(jnp.bfloat16)


def final_kernel(pieces, sel, tokens, mask, *rest):
    bases, bufs, (out, total, table) = rest[:pieces], rest[pieces:-3], rest[-3:]
    step, last = pl.program_id(0), pl.num_programs(0) - 1
    for i, buf in enumerate(bufs):
        table[pl.ds(16 * i, 16), :] = buf[0]

    @pl.when(step == 0)
    def _():
        total[...] = jnp.zeros_like(total)

    @pl.when(step < last)
    def _():
        total[...] += lax.dot_general(
            tokens[...], table[...], (((1,), (1,)), ((), ())), preferred_element_type=jnp.float32
        )

    @pl.when(step == last)
    def _():
        shrink = total[...] * mask[...].astype(jnp.float32)
        high = shrink.astype(jnp.bfloat16)
        low = (shrink - high.astype(jnp.float32)).astype(jnp.bfloat16)
        wide = out.shape[1] // pieces
        for i, base in enumerate(bases):
            cols = pl.ds(wide * i, wide)
            part = jnp.dot(high, table[:, cols], preferred_element_type=jnp.float32)
            part += jnp.dot(low, table[:, cols], preferred_element_type=jnp.float32)
            out[:, cols] = (base[...] + part).astype(out.dtype)


def finish(sel, tokens, mask, bases, bufs, key_width):
    rows, width = tokens.shape
    rank = bufs[0].shape[1]
    assert width % key_width == 0
    steps = width // key_width
    columns = rank * len(bufs)

    def chosen(i, k, sel):
        return (sel[i], 0, k)

    whole = lambda k, sel: (0, 0)
    return pl.pallas_call(
        functools.partial(final_kernel, len(bases)),
        out_shape=jax.ShapeDtypeStruct((rows, key_width), jnp.bfloat16),
        grid_spec=pltpu.PrefetchScalarGridSpec(
            num_scalar_prefetch=1,
            grid=(steps + 1,),
            in_specs=[
                pl.BlockSpec((rows, key_width), lambda k, sel: (0, jnp.minimum(k, steps - 1))),
                pl.BlockSpec((rows, columns), whole),
            ]
            + [pl.BlockSpec(b.shape, whole) for b in bases]
            + [
                pl.BlockSpec((1, rank, key_width), functools.partial(chosen, i))
                for i in range(len(bufs))
            ],
            out_specs=pl.BlockSpec((rows, key_width), whole),
            scratch_shapes=[
                pltpu.VMEM((rows, columns), jnp.float32),
                pltpu.VMEM((columns, key_width), jnp.bfloat16),
            ],
        ),
        compiler_params=pltpu.CompilerParams(
            dimension_semantics=("arbitrary",), vmem_limit_bytes=40 << 20
        ),
        cost_estimate=pl.CostEstimate(
            flops=2 * rows * width * columns, bytes_accessed=2 * rows * width, transcendentals=0
        ),
        name="shrink_expand",
    )(sel, tokens, mask, *bases, *bufs)


def gridded(tokens, base_weight, shrink_factors, expand_factors, home_rows, requests, block_slot):
    held, rank, width = shrink_factors.shape
    key_width = expand_factors.shape[2]
    rows_here = tokens.shape[0]
    me = lax.axis_index("store")
    z, y, c = me // 4, me // 2 % 2, me % 2
    inner = (z == 1) | (z == 2)

    def along_z(moves):
        return [(4 * a + r, 4 * b + r) for a, b in moves for r in range(4)]

    def along_y(levels):
        return [(4 * a + r, 4 * a + (r ^ 2)) for a in levels for r in range(4)]

    cores = [(i, i ^ 1) for i in range(16)]
    pairs = along_z([(0, 1), (1, 0), (2, 3), (3, 2)])
    middle = along_z([(1, 2), (2, 1)])
    outward = along_z([(1, 0), (2, 3)])
    send = lambda a, p: lax.ppermute(a, "store", p)

    own = jnp.concatenate([shrink_factors, expand_factors], axis=2)
    p1 = send(own, pairs)
    y0 = send(own, along_y(range(4)))
    p2 = send(own, middle)
    p4 = send(p2, outward)
    p3 = send(p1, middle)
    y1 = send(p1, along_y(range(4)))
    y2 = send(p2, along_y([1, 2]))
    p5 = send(p3, outward)
    y4 = send(p4, along_y([0, 3]))
    y3 = send(p3, along_y([1, 2]))
    y5 = send(p5, along_y([0, 3]))
    either = lambda a, b: jnp.where(inner, a, b)
    mine = [own, p1, y0, y1, either(p2, p4), either(p3, p5), either(y2, y4), either(y3, y5)]
    theirs = [send(b, cores) for b in mine]

    second = jnp.where(z < 2, 2, 1)
    third = jnp.where(z < 2, 3, 0)
    chip = lambda level, side: 2 * level + side
    chips = jnp.stack(
        [
            chip(z, y), chip(z ^ 1, y), chip(z, y ^ 1), chip(z ^ 1, y ^ 1),
            chip(second, y), chip(third, y), chip(second, y ^ 1), chip(third, y ^ 1),
        ]
    )
    source = jnp.concatenate([2 * chips + c, 2 * chips + 1 - c]).astype(jnp.int32)
    adapters = jnp.arange(home_rows.shape[0], dtype=jnp.int32)
    stored = jnp.sum(
        jnp.where(requests[0][:, None] == adapters[None, :], home_rows[None, :], 0), axis=1
    )
    hit = source[:, None] == (stored // held)[None, :]
    sel = jnp.sum(jnp.where(hit, (stored % held)[None, :], 0), axis=1)
    slots = jnp.arange(requests.shape[1], dtype=jnp.int32)
    column_slot = jnp.max(jnp.where(hit, slots[None, :], -1), axis=1)
    column_slot = jnp.broadcast_to(column_slot[:, None], (source.shape[0], rank)).reshape(-1)
    row_slot = jnp.broadcast_to(block_slot[0][:, None], (block_slot.shape[1], 16)).reshape(rows_here)
    mask = (row_slot[:, None] == column_slot[None, :]).astype(jnp.bfloat16)

    pieces = 4
    wide = key_width // pieces
    bases = [
        jnp.dot(
            tokens, base_weight[:, wide * i : wide * (i + 1)], preferred_element_type=jnp.float32
        )
        for i in range(pieces)
    ]
    return finish(sel, tokens, mask, bases, mine + theirs, key_width)


def solution(mesh):
    placed = (
        P(("groups", "store"), "tensor"),
        P("tensor", None),
        P(("groups", "store"), None, "tensor"),
        P(("groups", "store"), None, None),
        P("groups"),
        P(("groups", "store"), None),
        P(("groups", "store"), None),
    )
    by_grid = mesh.shape["tensor"] == 1 and mesh.shape["store"] == 16
    return jax.shard_map(
        gridded if by_grid else general,
        mesh=mesh,
        in_specs=placed,
        out_specs=P(("groups", "store", "tensor"), None),
        check_vma=False,
    )
```

time: 171 us -> 122 us (0.71)
  waiting for transfers between devices: 115 us -> 47 us
  starting transfers between devices: 0.04 us -> 20.4 us
  between operations: 13.4 us -> 0.29 us
  Pallas kernels: 0 us -> 13 us
  matrix products: 38.4 us -> 25.5 us
  local copies, waits for them, and re-layouts: 3 us -> 12.8 us
    all_gather x2 -> x0, waiting for transfers between devices: 113 us -> none  [the longest x1 72.7 us: shards(): piece_shrink = lax.all_gather(shrink_factors, 'store', axis=0, tiled=True)]
    ppermute x0 -> x19, waiting for transfers between devices: none -> 47 us  [gridded(): send = lambda a, p: lax.ppermute(a, 'store', p)]
    ppermute x0 -> x19, starting transfers between devices: none -> 20.4 us  [gridded(): send = lambda a, p: lax.ppermute(a, 'store', p)]
    pallas_call x0 -> x1, Pallas kernels: none -> 13 us  [finish(): pl.pallas_call(functools.partial(final_kernel, len(bases)), out_shape=jax...]
    dot_general x5 -> x4, matrix products: 38.4 us -> 25.5 us  [gridded(): jnp.dot(tokens, base_weight[:, wide * i:wide * (i + 1)], preferred_elemen...]
    unnamed x2 -> x35, local copies, waits for them, and re-layouts: 0.01 us -> 9.47 us
    convert_element_type x2 -> x0, local copies, waits for them, and re-layouts: 2.19 us -> none  [the longest x1 1.34 us: shards(): chosen_shrink = chosen_shrink.astype(jnp.bfloat16)]
  transfers between devices with their start and end apart: 2 -> 19, of which waited for: 2 -> 4; matrix products, arithmetic and copies ran while one was open for 3% -> 25% of each run, Pallas kernels for 0% -> 0%
where the time goes in v1:
time: 122 us; the launch traced here: 121 us
  waiting for transfers between devices  47 us (39%)
  matrix products  25.5 us (21%)
  starting transfers between devices  20.4 us (17%)
  Pallas kernels  13 us (11%)
  local copies, waits for them, and re-layouts  12.8 us (10%)
  other arithmetic  1.86 us (2%)
    ppermute x19, waiting for transfers between devices, gridded(): send = lambda a, p: lax.ppermute(a, 'store', p)  47 us
    dot_general x4, matrix products, gridded(): jnp.dot(tokens, base_weight[:, wide * i:wide * (i + 1)], preferred_elemen...  25.5 us
    ppermute x19, starting transfers between devices, gridded(): send = lambda a, p: lax.ppermute(a, 'store', p)  20.4 us
    pallas_call x1, Pallas kernels, finish(): pl.pallas_call(functools.partial(final_kernel, len(bases)), out_shape=jax...  13 us
    unnamed x35, local copies, waits for them, and re-layouts  9.47 us
  transfers between devices with their start and end apart: 19, of which 4 were waited for; matrix products, arithmetic and copies ran while one was open for 25% of the time, Pallas kernels for 0%

profile of v1, /device:TPU:0, one launch (start us, length us, event | category | flops | bytes accessed | tf_op | source)
XLA Modules:
  0.0 120.9 jit_solution(10915786856786220158)
XLA Ops:
  0.0 1.1 constant_dynamic-update-slice_fusion.1
  1.1 1.0 constant_dynamic-update-slice_fusion.rest_4_
  2.6 0.8 collective-permute-start.3
  3.4 2.6 %collective-permute-start.1 = (bf16[2,16,9216]{2,1,0:T(8,128)(2,1)S(1)}, bf16[2,16,9216]{2,1,0:T(8,128)(2,1)}, u32[]{:S(2)}, u32[]{:S(2)}) collective-permute-start(bf16[2,16,9216]{2,1,0:T(8,128)(2,1)S(1)} %constant_dynamic-update-slice_fusion.rest_4_), channel_id=1, source_target_pairs={{0,2},{1,3},{2,0},{3,1},{4,6},{5,7},{6,4},{7,5},{8,10},{9,11},{10,... | collective-permute-start | bytes 1769480 | tf_op jit(solution)/shard_map/ppermute | solution.py:130
  6.0 4.5 %collective-permute-start = (bf16[2,16,9216]{2,1,0:T(8,128)(2,1)S(1)}, bf16[2,16,9216]{2,1,0:T(8,128)(2,1)}, u32[]{:S(2)}, u32[]{:S(2)}) collective-permute-start(bf16[2,16,9216]{2,1,0:T(8,128)(2,1)S(1)} %constant_dynamic-update-slice_fusion.rest_4_), channel_id=1, source_target_pairs={{0,4},{1,5},{2,6},{3,7},{4,0},{5,1},{6,2},{7,3},{8,12},{9,13},{10,... | collective-permute-start | bytes 1769480 | tf_op jit(solution)/shard_map/ppermute | solution.py:130
  10.5 10.2 %fusion.4.rest_1_ = f32[768,256]{1,0:T(8,128)} fusion(bf16[768,8192]{1,0:T(8,128)(2,1)} %tokens.1, bf16[8192,1024]{1,0:T(8,128)(2,1)} %param.8), kind=kOutput, calls=%fused_computation.4 | convolution fusion | flops 3221225472 | bytes 17563648 | tf_op jit(solution)/shard_map/dot_general | solution.py:173
  20.8 6.7 %fusion.6.rest_0_ = f32[768,256]{1,0:T(8,128)} fusion(bf16[768,8192]{1,0:T(8,128)(2,1)S(1)} %bitcast.15, bf16[8192,1024]{1,0:T(8,128)(2,1)} %param.8), kind=kOutput, calls=%fused_computation.6 | convolution fusion | flops 3221225472 | bytes 17563648 | tf_op jit(solution)/shard_map/dot_general | solution.py:173
  27.5 4.3 %fusion.rest_3_ = f32[768,256]{1,0:T(8,128)} fusion(bf16[768,8192]{1,0:T(8,128)(2,1)S(1)} %bitcast.15, bf16[8192,1024]{1,0:T(8,128)(2,1)S(1)} %bitcast.18), kind=kOutput, calls=%fused_computation | convolution fusion | flops 3221225472 | bytes 17563648 | tf_op jit(solution)/shard_map/dot_general | solution.py:173
  31.9 1.4 %collective-permute-start.4 = (bf16[2,16,9216]{2,1,0:T(8,128)(2,1)S(1)}, bf16[2,16,9216]{2,1,0:T(8,128)(2,1)}, u32[]{:S(2)}, u32[]{:S(2)}) collective-permute-start(bf16[2,16,9216]{2,1,0:T(8,128)(2,1)S(1)} %collective-permute-done.3), channel_id=1, source_target_pairs={{4,0},{5,1},{6,2},{7,3},{8,12},{9,13},{10,14},{11,15},{20,16},{21,... | collective-permute-start | bytes 1769480 | tf_op jit(solution)/shard_map/ppermute | solution.py:130
  33.3 0.9 collective-permute-start.5
  34.2 4.3 %fusion.2.rest_2_ = f32[768,256]{1,0:T(8,128)} fusion(bf16[768,8192]{1,0:T(8,128)(2,1)S(1)} %bitcast.15, bf16[8192,1024]{1,0:T(8,128)(2,1)S(1)} %bitcast.18), kind=kOutput, calls=%fused_computation.2 | convolution fusion | flops 3221225472 | bytes 17563648 | tf_op jit(solution)/shard_map/dot_general | solution.py:173
  38.7 0.7 collective-permute-start.7
  39.5 9.4 %collective-permute-done.4 = bf16[2,16,9216]{2,1,0:T(8,128)(2,1)} collective-permute-done((bf16[2,16,9216]{2,1,0:T(8,128)(2,1)S(1)}, bf16[2,16,9216]{2,1,0:T(8,128)(2,1)}, u32[]{:S(2)}, u32[]{:S(2)}) %collective-permute-start.4) | collective-permute-done | bytes 589856 | tf_op jit(solution)/shard_map/ppermute | solution.py:130
  49.4 1.3 %collective-permute-start.6 = (bf16[2,16,9216]{2,1,0:T(8,128)(2,1)S(1)}, bf16[2,16,9216]{2,1,0:T(8,128)(2,1)S(1)}, u32[]{:S(2)}, u32[]{:S(2)}) collective-permute-start(bf16[2,16,9216]{2,1,0:T(8,128)(2,1)S(1)} %collective-permute-done.5), channel_id=1, source_target_pairs={{4,0},{5,1},{6,2},{7,3},{8,12},{9,13},{10,14},{11,15},{20,16},{21,... | collective-permute-start | bytes 1769480 | tf_op jit(solution)/shard_map/ppermute | solution.py:130
  50.7 1.1 broadcast_select_fusion.3.rest_8_
  51.8 14.8 %collective-permute-done.6 = bf16[2,16,9216]{2,1,0:T(8,128)(2,1)S(1)} collective-permute-done((bf16[2,16,9216]{2,1,0:T(8,128)(2,1)S(1)}, bf16[2,16,9216]{2,1,0:T(8,128)(2,1)S(1)}, u32[]{:S(2)}, u32[]{:S(2)}) %collective-permute-start.6) | collective-permute-done | bytes 589856 | tf_op jit(solution)/shard_map/ppermute | solution.py:130
  66.6 2.4 %collective-permute-start.8 = (bf16[2,16,9216]{2,1,0:T(8,128)(2,1)}, bf16[2,16,9216]{2,1,0:T(8,128)(2,1)S(1)}, u32[]{:S(2)}, u32[]{:S(2)}) collective-permute-start(bf16[2,16,9216]{2,1,0:T(8,128)(2,1)} %collective-permute-done.4), channel_id=1, source_target_pairs={{0,2},{1,3},{2,0},{3,1},{12,14},{13,15},{14,12},{15,13},{16,18},{1... | collective-permute-start | bytes 1769480 | tf_op jit(solution)/shard_map/ppermute | solution.py:130
  69.1 0.7 collective-permute-start.9
  69.8 11.9 %collective-permute-done.8 = bf16[2,16,9216]{2,1,0:T(8,128)(2,1)S(1)} collective-permute-done((bf16[2,16,9216]{2,1,0:T(8,128)(2,1)}, bf16[2,16,9216]{2,1,0:T(8,128)(2,1)S(1)}, u32[]{:S(2)}, u32[]{:S(2)}) %collective-permute-start.8) | collective-permute-done | bytes 589856 | tf_op jit(solution)/shard_map/ppermute | solution.py:130
  81.7 2.4 %collective-permute-start.10 = (bf16[2,16,9216]{2,1,0:T(8,128)(2,1)S(1)}, bf16[2,16,9216]{2,1,0:T(8,128)(2,1)S(1)}, u32[]{:S(2)}, u32[]{:S(2)}) collective-permute-start(bf16[2,16,9216]{2,1,0:T(8,128)(2,1)S(1)} %collective-permute-done.6), channel_id=1, source_target_pairs={{0,2},{1,3},{2,0},{3,1},{12,14},{13,15},{14,12},{15,13},{16,18},{1... | collective-permute-start | bytes 1769480 | tf_op jit(solution)/shard_map/ppermute | solution.py:130
  84.9 10.8 %collective-permute-done.10 = bf16[2,16,9216]{2,1,0:T(8,128)(2,1)S(1)} collective-permute-done((bf16[2,16,9216]{2,1,0:T(8,128)(2,1)S(1)}, bf16[2,16,9216]{2,1,0:T(8,128)(2,1)S(1)}, u32[]{:S(2)}, u32[]{:S(2)}) %collective-permute-start.10) | collective-permute-done | bytes 589856 | tf_op jit(solution)/shard_map/ppermute | solution.py:130
  96.4 0.8 copy-done.6
  97.2 0.9 copy-done.4
  98.9 1.3 %broadcast_in_dim.56 = s32[48,16]{1,0:T(8,128)} broadcast(s32[48]{0:T(128)} %bitcast.16), dimensions={0} | broadcast | bytes 3264 | tf_op jit(solution)/shard_map/broadcast_in_dim | solution.py:167
  100.3 0.8 eq.63
  101.3 1.1 copy-done
  102.5 1.1 copy-done.1
  103.6 1.1 copy-done.2
  104.7 1.1 copy-done.3
  105.9 1.1 copy-done.5
  106.9 1.1 copy-done.7
  108.0 13.0 %shrink_expand.1 = bf16[768,1024]{1,0:T(8,128)(2,1)} custom-call(s32[16]{0:T(128)S(1)} %get-tuple-element.6.sel, bf16[768,8192]{1,0:T(8,128)(2,1)} %tokens.1, bf16[768,256]{1,0:T(8,128)(2,1)S(1)} %compare_convert_fusion.mask, f32[768,256]{1,0:T(8,128)S(1)} %copy-done.1, f32[768,256]{1,0:T(8,128)S(1)} %copy-done, f32[768,256]{1,0:T(8,128)S(1)} %copy-done.3, ...), custom_call_target="tpu_custom_call" | custom-call | flops 3221225472 | bytes 12582912 | tf_op jit(solution)/shard_map/shrink_expand/pallas_call | solution.py:81
  (64 shorter events, 3.8 us)
Async XLA Ops:
  1.1 19.7 %slice-start = ((s8[12582912]{0:T(1024)(128)(4,1)}), s8[4194304]{0:T(1024)(128)(4,1)S(1)}, s32[]{:S(2)}) async-start(s8[12582912]{0:T(1024)(128)(4,1)} %bitcast.14), calls=%async_computation | async-start | bytes 8388608
  2.1 18.7 %slice-start.1 = ((s8[12582912]{0:T(1024)(128)(4,1)}), s8[4194304]{0:T(1024)(128)(4,1)S(1)}, s32[]{:S(2)}) async-start(s8[12582912]{0:T(1024)(128)(4,1)} %bitcast.14), calls=%async_computation.1 | async-start | bytes 8388608
  2.1 18.7 %slice-start.2 = ((s8[12582912]{0:T(1024)(128)(4,1)}), s8[4194304]{0:T(1024)(128)(4,1)S(1)}, s32[]{:S(2)}) async-start(s8[12582912]{0:T(1024)(128)(4,1)} %bitcast.14), calls=%async_computation.2 | async-start | bytes 8388608
  2.1 93.7 %collective-permute-start.11 = (bf16[2,16,9216]{2,1,0:T(8,128)(2,1)S(1)}, bf16[2,16,9216]{2,1,0:T(8,128)(2,1)S(1)}, u32[]{:S(2)}, u32[]{:S(2)}) collective-permute-start(bf16[2,16,9216]{2,1,0:T(8,128)(2,1)S(1)} %constant_dynamic-update-slice_fusion.rest_4_), channel_id=1, source_target_pairs={{0,1},{1,0},{2,3},{3,2},{4,5},{5,4},{6,7},{7,6},{8,9},{9,8},{10,11... | collective-permute-start | bytes 1769480 | tf_op jit(solution)/shard_map/ppermute | solution.py:130
  2.6 29.2 %collective-permute-start.3 = (bf16[2,16,9216]{2,1,0:T(8,128)(2,1)S(1)}, bf16[2,16,9216]{2,1,0:T(8,128)(2,1)S(1)}, u32[]{:S(2)}, u32[]{:S(2)}) collective-permute-start(bf16[2,16,9216]{2,1,0:T(8,128)(2,1)S(1)} %constant_dynamic-update-slice_fusion.rest_4_), channel_id=1, source_target_pairs={{4,8},{5,9},{6,10},{7,11},{8,4},{9,5},{10,6},{11,7},{20,24},{21,25... | collective-permute-start | bytes 1769480 | tf_op jit(solution)/shard_map/ppermute | solution.py:130
  3.4 80.8 %collective-permute-start.1 = (bf16[2,16,9216]{2,1,0:T(8,128)(2,1)S(1)}, bf16[2,16,9216]{2,1,0:T(8,128)(2,1)}, u32[]{:S(2)}, u32[]{:S(2)}) collective-permute-start(bf16[2,16,9216]{2,1,0:T(8,128)(2,1)S(1)} %constant_dynamic-update-slice_fusion.rest_4_), channel_id=1, source_target_pairs={{0,2},{1,3},{2,0},{3,1},{4,6},{5,7},{6,4},{7,5},{8,10},{9,11},{10,... | collective-permute-start | bytes 1769480 | tf_op jit(solution)/shard_map/ppermute | solution.py:130
  6.0 27.2 %collective-permute-start = (bf16[2,16,9216]{2,1,0:T(8,128)(2,1)S(1)}, bf16[2,16,9216]{2,1,0:T(8,128)(2,1)}, u32[]{:S(2)}, u32[]{:S(2)}) collective-permute-start(bf16[2,16,9216]{2,1,0:T(8,128)(2,1)S(1)} %constant_dynamic-update-slice_fusion.rest_4_), channel_id=1, source_target_pairs={{0,4},{1,5},{2,6},{3,7},{4,0},{5,1},{6,2},{7,3},{8,12},{9,13},{10,... | collective-permute-start | bytes 1769480 | tf_op jit(solution)/shard_map/ppermute | solution.py:130
  10.5 17.0 %slice-start.3 = ((s8[16777216]{0:T(1024)(128)(4,1)}), s8[4194304]{0:T(1024)(128)(4,1)S(1)}, s32[]{:S(2)}) async-start(s8[16777216]{0:T(1024)(128)(4,1)} %bitcast.17), calls=%async_computation.3 | async-start | bytes 8388608
  10.5 17.0 %slice-start.4 = ((s8[16777216]{0:T(1024)(128)(4,1)}), s8[4194304]{0:T(1024)(128)(4,1)S(1)}, s32[]{:S(2)}) async-start(s8[16777216]{0:T(1024)(128)(4,1)} %bitcast.17), calls=%async_computation.4 | async-start | bytes 8388608
  20.8 6.7 %slice-start.5 = ((s8[16777216]{0:T(1024)(128)(4,1)}), s8[4194304]{0:T(1024)(128)(4,1)S(1)}, s32[]{:S(2)}) async-start(s8[16777216]{0:T(1024)(128)(4,1)} %bitcast.17), calls=%async_computation.5 | async-start | bytes 8388608
  20.8 6.7 %slice-start.6 = ((s8[16777216]{0:T(1024)(128)(4,1)}), s8[4194304]{0:T(1024)(128)(4,1)S(1)}, s32[]{:S(2)}) async-start(s8[16777216]{0:T(1024)(128)(4,1)} %bitcast.17), calls=%async_computation.6 | async-start | bytes 8388608
  31.8 6.7 %copy-start.8 = (s32[32]{0:T(128)S(1)}, s32[32]{0:T(128)}, u32[]{:S(2)}) copy-start(s32[32]{0:T(128)} %param.11) | copy-start | bytes 388
  31.8 6.7 %copy-start.9 = (s32[1,8]{1,0:T(1,128)S(1)}, s32[1,8]{1,0:T(1,128)}, u32[]{:S(2)}) copy-start(s32[1,8]{1,0:T(1,128)} %param.12) | copy-start | bytes 100
  31.9 17.0 %collective-permute-start.4 = (bf16[2,16,9216]{2,1,0:T(8,128)(2,1)S(1)}, bf16[2,16,9216]{2,1,0:T(8,128)(2,1)}, u32[]{:S(2)}, u32[]{:S(2)}) collective-permute-start(bf16[2,16,9216]{2,1,0:T(8,128)(2,1)S(1)} %collective-permute-done.3), channel_id=1, source_target_pairs={{4,0},{5,1},{6,2},{7,3},{8,12},{9,13},{10,14},{11,15},{20,16},{21,... | collective-permute-start | bytes 1769480 | tf_op jit(solution)/shard_map/ppermute | solution.py:130
  33.3 16.1 %collective-permute-start.5 = (bf16[2,16,9216]{2,1,0:T(8,128)(2,1)}, bf16[2,16,9216]{2,1,0:T(8,128)(2,1)S(1)}, u32[]{:S(2)}, u32[]{:S(2)}) collective-permute-start(bf16[2,16,9216]{2,1,0:T(8,128)(2,1)} %collective-permute-done.rest_5_), channel_id=1, source_target_pairs={{4,8},{5,9},{6,10},{7,11},{8,4},{9,5},{10,6},{11,7},{20,24},{21,25... | collective-permute-start | bytes 1769480 | tf_op jit(solution)/shard_map/ppermute | solution.py:130
  38.7 30.4 %collective-permute-start.7 = (bf16[2,16,9216]{2,1,0:T(8,128)(2,1)S(1)}, bf16[2,16,9216]{2,1,0:T(8,128)(2,1)S(1)}, u32[]{:S(2)}, u32[]{:S(2)}) collective-permute-start(bf16[2,16,9216]{2,1,0:T(8,128)(2,1)S(1)} %collective-permute-done.3), channel_id=1, source_target_pairs={{4,6},{5,7},{6,4},{7,5},{8,10},{9,11},{10,8},{11,9},{20,22},{21,23... | collective-permute-start | bytes 1769480 | tf_op jit(solution)/shard_map/ppermute | solution.py:130
  48.9 35.5 %collective-permute-start.2 = (bf16[2,16,9216]{2,1,0:T(8,128)(2,1)}, bf16[2,16,9216]{2,1,0:T(8,128)(2,1)}, u32[]{:S(2)}, u32[]{:S(2)}) collective-permute-start(bf16[2,16,9216]{2,1,0:T(8,128)(2,1)} %collective-permute-done.rest_5_), channel_id=1, source_target_pairs={{0,2},{1,3},{2,0},{3,1},{4,6},{5,7},{6,4},{7,5},{8,10},{9,11},{10,... | collective-permute-start | bytes 1769480 | tf_op jit(solution)/shard_map/ppermute | solution.py:130
  49.4 17.3 %collective-permute-start.6 = (bf16[2,16,9216]{2,1,0:T(8,128)(2,1)S(1)}, bf16[2,16,9216]{2,1,0:T(8,128)(2,1)S(1)}, u32[]{:S(2)}, u32[]{:S(2)}) collective-permute-start(bf16[2,16,9216]{2,1,0:T(8,128)(2,1)S(1)} %collective-permute-done.5), channel_id=1, source_target_pairs={{4,0},{5,1},{6,2},{7,3},{8,12},{9,13},{10,14},{11,15},{20,16},{21,... | collective-permute-start | bytes 1769480 | tf_op jit(solution)/shard_map/ppermute | solution.py:130
  66.6 15.1 %collective-permute-start.8 = (bf16[2,16,9216]{2,1,0:T(8,128)(2,1)}, bf16[2,16,9216]{2,1,0:T(8,128)(2,1)S(1)}, u32[]{:S(2)}, u32[]{:S(2)}) collective-permute-start(bf16[2,16,9216]{2,1,0:T(8,128)(2,1)} %collective-permute-done.4), channel_id=1, source_target_pairs={{0,2},{1,3},{2,0},{3,1},{12,14},{13,15},{14,12},{15,13},{16,18},{1... | collective-permute-start | bytes 1769480 | tf_op jit(solution)/shard_map/ppermute | solution.py:130
  69.1 15.7 %collective-permute-start.9 = (bf16[2,16,9216]{2,1,0:T(8,128)(2,1)S(1)}, bf16[2,16,9216]{2,1,0:T(8,128)(2,1)S(1)}, u32[]{:S(2)}, u32[]{:S(2)}) collective-permute-start(bf16[2,16,9216]{2,1,0:T(8,128)(2,1)S(1)} %collective-permute-done.5), channel_id=1, source_target_pairs={{4,6},{5,7},{6,4},{7,5},{8,10},{9,11},{10,8},{11,9},{20,22},{21,23... | collective-permute-start | bytes 1769480 | tf_op jit(solution)/shard_map/ppermute | solution.py:130
  81.7 14.0 %collective-permute-start.10 = (bf16[2,16,9216]{2,1,0:T(8,128)(2,1)S(1)}, bf16[2,16,9216]{2,1,0:T(8,128)(2,1)S(1)}, u32[]{:S(2)}, u32[]{:S(2)}) collective-permute-start(bf16[2,16,9216]{2,1,0:T(8,128)(2,1)S(1)} %collective-permute-done.6), channel_id=1, source_target_pairs={{0,2},{1,3},{2,0},{3,1},{12,14},{13,15},{14,12},{15,13},{16,18},{1... | collective-permute-start | bytes 1769480 | tf_op jit(solution)/shard_map/ppermute | solution.py:130
  84.2 13.0 %collective-permute-start.12 = (bf16[2,16,9216]{2,1,0:T(8,128)(2,1)}, bf16[2,16,9216]{2,1,0:T(8,128)(2,1)S(1)}, u32[]{:S(2)}, u32[]{:S(2)}) collective-permute-start(bf16[2,16,9216]{2,1,0:T(8,128)(2,1)} %collective-permute-done.rest_5_), channel_id=1, source_target_pairs={{0,1},{1,0},{2,3},{3,2},{4,5},{5,4},{6,7},{7,6},{8,9},{9,8},{10,11... | collective-permute-start | bytes 1769480 | tf_op jit(solution)/shard_map/ppermute | solution.py:130
  84.3 12.1 %collective-permute-start.13 = (bf16[2,16,9216]{2,1,0:T(8,128)(2,1)}, bf16[2,16,9216]{2,1,0:T(8,128)(2,1)S(1)}, u32[]{:S(2)}, u32[]{:S(2)}) collective-permute-start(bf16[2,16,9216]{2,1,0:T(8,128)(2,1)} %collective-permute-done.1.rest_6_), channel_id=1, source_target_pairs={{0,1},{1,0},{2,3},{3,2},{4,5},{5,4},{6,7},{7,6},{8,9},{9,8},{10,11... | collective-permute-start | bytes 1769480 | tf_op jit(solution)/shard_map/ppermute | solution.py:130
  84.8 16.4 %collective-permute-start.15 = (bf16[2,16,9216]{2,1,0:T(8,128)(2,1)S(1)}, bf16[2,16,9216]{2,1,0:T(8,128)(2,1)}, u32[]{:S(2)}, u32[]{:S(2)}) collective-permute-start(bf16[2,16,9216]{2,1,0:T(8,128)(2,1)S(1)} %broadcast_select_fusion.3.rest_8_), channel_id=1, source_target_pairs={{0,1},{1,0},{2,3},{3,2},{4,5},{5,4},{6,7},{7,6},{8,9},{9,8},{10,11... | collective-permute-start | bytes 1769480 | tf_op jit(solution)/shard_map/ppermute | solution.py:130
  95.7 5.5 %collective-permute-start.14 = (bf16[2,16,9216]{2,1,0:T(8,128)(2,1)}, bf16[2,16,9216]{2,1,0:T(8,128)(2,1)}, u32[]{:S(2)}, u32[]{:S(2)}) collective-permute-start(bf16[2,16,9216]{2,1,0:T(8,128)(2,1)} %collective-permute-done.2.rest_7_), channel_id=1, source_target_pairs={{0,1},{1,0},{2,3},{3,2},{4,5},{5,4},{6,7},{7,6},{8,9},{9,8},{10,11... | collective-permute-start | bytes 1769480 | tf_op jit(solution)/shard_map/ppermute | solution.py:130
  95.8 5.5 %collective-permute-start.17 = (bf16[2,16,9216]{2,1,0:T(8,128)(2,1)S(1)}, bf16[2,16,9216]{2,1,0:T(8,128)(2,1)}, u32[]{:S(2)}, u32[]{:S(2)}) collective-permute-start(bf16[2,16,9216]{2,1,0:T(8,128)(2,1)S(1)} %broadcast_select_fusion.1.rest_10_), channel_id=1, source_target_pairs={{0,1},{1,0},{2,3},{3,2},{4,5},{5,4},{6,7},{7,6},{8,9},{9,8},{10,11... | collective-permute-start | bytes 1769480 | tf_op jit(solution)/shard_map/ppermute | solution.py:130
  97.2 4.1 %collective-permute-start.16 = (bf16[2,16,9216]{2,1,0:T(8,128)(2,1)S(1)}, bf16[2,16,9216]{2,1,0:T(8,128)(2,1)}, u32[]{:S(2)}, u32[]{:S(2)}) collective-permute-start(bf16[2,16,9216]{2,1,0:T(8,128)(2,1)S(1)} %broadcast_select_fusion.2.rest_9_), channel_id=1, source_target_pairs={{0,1},{1,0},{2,3},{3,2},{4,5},{5,4},{6,7},{7,6},{8,9},{9,8},{10,11... | collective-permute-start | bytes 1769480 | tf_op jit(solution)/shard_map/ppermute | solution.py:130
  98.1 3.2 %collective-permute-start.18 = (bf16[2,16,9216]{2,1,0:T(8,128)(2,1)S(1)}, bf16[2,16,9216]{2,1,0:T(8,128)(2,1)}, u32[]{:S(2)}, u32[]{:S(2)}) collective-permute-start(bf16[2,16,9216]{2,1,0:T(8,128)(2,1)S(1)} %broadcast_select_fusion.rest_11_), channel_id=1, source_target_pairs={{0,1},{1,0},{2,3},{3,2},{4,5},{5,4},{6,7},{7,6},{8,9},{9,8},{10,11... | collective-permute-start | bytes 1769480 | tf_op jit(solution)/shard_map/ppermute | solution.py:130
  101.3 1.1 copy-start
  102.5 1.1 copy-start.1
  103.6 1.1 copy-start.2
  104.7 1.1 copy-start.3
  (4 other events, 3.8 us)

commit v2 on v1

v2 whole, which is shorter than its diff:
```python
import functools

import jax
import jax.numpy as jnp
from jax import lax
from jax.experimental import pallas as pl
from jax.experimental.pallas import tpu as pltpu
from jax.sharding import PartitionSpec as P


def general(tokens, base_weight, shrink_factors, expand_factors, home_rows, requests, block_slot):
    slot_count = requests.shape[1]
    rank = shrink_factors.shape[1]
    width = shrink_factors.shape[2]
    rows_here = tokens.shape[0]
    wanted = requests[0]
    adapters = jnp.arange(home_rows.shape[0], dtype=jnp.int32)
    stored = jnp.sum(jnp.where(wanted[:, None] == adapters[None, :], home_rows[None, :], 0), axis=1)
    both = jnp.concatenate([shrink_factors, expand_factors], axis=2)
    everyone = lax.all_gather(both, "store", axis=0, tiled=True)
    picked = jnp.concatenate(
        [lax.dynamic_slice_in_dim(everyone, stored[s], 1, 0) for s in range(slot_count)], axis=0
    ).reshape(slot_count * rank, -1)
    slot_of_row = jnp.broadcast_to(block_slot[0][:, None], (block_slot.shape[1], 16)).reshape(rows_here)
    column_slot = jnp.arange(slot_count * rank, dtype=jnp.int32) // rank
    mask = (slot_of_row[:, None] == column_slot[None, :]).astype(jnp.float32)
    shrink = lax.dot_general(
        tokens, picked[:, :width], (((1,), (1,)), ((), ())), preferred_element_type=jnp.float32
    )
    shrink = lax.psum_scatter(shrink * mask, "tensor", scatter_dimension=0, tiled=True)
    base = lax.psum_scatter(
        jnp.dot(tokens, base_weight, preferred_element_type=jnp.float32),
        "tensor",
        scatter_dimension=0,
        tiled=True,
    )
    expand = jnp.dot(shrink, picked[:, width:].astype(jnp.float32), precision=lax.Precision.HIGHEST)
    return (base + expand).astype(jnp.bfloat16)


def base_kernel(depth, after, tokens, weight, out):
    step = pl.program_id(0)

    @pl.when(step == 0)
    def _():
        out[...] = jnp.zeros_like(out)

    depth_here = weight.shape[0]
    columns = pl.ds(pl.multiple_of(step * depth, 128), depth_here)
    out[...] += jnp.dot(tokens[:, columns], weight[...], preferred_element_type=jnp.float32)


def base_part(after, tokens, weight, part, parts, streamed=False):
    rows, width = tokens.shape
    wide = weight.shape[1] // parts
    steps = 4
    depth = width // steps
    home = pltpu.HBM if streamed else pltpu.VMEM
    tokens = pltpu.with_memory_space_constraint(tokens, home)
    weight = pltpu.with_memory_space_constraint(weight, pltpu.HBM)
    return pl.pallas_call(
        functools.partial(base_kernel, 0 if streamed else depth),
        out_shape=jax.ShapeDtypeStruct((rows, wide), jnp.float32),
        grid=(steps,),
        in_specs=[
            pl.BlockSpec(memory_space=pl.ANY),
            pl.BlockSpec((rows, depth), lambda k: (0, k))
            if streamed
            else pl.BlockSpec(memory_space=pltpu.VMEM),
            pl.BlockSpec((depth, wide), lambda k: (k, part)),
        ],
        out_specs=pl.BlockSpec((rows, wide), lambda k: (0, 0)),
        compiler_params=pltpu.CompilerParams(
            dimension_semantics=("arbitrary",), vmem_limit_bytes=16 << 20
        ),
        cost_estimate=pl.CostEstimate(
            flops=2 * rows * width * wide, bytes_accessed=2 * width * wide, transcendentals=0
        ),
        name=f"base{part}",
    )(after, tokens, weight)


def finish(choice, tokens, mask, bases, batches, given):
    rows, width = tokens.shape
    _, rank, whole = batches[0][0][0].shape
    key_width = whole - width
    count = len(batches) + len(given)
    last = choice.shape[0] - 1
    pieces = len(bases)
    entries = [entry for batch in batches for entry in batch] + given
    arrays, spots = listed(entries)
    owners = [(i, k, len(batch) > 2) for i, batch in enumerate(batches) for k in range(len(batch))]
    owners += [(len(batches) + i, None, False) for i in range(len(given))]
    places = [(i, buf, row, k, levels) for (i, k, levels), (buf, row) in zip(owners, spots)]
    half = whole // 2

    def kernel(choice, tokens, mask, *rest):
        base_refs, bufs = rest[:pieces], rest[pieces:-3]
        out, table, arrived = rest[-3:]

        def copy(i, buf, row, part):
            columns = pl.ds(half * part, half)
            return pltpu.make_async_copy(
                bufs[buf].at[row, :, columns],
                table.at[pl.ds(rank * i, rank), columns],
                arrived.at[part, i],
            )

        for part in range(2):
            for i, buf, row, k, levels in places:
                if k is None:
                    copy(i, buf, row, part).start()
                else:
                    want = choice[i] == k % 2
                    if levels:
                        want = want & (choice[last] == k // 2)
                    pl.when(want)(copy(i, buf, row, part).start)
        total = None
        for part in range(2):
            for i in range(count):
                copy(i, 0, 0, part).wait()
            columns = pl.ds(half * part, min(half, width - half * part))
            term = lax.dot_general(
                tokens[:, columns],
                table[:, columns],
                (((1,), (1,)), ((), ())),
                preferred_element_type=jnp.float32,
            )
            total = term if total is None else total + term
        shrink = total * mask[...].astype(jnp.float32)
        high = shrink.astype(jnp.bfloat16)
        low = (shrink - high.astype(jnp.float32)).astype(jnp.bfloat16)
        wide = key_width // pieces
        for i, base in enumerate(base_refs):
            cols = pl.ds(width + wide * i, wide)
            part = jnp.dot(high, table[:, cols], preferred_element_type=jnp.float32)
            part += jnp.dot(low, table[:, cols], preferred_element_type=jnp.float32)
            out[:, pl.ds(wide * i, wide)] = (base[...] + part).astype(out.dtype)

    vmem = pl.BlockSpec(memory_space=pltpu.VMEM)
    pin = lambda a: pltpu.with_memory_space_constraint(a, pltpu.VMEM)
    return pl.pallas_call(
        kernel,
        out_shape=jax.ShapeDtypeStruct((rows, key_width), jnp.bfloat16),
        in_specs=[pl.BlockSpec(memory_space=pltpu.SMEM)]
        + [vmem] * (2 + pieces)
        + [pl.BlockSpec(memory_space=pl.ANY)] * len(arrays),
        out_specs=vmem,
        scratch_shapes=[
            pltpu.VMEM((rank * count, whole), jnp.bfloat16),
            pltpu.SemaphoreType.DMA((2, count)),
        ],
        compiler_params=pltpu.CompilerParams(vmem_limit_bytes=24 << 20),
        cost_estimate=pl.CostEstimate(
            flops=2 * rows * width * rank * count,
            bytes_accessed=2 * whole * rank * count,
            transcendentals=0,
        ),
        name="shrink_expand",
    )(choice, pin(tokens), pin(mask), *map(pin, bases), *arrays)


def join_kernel(shrink, expand, out):
    width = shrink.shape[2]
    out[:, :, pl.ds(0, width)] = shrink[...]
    out[:, :, pl.ds(width, expand.shape[2])] = expand[...]


def joined(shrink, expand):
    held, rank, width = shrink.shape
    vmem = pl.BlockSpec(memory_space=pltpu.VMEM)
    return pl.pallas_call(
        join_kernel,
        out_shape=jax.ShapeDtypeStruct((held, rank, width + expand.shape[2]), shrink.dtype),
        in_specs=[vmem] * 2,
        out_specs=vmem,
        compiler_params=pltpu.CompilerParams(vmem_limit_bytes=8 << 20),
        name="join",
    )(shrink, expand)


def listed(entries):
    arrays, places = [], []
    for array, row in entries:
        known = [array is other for other in arrays]
        if True not in known:
            arrays.append(array)
            known.append(True)
        places.append((known.index(True), row))
    return arrays, places


def picked(choice, ids, batches):
    arrays, places = listed([entry for i in ids for entry in batches[i]])
    _, rank, whole = arrays[0].shape
    last = choice.shape[0] - 1
    held = 2

    def kernel(choice, *refs):
        out, n = refs[-1], 0
        for place, i in enumerate(ids):
            for k in range(len(batches[i])):
                want = choice[i] == k % held
                if len(batches[i]) > held:
                    want = want & (choice[last] == k // held)
                array, row = places[n]
                n += 1

                @pl.when(want)
                def _(place=place, array=array, row=row):
                    out[place] = refs[array][row]

    vmem = pl.BlockSpec(memory_space=pltpu.VMEM)
    return pl.pallas_call(
        kernel,
        out_shape=jax.ShapeDtypeStruct((len(ids), rank, whole), arrays[0].dtype),
        in_specs=[pl.BlockSpec(memory_space=pltpu.SMEM)] + [vmem] * len(arrays),
        out_specs=vmem,
        compiler_params=pltpu.CompilerParams(vmem_limit_bytes=16 << 20),
        name="pick" + "_".join(map(str, ids)),
    )(choice, *(pltpu.with_memory_space_constraint(a, pltpu.VMEM) for a in arrays))


def gridded(tokens, base_weight, shrink_factors, expand_factors, home_rows, requests, block_slot):
    held, rank, width = shrink_factors.shape
    rows_here = tokens.shape[0]
    me = lax.axis_index("store")
    z, y, c = me // 4, me // 2 % 2, me % 2
    inner = (z == 1) | (z == 2)

    def along_z(moves):
        return [(4 * a + r, 4 * b + r) for a, b in moves for r in range(4)]

    def along_y(levels):
        return [(4 * a + r, 4 * a + (r ^ 2)) for a in levels for r in range(4)]

    cores = [(i, i ^ 1) for i in range(16)]
    pairs = along_z([(0, 1), (1, 0), (2, 3), (3, 2)])
    middle = along_z([(1, 2), (2, 1)])
    outward = along_z([(1, 0), (2, 3)])
    inward = along_z([(0, 1), (3, 2)])
    every, outer_y, inner_y = along_y(range(4)), along_y([0, 3]), along_y([1, 2])
    send = lambda a, p: lax.ppermute(a, "store", p)
    together = lax.optimization_barrier

    own = joined(shrink_factors, expand_factors)
    p1, p2, y0 = send(own, pairs), send(own, middle), send(own, every)

    adapters = jnp.arange(home_rows.shape[0], dtype=jnp.int32)
    stored = jnp.sum(
        jnp.where(requests[0][:, None] == adapters[None, :], home_rows[None, :], 0), axis=1
    )
    stored_other = send(stored, cores)
    second = jnp.where(z < 2, 2, 1)
    third = jnp.where(z < 2, 3, 0)
    chip = lambda level, side: 2 * level + side
    chips = jnp.stack(
        [
            chip(z, y), chip(z ^ 1, y), chip(z, y ^ 1), chip(z ^ 1, y ^ 1),
            chip(second, y), chip(third, y), chip(second, y ^ 1), chip(third, y ^ 1),
        ]
    )
    here = (2 * chips + c).astype(jnp.int32)
    source = jnp.concatenate([here, (2 * chips + 1 - c).astype(jnp.int32)])
    hit = source[:, None] == (stored // held)[None, :]
    slots = jnp.arange(requests.shape[1], dtype=jnp.int32)
    column_slot = jnp.max(jnp.where(hit, slots[None, :], -1), axis=1)
    column_slot = jnp.broadcast_to(column_slot[:, None], (source.shape[0], rank)).reshape(-1)
    row_slot = jnp.broadcast_to(block_slot[0][:, None], (block_slot.shape[1], 16)).reshape(rows_here)
    mask = (row_slot[:, None] == column_slot[None, :]).astype(jnp.bfloat16)

    def second_wanted(rows):
        return jnp.max(
            jnp.where(here[:, None] == (rows // held)[None, :], (rows % held)[None, :], 0), axis=1
        )

    level = inner.astype(jnp.int32)[None]
    take_mine = jnp.concatenate([second_wanted(stored), level])
    take_other = jnp.concatenate([second_wanted(stored_other), level])

    pieces = 2
    after = lambda *a: together((take_mine, *a))[0]
    part = lambda i, order: base_part(order, tokens, base_weight, i, pieces)
    base0 = base_part(take_mine, tokens, base_weight, 0, pieces, streamed=True)
    p1, p2, y0, base0, mask, take_mine, take_other = together(
        (p1, p2, y0, base0, mask, take_mine, take_other)
    )
    p4, p3 = send(p2, outward), send(p1, middle)
    y1a, y1b = send(p1[:1], every), send(p1[1:], outer_y)
    w1 = send(y0[1:], inward)
    y2 = send(p2, inner_y)
    base1 = part(1, after(p1))
    p4, p3, base1 = together((p4, p3, base1))
    p5a, p5b = send(p3[:1], outward), send(p3[1:], outward)
    y4, y3a = send(p4, outer_y), send(p3[:1], inner_y)
    w2 = send(w1, middle)
    y5a = send(p5a, outer_y)
    w3 = send(w2, outward)

    batches = [
        [(own, 0), (own, 1)],
        [(p1, 0), (p1, 1)],
        [(y0, 0), (y0, 1)],
        [(y1a, 0), (y1b, 0), (y1a, 0), (w1, 0)],
        [(p4, 0), (p4, 1), (p2, 0), (p2, 1)],
        [(p5a, 0), (p5b, 0), (p3, 0), (p3, 1)],
        [(y4, 0), (y4, 1), (y2, 0), (y2, 1)],
        [(y5a, 0), (w3, 0), (y3a, 0), (w2, 0)],
    ]
    given = []
    for ids in ((0, 1, 2, 3, 4), (5, 6), (7,)):
        sent = send(picked(take_other, ids, batches), cores)
        given += [(sent, row) for row in range(len(ids))]
    return finish(take_mine, tokens, mask, [base0, base1], batches, given)


def solution(mesh):
    placed = (
        P(("groups", "store"), "tensor"),
        P("tensor", None),
        P(("groups", "store"), None, "tensor"),
        P(("groups", "store"), None, None),
        P("groups"),
        P(("groups", "store"), None),
        P(("groups", "store"), None),
    )
    by_grid = mesh.shape["tensor"] == 1 and mesh.shape["store"] == 16
    return jax.shard_map(
        gridded if by_grid else general,
        mesh=mesh,
        in_specs=placed,
        out_specs=P(("groups", "store", "tensor"), None),
        check_vma=False,
    )
```

time: 122 us -> 96.4 us (0.79)
  matrix products: 25.5 us -> 0 us
  Pallas kernels: 13 us -> 34.8 us
  waiting for transfers between devices: 47 us -> 26.4 us
  local copies, waits for them, and re-layouts: 12.8 us -> 3.05 us
  starting transfers between devices: 20.4 us -> 29.7 us
    dot_general x4 -> x0, matrix products: 25.5 us -> none  [gridded(): jnp.dot(tokens, base_weight[:, wide * i:wide * (i + 1)], preferred_elemen...]
    pallas_call x1 -> x7, Pallas kernels: 13 us -> 34.8 us  [the longest x2 20.7 us: base_part(): pl.pallas_call(functools.partial(base_kernel, 0 if streamed else depth),...]
    ppermute x19 -> x20, waiting for transfers between devices: 47 us -> 26.4 us  [gridded(): send = lambda a, p: lax.ppermute(a, 'store', p)]
    ppermute x19 -> x20, starting transfers between devices: 20.4 us -> 29.7 us  [gridded(): send = lambda a, p: lax.ppermute(a, 'store', p)]
    unnamed x35 -> x10, local copies, waits for them, and re-layouts: 9.47 us -> 1.89 us
    select_n x5 -> x2, other arithmetic: 1.34 us -> 0.02 us  [second_wanted(): rows // held]
  transfers between devices with their start and end apart: 19 -> 20, of which waited for: 4 -> 6; matrix products, arithmetic and copies ran while one was open for 25% -> 3% of each run, Pallas kernels for 0% -> 24%
where the time goes in v2:
time: 96.4 us; the launch traced here: 95.9 us
  Pallas kernels  34.8 us (36%)
  starting transfers between devices  29.7 us (31%)
  waiting for transfers between devices  26.4 us (27%)
  local copies, waits for them, and re-layouts  3.05 us (3%)
  other arithmetic  1.49 us (2%)
    ppermute x20, starting transfers between devices, gridded(): send = lambda a, p: lax.ppermute(a, 'store', p)  29.7 us
    ppermute x20, waiting for transfers between devices, gridded(): send = lambda a, p: lax.ppermute(a, 'store', p)  26.4 us
    pallas_call x2, Pallas kernels, base_part(): pl.pallas_call(functools.partial(base_kernel, 0 if streamed else depth),...  20.7 us
    pallas_call x1, Pallas kernels, finish(): pl.pallas_call(kernel, out_shape=jax.ShapeDtypeStruct((rows, key_width),...  12.1 us
    pallas_call x3, Pallas kernels, picked(): pl.pallas_call(kernel, out_shape=jax.ShapeDtypeStruct((len(ids), rank, wh...  1.96 us
  transfers between devices with their start and end apart: 20, of which 6 were waited for; matrix products, arithmetic and copies ran while one was open for 3% of the time, Pallas kernels for 24%

profile of v2, /device:TPU:0, one launch (start us, length us, event | category | flops | bytes accessed | tf_op | source)
XLA Modules:
  0.0 95.9 jit_solution(9440422873901026893)
XLA Ops:
  0.0 1.0 %copy-done = bf16[2,16,8192]{2,1,0:T(8,128)(2,1)S(1)} copy-done((bf16[2,16,8192]{2,1,0:T(8,128)(2,1)S(1)}, bf16[2,16,8192]{2,1,0:T(8,128)(2,1)}, u32[]{:S(2)}) %copy-start) | copy-done | bytes 524312
  1.0 0.8 copy-done.1
  1.9 3.0 %collective-permute-start.2 = (bf16[2,16,9216]{2,1,0:T(8,128)(2,1)S(1)}, bf16[2,16,9216]{2,1,0:T(8,128)(2,1)S(1)}, u32[]{:S(2)}, u32[]{:S(2)}) collective-permute-start(bf16[2,16,9216]{2,1,0:T(8,128)(2,1)S(1)} %join.1.refs_0_.rest_2_), channel_id=1, source_target_pairs={{0,2},{1,3},{2,0},{3,1},{4,6},{5,7},{6,4},{7,5},{8,10},{9,11},{10,... | collective-permute-start | bytes 1769480 | tf_op jit(solution)/shard_map/ppermute | solution.py:243
  5.0 0.7 collective-permute-start.1
  5.7 4.4 %collective-permute-start = (bf16[2,16,9216]{2,1,0:T(8,128)(2,1)S(1)}, bf16[2,16,9216]{2,1,0:T(8,128)(2,1)S(1)}, u32[]{:S(2)}, u32[]{:S(2)}) collective-permute-start(bf16[2,16,9216]{2,1,0:T(8,128)(2,1)S(1)} %join.1.refs_0_.rest_2_), channel_id=1, source_target_pairs={{0,4},{1,5},{2,6},{3,7},{4,0},{5,1},{6,2},{7,3},{8,12},{9,13},{10,... | collective-permute-start | bytes 1769480 | tf_op jit(solution)/shard_map/ppermute | solution.py:243
  10.1 0.9 select_reduce_fusion.3
  11.5 0.7 broadcast_in_dim.79
  12.8 11.8 %base0.1.rest_0_ = f32[768,512]{1,0:T(8,128)S(1)} custom-call(s32[9]{0:T(128)S(1)} %get-tuple-element.21.after.choice, bf16[768,8192]{1,0:T(8,128)(2,1)} %tokens.5, bf16[8192,1024]{1,0:T(8,128)(2,1)} %weight.3), custom_call_target="tpu_custom_call" | custom-call | flops 6442450944 | bytes 8388608 | tf_op jit(solution)/shard_map/base0/pallas_call | solution.py:61
  24.7 0.7 collective-permute-start.5
  25.4 3.6 %collective-permute-start.8 = (bf16[1,16,9216]{2,1,0:T(8,128)(2,1)S(1)}, bf16[1,16,9216]{2,1,0:T(8,128)(2,1)S(1)}, u32[]{:S(2)}, u32[]{:S(2)}) collective-permute-start(bf16[1,16,9216]{2,1,0:T(8,128)(2,1)S(1)} %slice.18), channel_id=1, source_target_pairs={{0,4},{1,5},{2,6},{3,7},{12,8},{13,9},{14,10},{15,11},{16,20},{17,... | collective-permute-start | bytes 884744 | tf_op jit(solution)/shard_map/ppermute | solution.py:243
  29.0 2.4 %collective-permute-start.7 = (bf16[1,16,9216]{2,1,0:T(8,128)(2,1)S(1)}, bf16[1,16,9216]{2,1,0:T(8,128)(2,1)S(1)}, u32[]{:S(2)}, u32[]{:S(2)}) collective-permute-start(bf16[1,16,9216]{2,1,0:T(8,128)(2,1)S(1)} %get-tuple-element.31), channel_id=1, source_target_pairs={{0,2},{1,3},{2,0},{3,1},{12,14},{13,15},{14,12},{15,13},{16,18},{1... | collective-permute-start | bytes 884744 | tf_op jit(solution)/shard_map/ppermute | solution.py:243
  31.4 1.6 %collective-permute-start.6 = (bf16[1,16,9216]{2,1,0:T(8,128)(2,1)S(1)}, bf16[1,16,9216]{2,1,0:T(8,128)(2,1)S(1)}, u32[]{:S(2)}, u32[]{:S(2)}) collective-permute-start(bf16[1,16,9216]{2,1,0:T(8,128)(2,1)S(1)} %get-tuple-element.32), channel_id=1, source_target_pairs={{0,2},{1,3},{2,0},{3,1},{4,6},{5,7},{6,4},{7,5},{8,10},{9,11},{10,... | collective-permute-start | bytes 884744 | tf_op jit(solution)/shard_map/ppermute | solution.py:243
  33.0 1.3 %collective-permute-start.4 = (bf16[2,16,9216]{2,1,0:T(8,128)(2,1)S(1)}, bf16[2,16,9216]{2,1,0:T(8,128)(2,1)S(1)}, u32[]{:S(2)}, u32[]{:S(2)}) collective-permute-start(bf16[2,16,9216]{2,1,0:T(8,128)(2,1)S(1)} %collective-permute-done.1.refs_7_.rest_9_), channel_id=1, source_target_pairs={{4,0},{5,1},{6,2},{7,3},{8,12},{9,13},{10,14},{11,15},{20,16},{21,... | collective-permute-start | bytes 1769480 | tf_op jit(solution)/shard_map/ppermute | solution.py:243
  34.3 9.0 %base1.1.rest_1_ = f32[768,512]{1,0:T(8,128)S(1)} custom-call(s32[9]{0:T(128)S(1)} %get-tuple-element.21.after.choice, bf16[768,8192]{1,0:T(8,128)(2,1)S(1)} %bitcast.12, bf16[8192,1024]{1,0:T(8,128)(2,1)} %weight.3), custom_call_target="tpu_custom_call" | custom-call | flops 6442450944 | bytes 8388608 | tf_op jit(solution)/shard_map/base1/pallas_call | solution.py:61
  43.3 0.7 collective-permute-start.12
  44.0 5.4 %collective-permute-done.4.refs_6_.rest_8_ = bf16[2,16,9216]{2,1,0:T(8,128)(2,1)S(1)} collective-permute-done((bf16[2,16,9216]{2,1,0:T(8,128)(2,1)S(1)}, bf16[2,16,9216]{2,1,0:T(8,128)(2,1)S(1)}, u32[]{:S(2)}, u32[]{:S(2)}) %collective-permute-start.4) | collective-permute-done | bytes 589856 | tf_op jit(solution)/shard_map/ppermute | solution.py:243
  49.5 0.7 collective-permute-start.14
  50.2 2.4 %collective-permute-start.11 = (bf16[2,16,9216]{2,1,0:T(8,128)(2,1)S(1)}, bf16[2,16,9216]{2,1,0:T(8,128)(2,1)S(1)}, u32[]{:S(2)}, u32[]{:S(2)}) collective-permute-start(bf16[2,16,9216]{2,1,0:T(8,128)(2,1)S(1)} %collective-permute-done.4.refs_6_.rest_8_), channel_id=1, source_target_pairs={{0,2},{1,3},{2,0},{3,1},{12,14},{13,15},{14,12},{15,13},{16,18},{1... | collective-permute-start | bytes 1769480 | tf_op jit(solution)/shard_map/ppermute | solution.py:243
  52.6 0.7 pick0_1_2_3_4.1
  53.5 1.3 %collective-permute-start.10 = (bf16[1,16,9216]{2,1,0:T(8,128)(2,1)S(1)}, bf16[1,16,9216]{2,1,0:T(8,128)(2,1)S(1)}, u32[]{:S(2)}, u32[]{:S(2)}) collective-permute-start(bf16[1,16,9216]{2,1,0:T(8,128)(2,1)S(1)} %get-tuple-element.29), channel_id=1, source_target_pairs={{4,0},{5,1},{6,2},{7,3},{8,12},{9,13},{10,14},{11,15},{20,16},{21,... | collective-permute-start | bytes 884744 | tf_op jit(solution)/shard_map/ppermute | solution.py:243
  54.8 1.3 %collective-permute-start.9 = (bf16[1,16,9216]{2,1,0:T(8,128)(2,1)S(1)}, bf16[1,16,9216]{2,1,0:T(8,128)(2,1)S(1)}, u32[]{:S(2)}, u32[]{:S(2)}) collective-permute-start(bf16[1,16,9216]{2,1,0:T(8,128)(2,1)S(1)} %get-tuple-element.30), channel_id=1, source_target_pairs={{4,0},{5,1},{6,2},{7,3},{8,12},{9,13},{10,14},{11,15},{20,16},{21,... | collective-permute-start | bytes 884744 | tf_op jit(solution)/shard_map/ppermute | solution.py:243
  56.1 0.7 collective-permute-start.16
  56.8 8.4 %collective-permute-done.10.refs_1_.rest_11_ = bf16[1,16,9216]{2,1,0:T(8,128)(2,1)S(1)} collective-permute-done((bf16[1,16,9216]{2,1,0:T(8,128)(2,1)S(1)}, bf16[1,16,9216]{2,1,0:T(8,128)(2,1)S(1)}, u32[]{:S(2)}, u32[]{:S(2)}) %collective-permute-start.10) | collective-permute-done | bytes 294944 | tf_op jit(solution)/shard_map/ppermute | solution.py:243
  65.2 1.3 %collective-permute-start.15 = (bf16[1,16,9216]{2,1,0:T(8,128)(2,1)S(1)}, bf16[1,16,9216]{2,1,0:T(8,128)(2,1)S(1)}, u32[]{:S(2)}, u32[]{:S(2)}) collective-permute-start(bf16[1,16,9216]{2,1,0:T(8,128)(2,1)S(1)} %collective-permute-done.14.refs_3_.rest_18_), channel_id=1, source_target_pairs={{4,0},{5,1},{6,2},{7,3},{8,12},{9,13},{10,14},{11,15},{20,16},{21,... | collective-permute-start | bytes 884744 | tf_op jit(solution)/shard_map/ppermute | solution.py:243
  66.5 5.0 %collective-permute-done.9.refs_0_.rest_10_ = bf16[1,16,9216]{2,1,0:T(8,128)(2,1)S(1)} collective-permute-done((bf16[1,16,9216]{2,1,0:T(8,128)(2,1)S(1)}, bf16[1,16,9216]{2,1,0:T(8,128)(2,1)S(1)}, u32[]{:S(2)}, u32[]{:S(2)}) %collective-permute-start.9) | collective-permute-done | bytes 294944 | tf_op jit(solution)/shard_map/ppermute | solution.py:243
  71.5 3.4 %collective-permute-start.13 = (bf16[1,16,9216]{2,1,0:T(8,128)(2,1)S(1)}, bf16[1,16,9216]{2,1,0:T(8,128)(2,1)S(1)}, u32[]{:S(2)}, u32[]{:S(2)}) collective-permute-start(bf16[1,16,9216]{2,1,0:T(8,128)(2,1)S(1)} %collective-permute-done.9.refs_0_.rest_10_), channel_id=1, source_target_pairs={{0,2},{1,3},{2,0},{3,1},{12,14},{13,15},{14,12},{15,13},{16,18},{1... | collective-permute-start | bytes 884744 | tf_op jit(solution)/shard_map/ppermute | solution.py:243
  74.9 0.6 pick5_6.1
  75.6 1.8 %collective-permute-done.15.refs_1_.rest_16_ = bf16[1,16,9216]{2,1,0:T(8,128)(2,1)S(1)} collective-permute-done((bf16[1,16,9216]{2,1,0:T(8,128)(2,1)S(1)}, bf16[1,16,9216]{2,1,0:T(8,128)(2,1)S(1)}, u32[]{:S(2)}, u32[]{:S(2)}) %collective-permute-start.15) | collective-permute-done | bytes 294944 | tf_op jit(solution)/shard_map/ppermute | solution.py:243
  77.4 4.2 %collective-permute-done.13.refs_0_.rest_15_ = bf16[1,16,9216]{2,1,0:T(8,128)(2,1)S(1)} collective-permute-done((bf16[1,16,9216]{2,1,0:T(8,128)(2,1)S(1)}, bf16[1,16,9216]{2,1,0:T(8,128)(2,1)S(1)}, u32[]{:S(2)}, u32[]{:S(2)}) %collective-permute-start.13) | collective-permute-done | bytes 294944 | tf_op jit(solution)/shard_map/ppermute | solution.py:243
  81.6 0.6 pick7.1
  82.3 1.6 %collective-permute-done.19.rest_21_ = bf16[1,16,9216]{2,1,0:T(8,128)(2,1)S(1)} collective-permute-done((bf16[1,16,9216]{2,1,0:T(8,128)(2,1)S(1)}, bf16[1,16,9216]{2,1,0:T(8,128)(2,1)S(1)}, u32[]{:S(2)}, u32[]{:S(2)}) %collective-permute-start.19) | collective-permute-done | bytes 294944 | tf_op jit(solution)/shard_map/ppermute | solution.py:243
  83.8 12.1 %shrink_expand.1 = bf16[768,1024]{1,0:T(8,128)(2,1)} custom-call(s32[9]{0:T(128)S(1)} %get-tuple-element.21.after.choice, bf16[768,8192]{1,0:T(8,128)(2,1)S(1)} %bitcast.12, bf16[768,256]{1,0:T(8,128)(2,1)S(1)} %compare_convert_fusion.mask, f32[768,512]{1,0:T(8,128)S(1)} %base0.1.rest_0_, f32[768,512]{1,0:T(8,128)S(1)} %base1.1.rest_1_, ...), custom_call_target="tpu_custom_call" | custom-call | flops 3221225472 | bytes 4718592 | tf_op jit(solution)/shard_map/shrink_expand/pallas_call | solution.py:142
  (43 shorter events, 1.4 us)
Async XLA Ops:
  0.0 1.0 %copy-start = (bf16[2,16,8192]{2,1,0:T(8,128)(2,1)S(1)}, bf16[2,16,8192]{2,1,0:T(8,128)(2,1)}, u32[]{:S(2)}) copy-start(bf16[2,16,8192]{2,1,0:T(8,128)(2,1)} %shrink.1) | copy-start | bytes 1572868
  1.0 0.8 copy-start.1
  1.9 22.7 %collective-permute-start.2 = (bf16[2,16,9216]{2,1,0:T(8,128)(2,1)S(1)}, bf16[2,16,9216]{2,1,0:T(8,128)(2,1)S(1)}, u32[]{:S(2)}, u32[]{:S(2)}) collective-permute-start(bf16[2,16,9216]{2,1,0:T(8,128)(2,1)S(1)} %join.1.refs_0_.rest_2_), channel_id=1, source_target_pairs={{0,2},{1,3},{2,0},{3,1},{4,6},{5,7},{6,4},{7,5},{8,10},{9,11},{10,... | collective-permute-start | bytes 1769480 | tf_op jit(solution)/shard_map/ppermute | solution.py:243
  5.0 19.6 %collective-permute-start.1 = (bf16[2,16,9216]{2,1,0:T(8,128)(2,1)S(1)}, bf16[2,16,9216]{2,1,0:T(8,128)(2,1)S(1)}, u32[]{:S(2)}, u32[]{:S(2)}) collective-permute-start(bf16[2,16,9216]{2,1,0:T(8,128)(2,1)S(1)} %join.1.refs_0_.rest_2_), channel_id=1, source_target_pairs={{4,8},{5,9},{6,10},{7,11},{8,4},{9,5},{10,6},{11,7},{20,24},{21,25... | collective-permute-start | bytes 1769480 | tf_op jit(solution)/shard_map/ppermute | solution.py:243
  5.7 19.0 %collective-permute-start = (bf16[2,16,9216]{2,1,0:T(8,128)(2,1)S(1)}, bf16[2,16,9216]{2,1,0:T(8,128)(2,1)S(1)}, u32[]{:S(2)}, u32[]{:S(2)}) collective-permute-start(bf16[2,16,9216]{2,1,0:T(8,128)(2,1)S(1)} %join.1.refs_0_.rest_2_), channel_id=1, source_target_pairs={{0,4},{1,5},{2,6},{3,7},{4,0},{5,1},{6,2},{7,3},{8,12},{9,13},{10,... | collective-permute-start | bytes 1769480 | tf_op jit(solution)/shard_map/ppermute | solution.py:243
  10.9 1.6 %collective-permute-start.3 = (s32[8]{0:T(128)S(1)}, s32[8]{0:T(128)S(1)}, u32[]{:S(2)}, u32[]{:S(2)}) collective-permute-start(s32[8]{0:T(128)S(1)} %select_reduce_fusion.3), channel_id=1, source_target_pairs={{0,1},{1,0},{2,3},{3,2},{4,5},{5,4},{6,7},{7,6},{8,9},{9,8},{10,11... | collective-permute-start | bytes 104 | tf_op jit(solution)/shard_map/ppermute | solution.py:243
  12.8 21.5 %slice-start = ((s8[12582912]{0:T(1024)(128)(4,1)}), s8[4194304]{0:T(1024)(128)(4,1)S(1)}, s32[]{:S(2)}) async-start(s8[12582912]{0:T(1024)(128)(4,1)} %bitcast.11), calls=%async_computation | async-start | bytes 8388608
  12.8 21.5 %slice-start.1 = ((s8[12582912]{0:T(1024)(128)(4,1)}), s8[4194304]{0:T(1024)(128)(4,1)S(1)}, s32[]{:S(2)}) async-start(s8[12582912]{0:T(1024)(128)(4,1)} %bitcast.11), calls=%async_computation.1 | async-start | bytes 8388608
  12.8 21.5 %slice-start.2 = ((s8[12582912]{0:T(1024)(128)(4,1)}), s8[4194304]{0:T(1024)(128)(4,1)S(1)}, s32[]{:S(2)}) async-start(s8[12582912]{0:T(1024)(128)(4,1)} %bitcast.11), calls=%async_computation.2 | async-start | bytes 8388608
  24.7 25.5 %collective-permute-start.5 = (bf16[2,16,9216]{2,1,0:T(8,128)(2,1)S(1)}, bf16[2,16,9216]{2,1,0:T(8,128)(2,1)S(1)}, u32[]{:S(2)}, u32[]{:S(2)}) collective-permute-start(bf16[2,16,9216]{2,1,0:T(8,128)(2,1)S(1)} %collective-permute-done.refs_1_.rest_3_), channel_id=1, source_target_pairs={{4,8},{5,9},{6,10},{7,11},{8,4},{9,5},{10,6},{11,7},{20,24},{21,25... | collective-permute-start | bytes 1769480 | tf_op jit(solution)/shard_map/ppermute | solution.py:243
  25.4 17.9 %collective-permute-start.8 = (bf16[1,16,9216]{2,1,0:T(8,128)(2,1)S(1)}, bf16[1,16,9216]{2,1,0:T(8,128)(2,1)S(1)}, u32[]{:S(2)}, u32[]{:S(2)}) collective-permute-start(bf16[1,16,9216]{2,1,0:T(8,128)(2,1)S(1)} %slice.18), channel_id=1, source_target_pairs={{0,4},{1,5},{2,6},{3,7},{12,8},{13,9},{14,10},{15,11},{16,20},{17,... | collective-permute-start | bytes 884744 | tf_op jit(solution)/shard_map/ppermute | solution.py:243
  29.0 23.6 %collective-permute-start.7 = (bf16[1,16,9216]{2,1,0:T(8,128)(2,1)S(1)}, bf16[1,16,9216]{2,1,0:T(8,128)(2,1)S(1)}, u32[]{:S(2)}, u32[]{:S(2)}) collective-permute-start(bf16[1,16,9216]{2,1,0:T(8,128)(2,1)S(1)} %get-tuple-element.31), channel_id=1, source_target_pairs={{0,2},{1,3},{2,0},{3,1},{12,14},{13,15},{14,12},{15,13},{16,18},{1... | collective-permute-start | bytes 884744 | tf_op jit(solution)/shard_map/ppermute | solution.py:243
  31.4 21.2 %collective-permute-start.6 = (bf16[1,16,9216]{2,1,0:T(8,128)(2,1)S(1)}, bf16[1,16,9216]{2,1,0:T(8,128)(2,1)S(1)}, u32[]{:S(2)}, u32[]{:S(2)}) collective-permute-start(bf16[1,16,9216]{2,1,0:T(8,128)(2,1)S(1)} %get-tuple-element.32), channel_id=1, source_target_pairs={{0,2},{1,3},{2,0},{3,1},{4,6},{5,7},{6,4},{7,5},{8,10},{9,11},{10,... | collective-permute-start | bytes 884744 | tf_op jit(solution)/shard_map/ppermute | solution.py:243
  33.0 16.4 %collective-permute-start.4 = (bf16[2,16,9216]{2,1,0:T(8,128)(2,1)S(1)}, bf16[2,16,9216]{2,1,0:T(8,128)(2,1)S(1)}, u32[]{:S(2)}, u32[]{:S(2)}) collective-permute-start(bf16[2,16,9216]{2,1,0:T(8,128)(2,1)S(1)} %collective-permute-done.1.refs_7_.rest_9_), channel_id=1, source_target_pairs={{4,0},{5,1},{6,2},{7,3},{8,12},{9,13},{10,14},{11,15},{20,16},{21,... | collective-permute-start | bytes 1769480 | tf_op jit(solution)/shard_map/ppermute | solution.py:243
  43.3 12.7 %collective-permute-start.12 = (bf16[2,16,9216]{2,1,0:T(8,128)(2,1)S(1)}, bf16[2,16,9216]{2,1,0:T(8,128)(2,1)S(1)}, u32[]{:S(2)}, u32[]{:S(2)}) collective-permute-start(bf16[2,16,9216]{2,1,0:T(8,128)(2,1)S(1)} %collective-permute-done.1.refs_7_.rest_9_), channel_id=1, source_target_pairs={{4,6},{5,7},{6,4},{7,5},{8,10},{9,11},{10,8},{11,9},{20,22},{21,23... | collective-permute-start | bytes 1769480 | tf_op jit(solution)/shard_map/ppermute | solution.py:243
  49.5 5.3 %collective-permute-start.14 = (bf16[1,16,9216]{2,1,0:T(8,128)(2,1)S(1)}, bf16[1,16,9216]{2,1,0:T(8,128)(2,1)S(1)}, u32[]{:S(2)}, u32[]{:S(2)}) collective-permute-start(bf16[1,16,9216]{2,1,0:T(8,128)(2,1)S(1)} %collective-permute-done.8.refs_5_.rest_7_), channel_id=1, source_target_pairs={{4,8},{5,9},{6,10},{7,11},{8,4},{9,5},{10,6},{11,7},{20,24},{21,25... | collective-permute-start | bytes 884744 | tf_op jit(solution)/shard_map/ppermute | solution.py:243
  50.2 24.8 %collective-permute-start.11 = (bf16[2,16,9216]{2,1,0:T(8,128)(2,1)S(1)}, bf16[2,16,9216]{2,1,0:T(8,128)(2,1)S(1)}, u32[]{:S(2)}, u32[]{:S(2)}) collective-permute-start(bf16[2,16,9216]{2,1,0:T(8,128)(2,1)S(1)} %collective-permute-done.4.refs_6_.rest_8_), channel_id=1, source_target_pairs={{0,2},{1,3},{2,0},{3,1},{12,14},{13,15},{14,12},{15,13},{16,18},{1... | collective-permute-start | bytes 1769480 | tf_op jit(solution)/shard_map/ppermute | solution.py:243
  53.3 30.5 %collective-permute-start.17 = (bf16[5,16,9216]{2,1,0:T(8,128)(2,1)S(1)}, bf16[5,16,9216]{2,1,0:T(8,128)(2,1)S(1)}, u32[]{:S(2)}, u32[]{:S(2)}) collective-permute-start(bf16[5,16,9216]{2,1,0:T(8,128)(2,1)S(1)} %pick0_1_2_3_4.1), channel_id=1, source_target_pairs={{0,1},{1,0},{2,3},{3,2},{4,5},{5,4},{6,7},{7,6},{8,9},{9,8},{10,11... | collective-permute-start | bytes 4423688 | tf_op jit(solution)/shard_map/ppermute | solution.py:243
  53.5 11.7 %collective-permute-start.10 = (bf16[1,16,9216]{2,1,0:T(8,128)(2,1)S(1)}, bf16[1,16,9216]{2,1,0:T(8,128)(2,1)S(1)}, u32[]{:S(2)}, u32[]{:S(2)}) collective-permute-start(bf16[1,16,9216]{2,1,0:T(8,128)(2,1)S(1)} %get-tuple-element.29), channel_id=1, source_target_pairs={{4,0},{5,1},{6,2},{7,3},{8,12},{9,13},{10,14},{11,15},{20,16},{21,... | collective-permute-start | bytes 884744 | tf_op jit(solution)/shard_map/ppermute | solution.py:243
  54.8 16.7 %collective-permute-start.9 = (bf16[1,16,9216]{2,1,0:T(8,128)(2,1)S(1)}, bf16[1,16,9216]{2,1,0:T(8,128)(2,1)S(1)}, u32[]{:S(2)}, u32[]{:S(2)}) collective-permute-start(bf16[1,16,9216]{2,1,0:T(8,128)(2,1)S(1)} %get-tuple-element.30), channel_id=1, source_target_pairs={{4,0},{5,1},{6,2},{7,3},{8,12},{9,13},{10,14},{11,15},{20,16},{21,... | collective-permute-start | bytes 884744 | tf_op jit(solution)/shard_map/ppermute | solution.py:243
  56.1 21.3 %collective-permute-start.16 = (bf16[1,16,9216]{2,1,0:T(8,128)(2,1)S(1)}, bf16[1,16,9216]{2,1,0:T(8,128)(2,1)S(1)}, u32[]{:S(2)}, u32[]{:S(2)}) collective-permute-start(bf16[1,16,9216]{2,1,0:T(8,128)(2,1)S(1)} %get-tuple-element.30), channel_id=1, source_target_pairs={{4,6},{5,7},{6,4},{7,5},{8,10},{9,11},{10,8},{11,9},{20,22},{21,23... | collective-permute-start | bytes 884744 | tf_op jit(solution)/shard_map/ppermute | solution.py:243
  65.2 12.2 %collective-permute-start.15 = (bf16[1,16,9216]{2,1,0:T(8,128)(2,1)S(1)}, bf16[1,16,9216]{2,1,0:T(8,128)(2,1)S(1)}, u32[]{:S(2)}, u32[]{:S(2)}) collective-permute-start(bf16[1,16,9216]{2,1,0:T(8,128)(2,1)S(1)} %collective-permute-done.14.refs_3_.rest_18_), channel_id=1, source_target_pairs={{4,0},{5,1},{6,2},{7,3},{8,12},{9,13},{10,14},{11,15},{20,16},{21,... | collective-permute-start | bytes 884744 | tf_op jit(solution)/shard_map/ppermute | solution.py:243
  71.5 10.1 %collective-permute-start.13 = (bf16[1,16,9216]{2,1,0:T(8,128)(2,1)S(1)}, bf16[1,16,9216]{2,1,0:T(8,128)(2,1)S(1)}, u32[]{:S(2)}, u32[]{:S(2)}) collective-permute-start(bf16[1,16,9216]{2,1,0:T(8,128)(2,1)S(1)} %collective-permute-done.9.refs_0_.rest_10_), channel_id=1, source_target_pairs={{0,2},{1,3},{2,0},{3,1},{12,14},{13,15},{14,12},{15,13},{16,18},{1... | collective-permute-start | bytes 884744 | tf_op jit(solution)/shard_map/ppermute | solution.py:243
  75.6 8.3 %collective-permute-start.18 = (bf16[2,16,9216]{2,1,0:T(8,128)(2,1)S(1)}, bf16[2,16,9216]{2,1,0:T(8,128)(2,1)S(1)}, u32[]{:S(2)}, u32[]{:S(2)}) collective-permute-start(bf16[2,16,9216]{2,1,0:T(8,128)(2,1)S(1)} %pick5_6.1), channel_id=1, source_target_pairs={{0,1},{1,0},{2,3},{3,2},{4,5},{5,4},{6,7},{7,6},{8,9},{9,8},{10,11... | collective-permute-start | bytes 1769480 | tf_op jit(solution)/shard_map/ppermute | solution.py:243
  82.2 1.6 %collective-permute-start.19 = (bf16[1,16,9216]{2,1,0:T(8,128)(2,1)S(1)}, bf16[1,16,9216]{2,1,0:T(8,128)(2,1)S(1)}, u32[]{:S(2)}, u32[]{:S(2)}) collective-permute-start(bf16[1,16,9216]{2,1,0:T(8,128)(2,1)S(1)} %pick7.1), channel_id=1, source_target_pairs={{0,1},{1,0},{2,3},{3,2},{4,5},{5,4},{6,7},{7,6},{8,9},{9,8},{10,11... | collective-permute-start | bytes 884744 | tf_op jit(solution)/shard_map/ppermute | solution.py:243

commit v3 on v2

--- a/solution.py
+++ b/solution.py
@@ -38,46 +38,49 @@
     return (base + expand).astype(jnp.bfloat16)
 
 
-def base_kernel(depth, after, tokens, weight, out):
-    step = pl.program_id(0)
-
-    @pl.when(step == 0)
-    def _():
-        out[...] = jnp.zeros_like(out)
-
-    depth_here = weight.shape[0]
-    columns = pl.ds(pl.multiple_of(step * depth, 128), depth_here)
-    out[...] += jnp.dot(tokens[:, columns], weight[...], preferred_element_type=jnp.float32)
-
-
-def base_part(after, tokens, weight, part, parts, streamed=False):
+def base_part(tokens, weight, start, wide, after):
     rows, width = tokens.shape
-    wide = weight.shape[1] // parts
-    steps = 4
-    depth = width // steps
-    home = pltpu.HBM if streamed else pltpu.VMEM
-    tokens = pltpu.with_memory_space_constraint(tokens, home)
-    weight = pltpu.with_memory_space_constraint(weight, pltpu.HBM)
+    chunks = 8
+    depth = width // chunks
+
+    def kernel(after, tokens, weight, out, kept, held, arrived):
+        copies = []
+        for k in range(chunks):
+            span = pl.ds(depth * k, depth)
+            for source, target, kind in (
+                (weight.at[span, pl.ds(start, wide)], held.at[span, :], 0),
+                (tokens.at[:, span], kept.at[:, span], 1),
+            ):
+                copies.append(pltpu.make_async_copy(source, target, arrived.at[kind, k]))
+        for copy in copies:
+            copy.start()
+        for k in range(chunks):
+            for copy in copies[2 * k : 2 * k + 2]:
+                copy.wait()
+            span = pl.ds(depth * k, depth)
+            term = jnp.dot(kept[:, span], held[span, :], preferred_element_type=jnp.float32)
+            if k == 0:
+                out[...] = term
+            else:
+                out[...] += term
+
+    anywhere = pl.BlockSpec(memory_space=pl.ANY)
     return pl.pallas_call(
-        functools.partial(base_kernel, 0 if streamed else depth),
+        kernel,
         out_shape=jax.ShapeDtypeStruct((rows, wide), jnp.float32),
-        grid=(steps,),
-        in_specs=[
-            pl.BlockSpec(memory_space=pl.ANY),
-            pl.BlockSpec((rows, depth), lambda k: (0, k))
-            if streamed
-            else pl.BlockSpec(memory_space=pltpu.VMEM),
-            pl.BlockSpec((depth, wide), lambda k: (k, part)),
+        in_specs=[anywhere] * 3,
+        out_specs=pl.BlockSpec(memory_space=pltpu.VMEM),
+        scratch_shapes=[
+            pltpu.VMEM((rows, width), tokens.dtype),
+            pltpu.VMEM((width, wide), weight.dtype),
+            pltpu.SemaphoreType.DMA((2, chunks)),
         ],
-        out_specs=pl.BlockSpec((rows, wide), lambda k: (0, 0)),
-        compiler_params=pltpu.CompilerParams(
-            dimension_semantics=("arbitrary",), vmem_limit_bytes=16 << 20
-        ),
+        compiler_params=pltpu.CompilerParams(vmem_limit_bytes=32 << 20),
         cost_estimate=pl.CostEstimate(
             flops=2 * rows * width * wide, bytes_accessed=2 * width * wide, transcendentals=0
         ),
-        name=f"base{part}",
-    )(after, tokens, weight)
+        name=f"base{start}",
+    )(after, *(pltpu.with_memory_space_constraint(a, pltpu.HBM) for a in (tokens, weight)))
 
 
 def finish(choice, tokens, mask, bases, batches, given):
@@ -92,50 +95,39 @@
     owners = [(i, k, len(batch) > 2) for i, batch in enumerate(batches) for k in range(len(batch))]
     owners += [(len(batches) + i, None, False) for i in range(len(given))]
     places = [(i, buf, row, k, levels) for (i, k, levels), (buf, row) in zip(owners, spots)]
-    half = whole // 2
 
     def kernel(choice, tokens, mask, *rest):
-        base_refs, bufs = rest[:pieces], rest[pieces:-3]
-        out, table, arrived = rest[-3:]
-
-        def copy(i, buf, row, part):
-            columns = pl.ds(half * part, half)
-            return pltpu.make_async_copy(
-                bufs[buf].at[row, :, columns],
-                table.at[pl.ds(rank * i, rank), columns],
-                arrived.at[part, i],
-            )
-
-        for part in range(2):
-            for i, buf, row, k, levels in places:
-                if k is None:
-                    copy(i, buf, row, part).start()
-                else:
-                    want = choice[i] == k % 2
-                    if levels:
-                        want = want & (choice[last] == k // 2)
-                    pl.when(want)(copy(i, buf, row, part).start)
-        total = None
-        for part in range(2):
-            for i in range(count):
-                copy(i, 0, 0, part).wait()
-            columns = pl.ds(half * part, min(half, width - half * part))
-            term = lax.dot_general(
-                tokens[:, columns],
-                table[:, columns],
-                (((1,), (1,)), ((), ())),
-                preferred_element_type=jnp.float32,
-            )
-            total = term if total is None else total + term
-        shrink = total * mask[...].astype(jnp.float32)
+        base_refs, bufs, (out, table) = rest[:pieces], rest[pieces:-2], rest[-2:]
+        for i, buf, row, k, levels in places:
+            at = pl.ds(rank * i, rank)
+            if k is None:
+                table[at, :] = bufs[buf][row]
+                continue
+            want = choice[i] == k % 2
+            if levels:
+                want = want & (choice[last] == k // 2)
+
+            @pl.when(want)
+            def _(at=at, buf=buf, row=row):
+                table[at, :] = bufs[buf][row]
+
+        shrink = lax.dot_general(
+            tokens[...],
+            table[:, :width],
+            (((1,), (1,)), ((), ())),
+            preferred_element_type=jnp.float32,
+        )
+        shrink = shrink * mask[...].astype(jnp.float32)
         high = shrink.astype(jnp.bfloat16)
         low = (shrink - high.astype(jnp.float32)).astype(jnp.bfloat16)
-        wide = key_width // pieces
-        for i, base in enumerate(base_refs):
-            cols = pl.ds(width + wide * i, wide)
+        start = 0
+        for base in base_refs:
+            wide = base.shape[1]
+            cols = pl.ds(width + start, wide)
             part = jnp.dot(high, table[:, cols], preferred_element_type=jnp.float32)
             part += jnp.dot(low, table[:, cols], preferred_element_type=jnp.float32)
-            out[:, pl.ds(wide * i, wide)] = (base[...] + part).astype(out.dtype)
+            out[:, pl.ds(start, wide)] = (base[...] + part).astype(out.dtype)
+            start += wide
 
     vmem = pl.BlockSpec(memory_space=pltpu.VMEM)
     pin = lambda a: pltpu.with_memory_space_constraint(a, pltpu.VMEM)
@@ -144,11 +136,10 @@
         out_shape=jax.ShapeDtypeStruct((rows, key_width), jnp.bfloat16),
         in_specs=[pl.BlockSpec(memory_space=pltpu.SMEM)]
         + [vmem] * (2 + pieces)
-        + [pl.BlockSpec(memory_space=pl.ANY)] * len(arrays),
+        + [vmem] * len(arrays),
         out_specs=vmem,
         scratch_shapes=[
             pltpu.VMEM((rank * count, whole), jnp.bfloat16),
-            pltpu.SemaphoreType.DMA((2, count)),
         ],
         compiler_params=pltpu.CompilerParams(vmem_limit_bytes=24 << 20),
         cost_estimate=pl.CostEstimate(
@@ -157,26 +148,33 @@
             transcendentals=0,
         ),
         name="shrink_expand",
-    )(choice, pin(tokens), pin(mask), *map(pin, bases), *arrays)
-
-
-def join_kernel(shrink, expand, out):
+    )(choice, pin(tokens), pin(mask), *map(pin, bases), *map(pin, arrays))
+
+
+def join_kernel(shrink, expand, out, arrived):
     width = shrink.shape[2]
-    out[:, :, pl.ds(0, width)] = shrink[...]
-    out[:, :, pl.ds(width, expand.shape[2])] = expand[...]
+    copies = [
+        pltpu.make_async_copy(shrink, out.at[:, :, pl.ds(0, width)], arrived.at[0]),
+        pltpu.make_async_copy(expand, out.at[:, :, pl.ds(width, expand.shape[2])], arrived.at[1]),
+    ]
+    for copy in copies:
+        copy.start()
+    for copy in copies:
+        copy.wait()
 
 
 def joined(shrink, expand):
     held, rank, width = shrink.shape
-    vmem = pl.BlockSpec(memory_space=pltpu.VMEM)
+    pin = lambda a: pltpu.with_memory_space_constraint(a, pltpu.HBM)
     return pl.pallas_call(
         join_kernel,
         out_shape=jax.ShapeDtypeStruct((held, rank, width + expand.shape[2]), shrink.dtype),
-        in_specs=[vmem] * 2,
-        out_specs=vmem,
+        in_specs=[pl.BlockSpec(memory_space=pl.ANY)] * 2,
+        out_specs=pl.BlockSpec(memory_space=pltpu.VMEM),
+        scratch_shapes=[pltpu.SemaphoreType.DMA((2,))],
         compiler_params=pltpu.CompilerParams(vmem_limit_bytes=8 << 20),
         name="join",
-    )(shrink, expand)
+    )(pin(shrink), pin(expand))
 
 
 def listed(entries):
@@ -238,13 +236,22 @@
     pairs = along_z([(0, 1), (1, 0), (2, 3), (3, 2)])
     middle = along_z([(1, 2), (2, 1)])
     outward = along_z([(1, 0), (2, 3)])
-    inward = along_z([(0, 1), (3, 2)])
-    every, outer_y, inner_y = along_y(range(4)), along_y([0, 3]), along_y([1, 2])
+    every, outer_y = along_y(range(4)), along_y([0, 3])
     send = lambda a, p: lax.ppermute(a, "store", p)
     together = lax.optimization_barrier
 
     own = joined(shrink_factors, expand_factors)
-    p1, p2, y0 = send(own, pairs), send(own, middle), send(own, every)
+    p1, y0, p2 = send(own, pairs), send(own, every), send(own, middle)
+
+    wide = expand_factors.shape[2] // 2
+    base0 = base_part(tokens, base_weight, 0, wide, requests)
+    p1, p2, y0, base0, home_rows, requests, block_slot = together(
+        (p1, p2, y0, base0, home_rows, requests, block_slot)
+    )
+    either = lambda a, b: jnp.where(inner, a, b)
+    m1 = send(either(p2, y0), pairs)
+    p3 = send(p1, middle)
+    n1 = send(either(p2, p1), every)
 
     adapters = jnp.arange(home_rows.shape[0], dtype=jnp.int32)
     stored = jnp.sum(
@@ -278,34 +285,24 @@
     take_mine = jnp.concatenate([second_wanted(stored), level])
     take_other = jnp.concatenate([second_wanted(stored_other), level])
 
-    pieces = 2
-    after = lambda *a: together((take_mine, *a))[0]
-    part = lambda i, order: base_part(order, tokens, base_weight, i, pieces)
-    base0 = base_part(take_mine, tokens, base_weight, 0, pieces, streamed=True)
-    p1, p2, y0, base0, mask, take_mine, take_other = together(
-        (p1, p2, y0, base0, mask, take_mine, take_other)
-    )
-    p4, p3 = send(p2, outward), send(p1, middle)
-    y1a, y1b = send(p1[:1], every), send(p1[1:], outer_y)
-    w1 = send(y0[1:], inward)
-    y2 = send(p2, inner_y)
-    base1 = part(1, after(p1))
-    p4, p3, base1 = together((p4, p3, base1))
-    p5a, p5b = send(p3[:1], outward), send(p3[1:], outward)
-    y4, y3a = send(p4, outer_y), send(p3[:1], inner_y)
-    w2 = send(w1, middle)
-    y5a = send(p5a, outer_y)
-    w3 = send(w2, outward)
+    after = lambda a: together((requests, a))[0]
+    base1 = base_part(tokens, base_weight, wide, wide, after(p1))
+    m1, p3, n1, base1, mask, take_mine, take_other = together(
+        (m1, p3, n1, base1, mask, take_mine, take_other)
+    )
+    p5a, n2b = send(p3[:1], outward), send(either(p3, m1)[1:], every)
+    p5b, n2a = send(p3[1:], outward), send(either(p3, m1)[:1], every)
+    y5, w5 = send(p5a, outer_y), send(n2b, outward)
 
     batches = [
         [(own, 0), (own, 1)],
         [(p1, 0), (p1, 1)],
         [(y0, 0), (y0, 1)],
-        [(y1a, 0), (y1b, 0), (y1a, 0), (w1, 0)],
-        [(p4, 0), (p4, 1), (p2, 0), (p2, 1)],
+        [(n1, 0), (n1, 1), (m1, 0), (m1, 1)],
+        [(m1, 0), (m1, 1), (p2, 0), (p2, 1)],
         [(p5a, 0), (p5b, 0), (p3, 0), (p3, 1)],
-        [(y4, 0), (y4, 1), (y2, 0), (y2, 1)],
-        [(y5a, 0), (w3, 0), (y3a, 0), (w2, 0)],
+        [(n2a, 0), (n2b, 0), (n1, 0), (n1, 1)],
+        [(y5, 0), (w5, 0), (n2a, 0), (n2b, 0)],
     ]
     given = []
     for ids in ((0, 1, 2, 3, 4), (5, 6), (7,)):

time: 96.4 us -> 80.3 us (0.83)
  starting transfers between devices: 29.7 us -> 21.5 us
  Pallas kernels: 34.8 us -> 29.9 us
  local copies, waits for them, and re-layouts: 3.05 us -> 1.16 us
  waiting for transfers between devices: 26.4 us -> 24.8 us
    ppermute x20 -> x16, starting transfers between devices: 29.7 us -> 21.5 us  [gridded(): send = lambda a, p: lax.ppermute(a, 'store', p)]
    pallas_call x1, Pallas kernels: 12.1 us -> 8.57 us  [finish(): pl.pallas_call(kernel, out_shape=jax.ShapeDtypeStruct((rows, key_width),...]
    pallas_call x2, Pallas kernels: 20.7 us -> 17.8 us  [base_part(): pl.pallas_call(kernel, out_shape=jax.ShapeDtypeStruct((rows, wide), jnp.f...]
    ppermute x20 -> x16, waiting for transfers between devices: 26.4 us -> 24.8 us  [gridded(): send = lambda a, p: lax.ppermute(a, 'store', p)]
    select_n x0 -> x3, other arithmetic: none -> 1.6 us  [the longest x2 1.58 us: gridded(): either = lambda a, b: jnp.where(inner, a, b)]
    unnamed x10 -> x18, local copies, waits for them, and re-layouts: 1.89 us -> 0.7 us
    pallas_call x1, Pallas kernels: 0.04 us -> 1.06 us  [joined(): pl.pallas_call(join_kernel, out_shape=jax.ShapeDtypeStruct((held, rank, w...]
  transfers between devices with their start and end apart: 20 -> 16, of which waited for: 6 -> 9; matrix products, arithmetic and copies ran while one was open for 3% -> 3% of each run, Pallas kernels for 24% -> 24%
where the time goes in v3:
time: 80.3 us; the launch traced here: 80 us
  Pallas kernels  29.9 us (37%)
  waiting for transfers between devices  24.8 us (31%)
  starting transfers between devices  21.5 us (27%)
  other arithmetic  2.39 us (3%)
  local copies, waits for them, and re-layouts  1.16 us (1%)
    ppermute x16, waiting for transfers between devices, gridded(): send = lambda a, p: lax.ppermute(a, 'store', p)  24.8 us
    ppermute x16, starting transfers between devices, gridded(): send = lambda a, p: lax.ppermute(a, 'store', p)  21.5 us
    pallas_call x2, Pallas kernels, base_part(): pl.pallas_call(kernel, out_shape=jax.ShapeDtypeStruct((rows, wide), jnp.f...  17.8 us
    pallas_call x1, Pallas kernels, finish(): pl.pallas_call(kernel, out_shape=jax.ShapeDtypeStruct((rows, key_width),...  8.57 us
    pallas_call x3, Pallas kernels, picked(): pl.pallas_call(kernel, out_shape=jax.ShapeDtypeStruct((len(ids), rank, wh...  2.5 us
  transfers between devices with their start and end apart: 16, of which 9 were waited for; matrix products, arithmetic and copies ran while one was open for 3% of the time, Pallas kernels for 24%

profile of v3, /device:TPU:0, one launch (start us, length us, event | category | flops | bytes accessed | tf_op | source)
XLA Modules:
  0.0 80.0 jit_solution(12836788884185775593)
XLA Ops:
  0.0 1.1 %join.1.refs_0_.rest_2_ = bf16[2,16,9216]{2,1,0:T(8,128)(2,1)S(1)} custom-call(bf16[2,16,8192]{2,1,0:T(8,128)(2,1)} %shrink.1, bf16[2,16,1024]{2,1,0:T(8,128)(2,1)} %expand.1), custom_call_target="tpu_custom_call" | custom-call | tf_op jit(solution)/shard_map/join/pallas_call | solution.py:169
  1.1 3.0 %collective-permute-start.2 = (bf16[2,16,9216]{2,1,0:T(8,128)(2,1)S(1)}, bf16[2,16,9216]{2,1,0:T(8,128)(2,1)S(1)}, u32[]{:S(2)}, u32[]{:S(2)}) collective-permute-start(bf16[2,16,9216]{2,1,0:T(8,128)(2,1)S(1)} %join.1.refs_0_.rest_2_), channel_id=1, source_target_pairs={{0,2},{1,3},{2,0},{3,1},{4,6},{5,7},{6,4},{7,5},{8,10},{9,11},{10,... | collective-permute-start | bytes 1769480 | tf_op jit(solution)/shard_map/ppermute | solution.py:240
  4.1 0.7 collective-permute-start.1
  4.8 4.4 %collective-permute-start = (bf16[2,16,9216]{2,1,0:T(8,128)(2,1)S(1)}, bf16[2,16,9216]{2,1,0:T(8,128)(2,1)}, u32[]{:S(2)}, u32[]{:S(2)}) collective-permute-start(bf16[2,16,9216]{2,1,0:T(8,128)(2,1)S(1)} %join.1.refs_0_.rest_2_), channel_id=1, source_target_pairs={{0,4},{1,5},{2,6},{3,7},{4,0},{5,1},{6,2},{7,3},{8,12},{9,13},{10,... | collective-permute-start | bytes 1769480 | tf_op jit(solution)/shard_map/ppermute | solution.py:240
  9.4 0.7 copy-done.2
  10.1 8.9 %base0.1.rest_0_ = f32[768,512]{1,0:T(8,128)S(1)} custom-call(s32[1,8]{1,0:T(1,128)S(1)} %copy-done.2, bf16[768,8192]{1,0:T(8,128)(2,1)} %tokens.5, bf16[8192,1024]{1,0:T(8,128)(2,1)} %weight.3), custom_call_target="tpu_custom_call" | custom-call | flops 6442450944 | bytes 8388608 | tf_op jit(solution)/shard_map/base0/pallas_call | solution.py:68
  19.0 3.1 %collective-permute-done.refs_1_.rest_3_ = bf16[2,16,9216]{2,1,0:T(8,128)(2,1)} collective-permute-done((bf16[2,16,9216]{2,1,0:T(8,128)(2,1)S(1)}, bf16[2,16,9216]{2,1,0:T(8,128)(2,1)}, u32[]{:S(2)}, u32[]{:S(2)}) %collective-permute-start) | collective-permute-done | bytes 589856 | tf_op jit(solution)/shard_map/ppermute | solution.py:240
  22.1 0.2 select_reduce_fusion.3
  22.4 0.7 collective-permute-start.4
  23.5 1.5 %broadcast_select_fusion.1 = (bf16[2,16,9216]{2,1,0:T(8,128)(2,1)S(1)}, bf16[2,16,9216]{2,1,0:T(8,128)(2,1)S(1)}) fusion(bf16[2,16,9216]{2,1,0:T(8,128)(2,1)} %copy-done, bf16[2,16,9216]{2,1,0:T(8,128)(2,1)} %collective-permute-done.refs_1_.rest_3_, pred[]{:T(512)S(6)} %or.3, bf16[2,16,9216]{2,1,0:T(8,128)(2,1)S(1)} %collective-permute-done.2.refs_2_.rest_4_), kind=kLoop, calls=%fused_computation.2 | loop fusion | flops 589824 | bytes 2949121 | tf_op jit(solution)/shard_map/jit(_where)/select_n | solution.py:251
  25.0 0.6 collective-permute-start.5
  25.6 3.4 %collective-permute-start.3 = (bf16[2,16,9216]{2,1,0:T(8,128)(2,1)S(1)}, bf16[2,16,9216]{2,1,0:T(8,128)(2,1)S(1)}, u32[]{:S(2)}, u32[]{:S(2)}) collective-permute-start(bf16[2,16,9216]{2,1,0:T(8,128)(2,1)S(1)} %get-tuple-element.42), channel_id=1, source_target_pairs={{0,4},{1,5},{2,6},{3,7},{4,0},{5,1},{6,2},{7,3},{8,12},{9,13},{10,... | collective-permute-start | bytes 1769480 | tf_op jit(solution)/shard_map/ppermute | solution.py:240
  28.9 8.9 %base512.1.rest_1_ = f32[768,512]{1,0:T(8,128)S(1)} custom-call(s32[1,8]{1,0:T(1,128)S(1)} %copy-done.3, bf16[768,8192]{1,0:T(8,128)(2,1)} %tokens.5, bf16[8192,1024]{1,0:T(8,128)(2,1)} %weight.3), custom_call_target="tpu_custom_call" | custom-call | flops 6442450944 | bytes 8388608 | tf_op jit(solution)/shard_map/base512/pallas_call | solution.py:68
  37.8 0.2 compare_convert_fusion.mask
  38.1 0.2 select_reduce_fusion
  38.3 2.4 %collective-permute-done.5.refs_3_.refs_5_.rest_5_ = bf16[2,16,9216]{2,1,0:T(8,128)(2,1)S(1)} collective-permute-done((bf16[2,16,9216]{2,1,0:T(8,128)(2,1)S(1)}, bf16[2,16,9216]{2,1,0:T(8,128)(2,1)S(1)}, u32[]{:S(2)}, u32[]{:S(2)}) %collective-permute-start.5) | collective-permute-done | bytes 589856 | tf_op jit(solution)/shard_map/ppermute | solution.py:240
  40.8 1.6 %collective-permute-done.3.refs_4_.rest_6_ = bf16[2,16,9216]{2,1,0:T(8,128)(2,1)S(1)} collective-permute-done((bf16[2,16,9216]{2,1,0:T(8,128)(2,1)S(1)}, bf16[2,16,9216]{2,1,0:T(8,128)(2,1)S(1)}, u32[]{:S(2)}, u32[]{:S(2)}) %collective-permute-start.3) | collective-permute-done | bytes 589856 | tf_op jit(solution)/shard_map/ppermute | solution.py:240
  42.5 1.3 %pick0_1_2_3_4.1 = bf16[5,16,9216]{2,1,0:T(8,128)(2,1)S(1)} custom-call(s32[9]{0:T(128)S(1)} %get-tuple-element.34.choice, bf16[2,16,9216]{2,1,0:T(8,128)(2,1)S(1)} %join.1.refs_0_.rest_2_, bf16[2,16,9216]{2,1,0:T(8,128)(2,1)} %collective-permute-done.refs_1_.rest_3_, bf16[2,16,9216]{2,1,0:T(8,128)(2,1)S(1)} %collective-permute-done.2.refs_2_.rest_4_, ...), custom_call_target="tpu_custom_call" | custom-call | tf_op jit(solution)/shard_map/pick0_1_2_3_4/pallas_call | solution.py:212
  43.9 1.6 %collective-permute-start.10 = (bf16[1,16,9216]{2,1,0:T(8,128)(2,1)S(1)}, bf16[1,16,9216]{2,1,0:T(8,128)(2,1)S(1)}, u32[]{:S(2)}, u32[]{:S(2)}) collective-permute-start(bf16[1,16,9216]{2,1,0:T(8,128)(2,1)S(1)} %get-tuple-element.37), channel_id=1, source_target_pairs={{0,2},{1,3},{2,0},{3,1},{4,6},{5,7},{6,4},{7,5},{8,10},{9,11},{10,... | collective-permute-start | bytes 884744 | tf_op jit(solution)/shard_map/ppermute | solution.py:240
  45.5 1.3 %collective-permute-start.7 = (bf16[1,16,9216]{2,1,0:T(8,128)(2,1)S(1)}, bf16[1,16,9216]{2,1,0:T(8,128)(2,1)S(1)}, u32[]{:S(2)}, u32[]{:S(2)}) collective-permute-start(bf16[1,16,9216]{2,1,0:T(8,128)(2,1)S(1)} %get-tuple-element.40), channel_id=1, source_target_pairs={{4,0},{5,1},{6,2},{7,3},{8,12},{9,13},{10,14},{11,15},{20,16},{21,... | collective-permute-start | bytes 884744 | tf_op jit(solution)/shard_map/ppermute | solution.py:240
  46.8 0.6 collective-permute-start.9
  47.4 1.3 %collective-permute-start.8 = (bf16[1,16,9216]{2,1,0:T(8,128)(2,1)S(1)}, bf16[1,16,9216]{2,1,0:T(8,128)(2,1)S(1)}, u32[]{:S(2)}, u32[]{:S(2)}) collective-permute-start(bf16[1,16,9216]{2,1,0:T(8,128)(2,1)S(1)} %get-tuple-element.39), channel_id=1, source_target_pairs={{4,0},{5,1},{6,2},{7,3},{8,12},{9,13},{10,14},{11,15},{20,16},{21,... | collective-permute-start | bytes 884744 | tf_op jit(solution)/shard_map/ppermute | solution.py:240
  48.7 5.1 %collective-permute-done.10.refs_4_.refs_3_.rest_12_ = bf16[1,16,9216]{2,1,0:T(8,128)(2,1)S(1)} collective-permute-done((bf16[1,16,9216]{2,1,0:T(8,128)(2,1)S(1)}, bf16[1,16,9216]{2,1,0:T(8,128)(2,1)S(1)}, u32[]{:S(2)}, u32[]{:S(2)}) %collective-permute-start.10) | collective-permute-done | bytes 294944 | tf_op jit(solution)/shard_map/ppermute | solution.py:240
  53.8 1.3 %collective-permute-start.12 = (bf16[1,16,9216]{2,1,0:T(8,128)(2,1)S(1)}, bf16[1,16,9216]{2,1,0:T(8,128)(2,1)S(1)}, u32[]{:S(2)}, u32[]{:S(2)}) collective-permute-start(bf16[1,16,9216]{2,1,0:T(8,128)(2,1)S(1)} %collective-permute-done.10.refs_4_.refs_3_.rest_12_), channel_id=1, source_target_pairs={{4,0},{5,1},{6,2},{7,3},{8,12},{9,13},{10,14},{11,15},{20,16},{21,... | collective-permute-start | bytes 884744 | tf_op jit(solution)/shard_map/ppermute | solution.py:240
  55.1 2.2 %collective-permute-done.7.refs_0_.rest_8_ = bf16[1,16,9216]{2,1,0:T(8,128)(2,1)S(1)} collective-permute-done((bf16[1,16,9216]{2,1,0:T(8,128)(2,1)S(1)}, bf16[1,16,9216]{2,1,0:T(8,128)(2,1)S(1)}, u32[]{:S(2)}, u32[]{:S(2)}) %collective-permute-start.7) | collective-permute-done | bytes 294944 | tf_op jit(solution)/shard_map/ppermute | solution.py:240
  57.2 2.4 %collective-permute-start.11 = (bf16[1,16,9216]{2,1,0:T(8,128)(2,1)S(1)}, bf16[1,16,9216]{2,1,0:T(8,128)(2,1)S(1)}, u32[]{:S(2)}, u32[]{:S(2)}) collective-permute-start(bf16[1,16,9216]{2,1,0:T(8,128)(2,1)S(1)} %collective-permute-done.7.refs_0_.rest_8_), channel_id=1, source_target_pairs={{0,2},{1,3},{2,0},{3,1},{12,14},{13,15},{14,12},{15,13},{16,18},{1... | collective-permute-start | bytes 884744 | tf_op jit(solution)/shard_map/ppermute | solution.py:240
  59.7 3.8 %collective-permute-done.8.refs_1_.rest_9_ = bf16[1,16,9216]{2,1,0:T(8,128)(2,1)S(1)} collective-permute-done((bf16[1,16,9216]{2,1,0:T(8,128)(2,1)S(1)}, bf16[1,16,9216]{2,1,0:T(8,128)(2,1)S(1)}, u32[]{:S(2)}, u32[]{:S(2)}) %collective-permute-start.8) | collective-permute-done | bytes 294944 | tf_op jit(solution)/shard_map/ppermute | solution.py:240
  63.6 0.6 pick5_6.1
  64.3 4.9 %collective-permute-done.12.refs_1_.rest_14_ = bf16[1,16,9216]{2,1,0:T(8,128)(2,1)S(1)} collective-permute-done((bf16[1,16,9216]{2,1,0:T(8,128)(2,1)S(1)}, bf16[1,16,9216]{2,1,0:T(8,128)(2,1)S(1)}, u32[]{:S(2)}, u32[]{:S(2)}) %collective-permute-start.12) | collective-permute-done | bytes 294944 | tf_op jit(solution)/shard_map/ppermute | solution.py:240
  69.2 0.6 pick7.1
  69.8 1.6 %collective-permute-done.15.rest_17_ = bf16[1,16,9216]{2,1,0:T(8,128)(2,1)S(1)} collective-permute-done((bf16[1,16,9216]{2,1,0:T(8,128)(2,1)S(1)}, bf16[1,16,9216]{2,1,0:T(8,128)(2,1)S(1)}, u32[]{:S(2)}, u32[]{:S(2)}) %collective-permute-start.15) | collective-permute-done | bytes 294944 | tf_op jit(solution)/shard_map/ppermute | solution.py:240
  71.4 8.6 %shrink_expand.1 = bf16[768,1024]{1,0:T(8,128)(2,1)} custom-call(s32[9]{0:T(128)S(1)} %get-tuple-element.27.choice, bf16[768,8192]{1,0:T(8,128)(2,1)S(1)} %bitcast.12, bf16[768,256]{1,0:T(8,128)(2,1)S(1)} %compare_convert_fusion.mask, f32[768,512]{1,0:T(8,128)S(1)} %base0.1.rest_0_, f32[768,512]{1,0:T(8,128)S(1)} %base512.1.rest_1_, ...), custom_call_target="tpu_custom_call" | custom-call | flops 3221225472 | bytes 4718592 | tf_op jit(solution)/shard_map/shrink_expand/pallas_call | solution.py:134
  (44 shorter events, 1.2 us)
Async XLA Ops:
  1.1 17.9 %collective-permute-start.2 = (bf16[2,16,9216]{2,1,0:T(8,128)(2,1)S(1)}, bf16[2,16,9216]{2,1,0:T(8,128)(2,1)S(1)}, u32[]{:S(2)}, u32[]{:S(2)}) collective-permute-start(bf16[2,16,9216]{2,1,0:T(8,128)(2,1)S(1)} %join.1.refs_0_.rest_2_), channel_id=1, source_target_pairs={{0,2},{1,3},{2,0},{3,1},{4,6},{5,7},{6,4},{7,5},{8,10},{9,11},{10,... | collective-permute-start | bytes 1769480 | tf_op jit(solution)/shard_map/ppermute | solution.py:240
  4.1 14.9 %collective-permute-start.1 = (bf16[2,16,9216]{2,1,0:T(8,128)(2,1)S(1)}, bf16[2,16,9216]{2,1,0:T(8,128)(2,1)S(1)}, u32[]{:S(2)}, u32[]{:S(2)}) collective-permute-start(bf16[2,16,9216]{2,1,0:T(8,128)(2,1)S(1)} %join.1.refs_0_.rest_2_), channel_id=1, source_target_pairs={{4,8},{5,9},{6,10},{7,11},{8,4},{9,5},{10,6},{11,7},{20,24},{21,25... | collective-permute-start | bytes 1769480 | tf_op jit(solution)/shard_map/ppermute | solution.py:240
  4.8 17.3 %collective-permute-start = (bf16[2,16,9216]{2,1,0:T(8,128)(2,1)S(1)}, bf16[2,16,9216]{2,1,0:T(8,128)(2,1)}, u32[]{:S(2)}, u32[]{:S(2)}) collective-permute-start(bf16[2,16,9216]{2,1,0:T(8,128)(2,1)S(1)} %join.1.refs_0_.rest_2_), channel_id=1, source_target_pairs={{0,4},{1,5},{2,6},{3,7},{4,0},{5,1},{6,2},{7,3},{8,12},{9,13},{10,... | collective-permute-start | bytes 1769480 | tf_op jit(solution)/shard_map/ppermute | solution.py:240
  9.4 0.7 copy-start.2
  10.1 12.0 %copy-start.5 = (s32[32]{0:T(128)S(1)}, s32[32]{0:T(128)}, u32[]{:S(2)}) copy-start(s32[32]{0:T(128)} %param.11) | copy-start | bytes 388
  10.1 13.3 %copy-start.4 = (s32[1,48]{1,0:T(1,128)S(1)}, s32[1,48]{1,0:T(1,128)}, u32[]{:S(2)}) copy-start(s32[1,48]{1,0:T(1,128)} %param.13) | copy-start | bytes 580
  19.0 10.0 %copy-start.3 = (s32[1,8]{1,0:T(1,128)S(1)}, s32[1,8]{1,0:T(1,128)}, u32[]{:S(2)}) copy-start(s32[1,8]{1,0:T(1,128)} %after.2) | copy-start | bytes 100
  19.0 3.3 %copy-start = (bf16[2,16,9216]{2,1,0:T(8,128)(2,1)}, bf16[2,16,9216]{2,1,0:T(8,128)(2,1)S(1)}, u32[]{:S(2)}) copy-start(bf16[2,16,9216]{2,1,0:T(8,128)(2,1)S(1)} %collective-permute-done.1.refs_5_.rest_7_) | copy-start | bytes 1769476
  22.3 15.7 %collective-permute-start.6 = (s32[8]{0:T(128)S(1)}, s32[8]{0:T(128)S(1)}, u32[]{:S(2)}, u32[]{:S(2)}) collective-permute-start(s32[8]{0:T(128)S(1)} %select_reduce_fusion.3), channel_id=1, source_target_pairs={{0,1},{1,0},{2,3},{3,2},{4,5},{5,4},{6,7},{7,6},{8,9},{9,8},{10,11... | collective-permute-start | bytes 104 | tf_op jit(solution)/shard_map/ppermute | solution.py:240
  22.4 15.9 %collective-permute-start.4 = (bf16[2,16,9216]{2,1,0:T(8,128)(2,1)}, bf16[2,16,9216]{2,1,0:T(8,128)(2,1)S(1)}, u32[]{:S(2)}, u32[]{:S(2)}) collective-permute-start(bf16[2,16,9216]{2,1,0:T(8,128)(2,1)} %collective-permute-done.refs_1_.rest_3_), channel_id=1, source_target_pairs={{4,8},{5,9},{6,10},{7,11},{8,4},{9,5},{10,6},{11,7},{20,24},{21,25... | collective-permute-start | bytes 1769480 | tf_op jit(solution)/shard_map/ppermute | solution.py:240
  23.5 47.9 %slice-start = ((s8[12582912]{0:T(1024)(128)(4,1)}), s8[4194304]{0:T(1024)(128)(4,1)S(1)}, s32[]{:S(2)}) async-start(s8[12582912]{0:T(1024)(128)(4,1)} %bitcast.11), calls=%async_computation | async-start | bytes 8388608
  25.0 15.8 %collective-permute-start.5 = (bf16[2,16,9216]{2,1,0:T(8,128)(2,1)S(1)}, bf16[2,16,9216]{2,1,0:T(8,128)(2,1)S(1)}, u32[]{:S(2)}, u32[]{:S(2)}) collective-permute-start(bf16[2,16,9216]{2,1,0:T(8,128)(2,1)S(1)} %get-tuple-element.41), channel_id=1, source_target_pairs={{0,2},{1,3},{2,0},{3,1},{4,6},{5,7},{6,4},{7,5},{8,10},{9,11},{10,... | collective-permute-start | bytes 1769480 | tf_op jit(solution)/shard_map/ppermute | solution.py:240
  25.6 45.9 %slice-start.1 = ((s8[12582912]{0:T(1024)(128)(4,1)}), s8[4194304]{0:T(1024)(128)(4,1)S(1)}, s32[]{:S(2)}) async-start(s8[12582912]{0:T(1024)(128)(4,1)} %bitcast.11), calls=%async_computation.1 | async-start | bytes 8388608
  25.6 45.9 %slice-start.2 = ((s8[12582912]{0:T(1024)(128)(4,1)}), s8[4194304]{0:T(1024)(128)(4,1)S(1)}, s32[]{:S(2)}) async-start(s8[12582912]{0:T(1024)(128)(4,1)} %bitcast.11), calls=%async_computation.2 | async-start | bytes 8388608
  25.6 16.8 %collective-permute-start.3 = (bf16[2,16,9216]{2,1,0:T(8,128)(2,1)S(1)}, bf16[2,16,9216]{2,1,0:T(8,128)(2,1)S(1)}, u32[]{:S(2)}, u32[]{:S(2)}) collective-permute-start(bf16[2,16,9216]{2,1,0:T(8,128)(2,1)S(1)} %get-tuple-element.42), channel_id=1, source_target_pairs={{0,4},{1,5},{2,6},{3,7},{4,0},{5,1},{6,2},{7,3},{8,12},{9,13},{10,... | collective-permute-start | bytes 1769480 | tf_op jit(solution)/shard_map/ppermute | solution.py:240
  38.0 4.5 %copy-start.1 = (bf16[2,16,9216]{2,1,0:T(8,128)(2,1)S(1)}, bf16[2,16,9216]{2,1,0:T(8,128)(2,1)}, u32[]{:S(2)}) copy-start(bf16[2,16,9216]{2,1,0:T(8,128)(2,1)} %copy-done) | copy-start | bytes 1769476
  43.8 27.6 %collective-permute-start.13 = (bf16[5,16,9216]{2,1,0:T(8,128)(2,1)S(1)}, bf16[5,16,9216]{2,1,0:T(8,128)(2,1)S(1)}, u32[]{:S(2)}, u32[]{:S(2)}) collective-permute-start(bf16[5,16,9216]{2,1,0:T(8,128)(2,1)S(1)} %pick0_1_2_3_4.1), channel_id=1, source_target_pairs={{0,1},{1,0},{2,3},{3,2},{4,5},{5,4},{6,7},{7,6},{8,9},{9,8},{10,11... | collective-permute-start | bytes 4423688 | tf_op jit(solution)/shard_map/ppermute | solution.py:240
  43.9 9.9 %collective-permute-start.10 = (bf16[1,16,9216]{2,1,0:T(8,128)(2,1)S(1)}, bf16[1,16,9216]{2,1,0:T(8,128)(2,1)S(1)}, u32[]{:S(2)}, u32[]{:S(2)}) collective-permute-start(bf16[1,16,9216]{2,1,0:T(8,128)(2,1)S(1)} %get-tuple-element.37), channel_id=1, source_target_pairs={{0,2},{1,3},{2,0},{3,1},{4,6},{5,7},{6,4},{7,5},{8,10},{9,11},{10,... | collective-permute-start | bytes 884744 | tf_op jit(solution)/shard_map/ppermute | solution.py:240
  45.5 11.7 %collective-permute-start.7 = (bf16[1,16,9216]{2,1,0:T(8,128)(2,1)S(1)}, bf16[1,16,9216]{2,1,0:T(8,128)(2,1)S(1)}, u32[]{:S(2)}, u32[]{:S(2)}) collective-permute-start(bf16[1,16,9216]{2,1,0:T(8,128)(2,1)S(1)} %get-tuple-element.40), channel_id=1, source_target_pairs={{4,0},{5,1},{6,2},{7,3},{8,12},{9,13},{10,14},{11,15},{20,16},{21,... | collective-permute-start | bytes 884744 | tf_op jit(solution)/shard_map/ppermute | solution.py:240
  46.8 12.9 %collective-permute-start.9 = (bf16[1,16,9216]{2,1,0:T(8,128)(2,1)S(1)}, bf16[1,16,9216]{2,1,0:T(8,128)(2,1)S(1)}, u32[]{:S(2)}, u32[]{:S(2)}) collective-permute-start(bf16[1,16,9216]{2,1,0:T(8,128)(2,1)S(1)} %get-tuple-element.38), channel_id=1, source_target_pairs={{0,2},{1,3},{2,0},{3,1},{4,6},{5,7},{6,4},{7,5},{8,10},{9,11},{10,... | collective-permute-start | bytes 884744 | tf_op jit(solution)/shard_map/ppermute | solution.py:240
  47.4 16.2 %collective-permute-start.8 = (bf16[1,16,9216]{2,1,0:T(8,128)(2,1)S(1)}, bf16[1,16,9216]{2,1,0:T(8,128)(2,1)S(1)}, u32[]{:S(2)}, u32[]{:S(2)}) collective-permute-start(bf16[1,16,9216]{2,1,0:T(8,128)(2,1)S(1)} %get-tuple-element.39), channel_id=1, source_target_pairs={{4,0},{5,1},{6,2},{7,3},{8,12},{9,13},{10,14},{11,15},{20,16},{21,... | collective-permute-start | bytes 884744 | tf_op jit(solution)/shard_map/ppermute | solution.py:240
  53.8 15.4 %collective-permute-start.12 = (bf16[1,16,9216]{2,1,0:T(8,128)(2,1)S(1)}, bf16[1,16,9216]{2,1,0:T(8,128)(2,1)S(1)}, u32[]{:S(2)}, u32[]{:S(2)}) collective-permute-start(bf16[1,16,9216]{2,1,0:T(8,128)(2,1)S(1)} %collective-permute-done.10.refs_4_.refs_3_.rest_12_), channel_id=1, source_target_pairs={{4,0},{5,1},{6,2},{7,3},{8,12},{9,13},{10,14},{11,15},{20,16},{21,... | collective-permute-start | bytes 884744 | tf_op jit(solution)/shard_map/ppermute | solution.py:240
  57.2 11.9 %collective-permute-start.11 = (bf16[1,16,9216]{2,1,0:T(8,128)(2,1)S(1)}, bf16[1,16,9216]{2,1,0:T(8,128)(2,1)S(1)}, u32[]{:S(2)}, u32[]{:S(2)}) collective-permute-start(bf16[1,16,9216]{2,1,0:T(8,128)(2,1)S(1)} %collective-permute-done.7.refs_0_.rest_8_), channel_id=1, source_target_pairs={{0,2},{1,3},{2,0},{3,1},{12,14},{13,15},{14,12},{15,13},{16,18},{1... | collective-permute-start | bytes 884744 | tf_op jit(solution)/shard_map/ppermute | solution.py:240
  64.2 7.2 %collective-permute-start.14 = (bf16[2,16,9216]{2,1,0:T(8,128)(2,1)S(1)}, bf16[2,16,9216]{2,1,0:T(8,128)(2,1)S(1)}, u32[]{:S(2)}, u32[]{:S(2)}) collective-permute-start(bf16[2,16,9216]{2,1,0:T(8,128)(2,1)S(1)} %pick5_6.1), channel_id=1, source_target_pairs={{0,1},{1,0},{2,3},{3,2},{4,5},{5,4},{6,7},{7,6},{8,9},{9,8},{10,11... | collective-permute-start | bytes 1769480 | tf_op jit(solution)/shard_map/ppermute | solution.py:240
  69.8 1.6 %collective-permute-start.15 = (bf16[1,16,9216]{2,1,0:T(8,128)(2,1)S(1)}, bf16[1,16,9216]{2,1,0:T(8,128)(2,1)S(1)}, u32[]{:S(2)}, u32[]{:S(2)}) collective-permute-start(bf16[1,16,9216]{2,1,0:T(8,128)(2,1)S(1)} %pick7.1), channel_id=1, source_target_pairs={{0,1},{1,0},{2,3},{3,2},{4,5},{5,4},{6,7},{7,6},{8,9},{9,8},{10,11... | collective-permute-start | bytes 884744 | tf_op jit(solution)/shard_map/ppermute | solution.py:240

commit v4 on v3

--- a/solution.py
+++ b/solution.py
@@ -249,9 +249,8 @@
         (p1, p2, y0, base0, home_rows, requests, block_slot)
     )
     either = lambda a, b: jnp.where(inner, a, b)
-    m1 = send(either(p2, y0), pairs)
-    p3 = send(p1, middle)
-    n1 = send(either(p2, p1), every)
+    for_m1, for_n1, for_p3 = together((either(p2, y0), either(p2, p1), p1))
+    m1, n1, p3 = send(for_m1, pairs), send(for_n1, every), send(for_p3, middle)
 
     adapters = jnp.arange(home_rows.shape[0], dtype=jnp.int32)
     stored = jnp.sum(
@@ -287,27 +286,28 @@
 
     after = lambda a: together((requests, a))[0]
     base1 = base_part(tokens, base_weight, wide, wide, after(p1))
-    m1, p3, n1, base1, mask, take_mine, take_other = together(
-        (m1, p3, n1, base1, mask, take_mine, take_other)
-    )
-    p5a, n2b = send(p3[:1], outward), send(either(p3, m1)[1:], every)
-    p5b, n2a = send(p3[1:], outward), send(either(p3, m1)[:1], every)
-    y5, w5 = send(p5a, outer_y), send(n2b, outward)
-
+    m1, n1, p3, base1, mask, take_mine, take_other = together(
+        (m1, n1, p3, base1, mask, take_mine, take_other)
+    )
     batches = [
         [(own, 0), (own, 1)],
         [(p1, 0), (p1, 1)],
         [(y0, 0), (y0, 1)],
         [(n1, 0), (n1, 1), (m1, 0), (m1, 1)],
         [(m1, 0), (m1, 1), (p2, 0), (p2, 1)],
+    ]
+    p5a, p5b = send(p3[:1], outward), send(p3[1:], outward)
+    for_n2, first = together((either(p3, m1), picked(take_other, range(5), batches)))
+    n2b, n2a = send(for_n2[1:], every), send(for_n2[:1], every)
+    y5, w5 = send(p5a, outer_y), send(n2b, outward)
+    batches += [
         [(p5a, 0), (p5b, 0), (p3, 0), (p3, 1)],
         [(n2a, 0), (n2b, 0), (n1, 0), (n1, 1)],
         [(y5, 0), (w5, 0), (n2a, 0), (n2b, 0)],
     ]
-    given = []
-    for ids in ((0, 1, 2, 3, 4), (5, 6), (7,)):
-        sent = send(picked(take_other, ids, batches), cores)
-        given += [(sent, row) for row in range(len(ids))]
+    picks = [first] + [picked(take_other, ids, batches) for ids in ((5, 6), (7,))]
+    sent = [send(a, cores) for a in picks]
+    given = [(a, row) for a in sent for row in range(a.shape[0])]
     return finish(take_mine, tokens, mask, [base0, base1], batches, given)
 
 

time: 80.3 us -> 76.8 us (0.956)
  waiting for transfers between devices: 24.8 us -> 21.7 us
  starting transfers between devices: 21.5 us -> 20.6 us
    ppermute x16, waiting for transfers between devices: 24.8 us -> 21.7 us  [gridded(): send = lambda a, p: lax.ppermute(a, 'store', p)]
    ppermute x16, starting transfers between devices: 21.5 us -> 20.6 us  [gridded(): send = lambda a, p: lax.ppermute(a, 'store', p)]
  transfers between devices with their start and end apart: 16 -> 16, of which waited for: 9 -> 8; matrix products, arithmetic and copies ran while one was open for 3% -> 3% of each run, Pallas kernels for 24% -> 27%
where the time goes in v4:
time: 76.8 us; the launch traced here: 76.5 us
  Pallas kernels  30.5 us (40%)
  waiting for transfers between devices  21.7 us (28%)
  starting transfers between devices  20.6 us (27%)
  other arithmetic  2.2 us (3%)
  local copies, waits for them, and re-layouts  1.15 us (1%)
    ppermute x16, waiting for transfers between devices, gridded(): send = lambda a, p: lax.ppermute(a, 'store', p)  21.7 us
    ppermute x16, starting transfers between devices, gridded(): send = lambda a, p: lax.ppermute(a, 'store', p)  20.6 us
    pallas_call x2, Pallas kernels, base_part(): pl.pallas_call(kernel, out_shape=jax.ShapeDtypeStruct((rows, wide), jnp.f...  18.3 us
    pallas_call x1, Pallas kernels, finish(): pl.pallas_call(kernel, out_shape=jax.ShapeDtypeStruct((rows, key_width),...  8.62 us
    pallas_call x3, Pallas kernels, picked(): pl.pallas_call(kernel, out_shape=jax.ShapeDtypeStruct((len(ids), rank, wh...  2.49 us
  transfers between devices with their start and end apart: 16, of which 8 were waited for; matrix products, arithmetic and copies ran while one was open for 3% of the time, Pallas kernels for 27%

profile of v4, /device:TPU:0, one launch (start us, length us, event | category | flops | bytes accessed | tf_op | source)
XLA Modules:
  0.0 76.5 jit_solution(8190588847763341256)
XLA Ops:
  0.0 1.1 %join.1.refs_0_.rest_2_ = bf16[2,16,9216]{2,1,0:T(8,128)(2,1)S(1)} custom-call(bf16[2,16,8192]{2,1,0:T(8,128)(2,1)} %shrink.1, bf16[2,16,1024]{2,1,0:T(8,128)(2,1)} %expand.1), custom_call_target="tpu_custom_call" | custom-call | tf_op jit(solution)/shard_map/join/pallas_call | solution.py:169
  1.1 3.0 %collective-permute-start.2 = (bf16[2,16,9216]{2,1,0:T(8,128)(2,1)S(1)}, bf16[2,16,9216]{2,1,0:T(8,128)(2,1)S(1)}, u32[]{:S(2)}, u32[]{:S(2)}) collective-permute-start(bf16[2,16,9216]{2,1,0:T(8,128)(2,1)S(1)} %join.1.refs_0_.rest_2_), channel_id=1, source_target_pairs={{0,2},{1,3},{2,0},{3,1},{4,6},{5,7},{6,4},{7,5},{8,10},{9,11},{10,... | collective-permute-start | bytes 1769480 | tf_op jit(solution)/shard_map/ppermute | solution.py:240
  4.1 0.7 collective-permute-start.1
  4.8 4.4 %collective-permute-start = (bf16[2,16,9216]{2,1,0:T(8,128)(2,1)S(1)}, bf16[2,16,9216]{2,1,0:T(8,128)(2,1)}, u32[]{:S(2)}, u32[]{:S(2)}) collective-permute-start(bf16[2,16,9216]{2,1,0:T(8,128)(2,1)S(1)} %join.1.refs_0_.rest_2_), channel_id=1, source_target_pairs={{0,4},{1,5},{2,6},{3,7},{4,0},{5,1},{6,2},{7,3},{8,12},{9,13},{10,... | collective-permute-start | bytes 1769480 | tf_op jit(solution)/shard_map/ppermute | solution.py:240
  9.4 0.7 copy-done
  10.1 8.9 %base0.1.rest_0_ = f32[768,512]{1,0:T(8,128)S(1)} custom-call(s32[1,8]{1,0:T(1,128)S(1)} %copy-done, bf16[768,8192]{1,0:T(8,128)(2,1)} %tokens.5, bf16[8192,1024]{1,0:T(8,128)(2,1)} %weight.3), custom_call_target="tpu_custom_call" | custom-call | flops 6442450944 | bytes 8388608 | tf_op jit(solution)/shard_map/base0/pallas_call | solution.py:68
  19.0 3.1 %collective-permute-done.refs_1_.rest_3_ = bf16[2,16,9216]{2,1,0:T(8,128)(2,1)} collective-permute-done((bf16[2,16,9216]{2,1,0:T(8,128)(2,1)S(1)}, bf16[2,16,9216]{2,1,0:T(8,128)(2,1)}, u32[]{:S(2)}, u32[]{:S(2)}) %collective-permute-start) | collective-permute-done | bytes 589856 | tf_op jit(solution)/shard_map/ppermute | solution.py:240
  22.1 0.2 select_reduce_fusion.3
  22.8 1.3 %broadcast_select_fusion.1 = (bf16[2,16,9216]{2,1,0:T(8,128)(2,1)S(1)}, bf16[2,16,9216]{2,1,0:T(8,128)(2,1)S(1)}) fusion(bf16[2,16,9216]{2,1,0:T(8,128)(2,1)S(1)} %collective-permute-done.1.refs_5_.rest_7_, bf16[2,16,9216]{2,1,0:T(8,128)(2,1)} %collective-permute-done.refs_1_.rest_3_, pred[]{:T(512)S(6)} %or.3, ...), kind=kLoop, calls=%fused_computation.2 | loop fusion | flops 589824 | bytes 2949121 | tf_op jit(solution)/shard_map/jit(_where)/select_n | solution.py:251
  24.1 0.6 collective-permute-start.3
  24.7 0.5 collective-permute-start.4
  25.2 0.8 %collective-permute-start.5 = (bf16[2,16,9216]{2,1,0:T(8,128)(2,1)}, bf16[2,16,9216]{2,1,0:T(8,128)(2,1)S(1)}, u32[]{:S(2)}, u32[]{:S(2)}) collective-permute-start(bf16[2,16,9216]{2,1,0:T(8,128)(2,1)} %collective-permute-done.refs_1_.rest_3_), channel_id=1, source_target_pairs={{4,8},{5,9},{6,10},{7,11},{8,4},{9,5},{10,6},{11,7},{20,24},{21,25... | collective-permute-start | bytes 1769480 | tf_op jit(solution)/shard_map/ppermute | solution.py:240
  26.1 9.4 %base512.1.rest_1_ = f32[768,512]{1,0:T(8,128)S(1)} custom-call(s32[1,8]{1,0:T(1,128)S(1)} %copy-done.1, bf16[768,8192]{1,0:T(8,128)(2,1)} %tokens.5, bf16[8192,1024]{1,0:T(8,128)(2,1)} %weight.3), custom_call_target="tpu_custom_call" | custom-call | flops 6442450944 | bytes 8388608 | tf_op jit(solution)/shard_map/base512/pallas_call | solution.py:68
  35.5 0.2 compare_convert_fusion.mask
  35.7 0.2 select_reduce_fusion
  36.0 3.9 %collective-permute-done.3.refs_4_.rest_6_ = bf16[2,16,9216]{2,1,0:T(8,128)(2,1)S(1)} collective-permute-done((bf16[2,16,9216]{2,1,0:T(8,128)(2,1)S(1)}, bf16[2,16,9216]{2,1,0:T(8,128)(2,1)S(1)}, u32[]{:S(2)}, u32[]{:S(2)}) %collective-permute-start.3) | collective-permute-done | bytes 589856 | tf_op jit(solution)/shard_map/ppermute | solution.py:240
  39.9 0.3 collective-permute-done.4.refs_3_.refs_5_.rest_5_
  40.3 1.3 %collective-permute-start.7 = (bf16[1,16,9216]{2,1,0:T(8,128)(2,1)S(1)}, bf16[1,16,9216]{2,1,0:T(8,128)(2,1)S(1)}, u32[]{:S(2)}, u32[]{:S(2)}) collective-permute-start(bf16[1,16,9216]{2,1,0:T(8,128)(2,1)S(1)} %get-tuple-element.50), channel_id=1, source_target_pairs={{4,0},{5,1},{6,2},{7,3},{8,12},{9,13},{10,14},{11,15},{20,16},{21,... | collective-permute-start | bytes 884744 | tf_op jit(solution)/shard_map/ppermute | solution.py:240
  41.6 1.3 %pick0_1_2_3_4.1 = bf16[5,16,9216]{2,1,0:T(8,128)(2,1)S(1)} custom-call(s32[9]{0:T(128)S(1)} %get-tuple-element.42.choice, bf16[2,16,9216]{2,1,0:T(8,128)(2,1)S(1)} %join.1.refs_0_.rest_2_, bf16[2,16,9216]{2,1,0:T(8,128)(2,1)} %collective-permute-done.refs_1_.rest_3_, bf16[2,16,9216]{2,1,0:T(8,128)(2,1)S(1)} %collective-permute-done.2.refs_2_.rest_4_, ...), custom_call_target="tpu_custom_call" | custom-call | tf_op jit(solution)/shard_map/pick0_1_2_3_4/pallas_call | solution.py:212
  43.0 0.6 collective-permute-start.10
  43.6 1.3 %collective-permute-start.8 = (bf16[1,16,9216]{2,1,0:T(8,128)(2,1)S(1)}, bf16[1,16,9216]{2,1,0:T(8,128)(2,1)S(1)}, u32[]{:S(2)}, u32[]{:S(2)}) collective-permute-start(bf16[1,16,9216]{2,1,0:T(8,128)(2,1)S(1)} %get-tuple-element.49), channel_id=1, source_target_pairs={{4,0},{5,1},{6,2},{7,3},{8,12},{9,13},{10,14},{11,15},{20,16},{21,... | collective-permute-start | bytes 884744 | tf_op jit(solution)/shard_map/ppermute | solution.py:240
  44.8 1.6 %collective-permute-start.9 = (bf16[1,16,9216]{2,1,0:T(8,128)(2,1)S(1)}, bf16[1,16,9216]{2,1,0:T(8,128)(2,1)S(1)}, u32[]{:S(2)}, u32[]{:S(2)}) collective-permute-start(bf16[1,16,9216]{2,1,0:T(8,128)(2,1)S(1)} %get-tuple-element.48), channel_id=1, source_target_pairs={{0,2},{1,3},{2,0},{3,1},{4,6},{5,7},{6,4},{7,5},{8,10},{9,11},{10,... | collective-permute-start | bytes 884744 | tf_op jit(solution)/shard_map/ppermute | solution.py:240
  46.4 6.3 %collective-permute-done.7.refs_0_.rest_8_ = bf16[1,16,9216]{2,1,0:T(8,128)(2,1)S(1)} collective-permute-done((bf16[1,16,9216]{2,1,0:T(8,128)(2,1)S(1)}, bf16[1,16,9216]{2,1,0:T(8,128)(2,1)S(1)}, u32[]{:S(2)}, u32[]{:S(2)}) %collective-permute-start.7) | collective-permute-done | bytes 294944 | tf_op jit(solution)/shard_map/ppermute | solution.py:240
  52.7 4.3 %collective-permute-start.11 = (bf16[1,16,9216]{2,1,0:T(8,128)(2,1)S(1)}, bf16[1,16,9216]{2,1,0:T(8,128)(2,1)S(1)}, u32[]{:S(2)}, u32[]{:S(2)}) collective-permute-start(bf16[1,16,9216]{2,1,0:T(8,128)(2,1)S(1)} %collective-permute-done.7.refs_0_.rest_8_), channel_id=1, source_target_pairs={{0,2},{1,3},{2,0},{3,1},{12,14},{13,15},{14,12},{15,13},{16,18},{1... | collective-permute-start | bytes 884744 | tf_op jit(solution)/shard_map/ppermute | solution.py:240
  57.0 1.3 %collective-permute-start.12 = (bf16[1,16,9216]{2,1,0:T(8,128)(2,1)S(1)}, bf16[1,16,9216]{2,1,0:T(8,128)(2,1)S(1)}, u32[]{:S(2)}, u32[]{:S(2)}) collective-permute-start(bf16[1,16,9216]{2,1,0:T(8,128)(2,1)S(1)} %collective-permute-done.10.refs_4_.refs_3_.rest_12_), channel_id=1, source_target_pairs={{4,0},{5,1},{6,2},{7,3},{8,12},{9,13},{10,14},{11,15},{20,16},{21,... | collective-permute-start | bytes 884744 | tf_op jit(solution)/shard_map/ppermute | solution.py:240
  58.3 0.9 %collective-permute-done.9.refs_3_.refs_2_.rest_11_ = bf16[1,16,9216]{2,1,0:T(8,128)(2,1)S(1)} collective-permute-done((bf16[1,16,9216]{2,1,0:T(8,128)(2,1)S(1)}, bf16[1,16,9216]{2,1,0:T(8,128)(2,1)S(1)}, u32[]{:S(2)}, u32[]{:S(2)}) %collective-permute-start.9) | collective-permute-done | bytes 294944 | tf_op jit(solution)/shard_map/ppermute | solution.py:240
  59.2 0.6 pick5_6.1
  59.9 5.2 %collective-permute-done.11.refs_0_.rest_13_ = bf16[1,16,9216]{2,1,0:T(8,128)(2,1)S(1)} collective-permute-done((bf16[1,16,9216]{2,1,0:T(8,128)(2,1)S(1)}, bf16[1,16,9216]{2,1,0:T(8,128)(2,1)S(1)}, u32[]{:S(2)}, u32[]{:S(2)}) %collective-permute-start.11) | collective-permute-done | bytes 294944 | tf_op jit(solution)/shard_map/ppermute | solution.py:240
  65.1 0.5 collective-permute-done.12.refs_1_.rest_14_
  65.6 0.6 pick7.1
  66.3 1.6 %collective-permute-done.15.rest_17_ = bf16[1,16,9216]{2,1,0:T(8,128)(2,1)S(1)} collective-permute-done((bf16[1,16,9216]{2,1,0:T(8,128)(2,1)S(1)}, bf16[1,16,9216]{2,1,0:T(8,128)(2,1)S(1)}, u32[]{:S(2)}, u32[]{:S(2)}) %collective-permute-start.15) | collective-permute-done | bytes 294944 | tf_op jit(solution)/shard_map/ppermute | solution.py:240
  67.9 8.6 %shrink_expand.1 = bf16[768,1024]{1,0:T(8,128)(2,1)} custom-call(s32[9]{0:T(128)S(1)} %get-tuple-element.35.choice, bf16[768,8192]{1,0:T(8,128)(2,1)S(1)} %bitcast.12, bf16[768,256]{1,0:T(8,128)(2,1)S(1)} %compare_convert_fusion.mask, f32[768,512]{1,0:T(8,128)S(1)} %base0.1.rest_0_, f32[768,512]{1,0:T(8,128)S(1)} %base512.1.rest_1_, ...), custom_call_target="tpu_custom_call" | custom-call | flops 3221225472 | bytes 4718592 | tf_op jit(solution)/shard_map/shrink_expand/pallas_call | solution.py:134
  (40 shorter events, 1.1 us)
Async XLA Ops:
  1.1 17.9 %collective-permute-start.2 = (bf16[2,16,9216]{2,1,0:T(8,128)(2,1)S(1)}, bf16[2,16,9216]{2,1,0:T(8,128)(2,1)S(1)}, u32[]{:S(2)}, u32[]{:S(2)}) collective-permute-start(bf16[2,16,9216]{2,1,0:T(8,128)(2,1)S(1)} %join.1.refs_0_.rest_2_), channel_id=1, source_target_pairs={{0,2},{1,3},{2,0},{3,1},{4,6},{5,7},{6,4},{7,5},{8,10},{9,11},{10,... | collective-permute-start | bytes 1769480 | tf_op jit(solution)/shard_map/ppermute | solution.py:240
  4.1 14.9 %collective-permute-start.1 = (bf16[2,16,9216]{2,1,0:T(8,128)(2,1)S(1)}, bf16[2,16,9216]{2,1,0:T(8,128)(2,1)S(1)}, u32[]{:S(2)}, u32[]{:S(2)}) collective-permute-start(bf16[2,16,9216]{2,1,0:T(8,128)(2,1)S(1)} %join.1.refs_0_.rest_2_), channel_id=1, source_target_pairs={{4,8},{5,9},{6,10},{7,11},{8,4},{9,5},{10,6},{11,7},{20,24},{21,25... | collective-permute-start | bytes 1769480 | tf_op jit(solution)/shard_map/ppermute | solution.py:240
  4.8 17.3 %collective-permute-start = (bf16[2,16,9216]{2,1,0:T(8,128)(2,1)S(1)}, bf16[2,16,9216]{2,1,0:T(8,128)(2,1)}, u32[]{:S(2)}, u32[]{:S(2)}) collective-permute-start(bf16[2,16,9216]{2,1,0:T(8,128)(2,1)S(1)} %join.1.refs_0_.rest_2_), channel_id=1, source_target_pairs={{0,4},{1,5},{2,6},{3,7},{4,0},{5,1},{6,2},{7,3},{8,12},{9,13},{10,... | collective-permute-start | bytes 1769480 | tf_op jit(solution)/shard_map/ppermute | solution.py:240
  9.4 0.7 copy-start
  10.1 12.0 %copy-start.3 = (s32[32]{0:T(128)S(1)}, s32[32]{0:T(128)}, u32[]{:S(2)}) copy-start(s32[32]{0:T(128)} %param.11) | copy-start | bytes 388
  10.1 12.6 %copy-start.2 = (s32[1,48]{1,0:T(1,128)S(1)}, s32[1,48]{1,0:T(1,128)}, u32[]{:S(2)}) copy-start(s32[1,48]{1,0:T(1,128)} %param.13) | copy-start | bytes 580
  19.0 7.1 %copy-start.1 = (s32[1,8]{1,0:T(1,128)S(1)}, s32[1,8]{1,0:T(1,128)}, u32[]{:S(2)}) copy-start(s32[1,8]{1,0:T(1,128)} %after.2) | copy-start | bytes 100
  22.3 13.4 %collective-permute-start.6 = (s32[8]{0:T(128)S(1)}, s32[8]{0:T(128)S(1)}, u32[]{:S(2)}, u32[]{:S(2)}) collective-permute-start(s32[8]{0:T(128)S(1)} %select_reduce_fusion.3), channel_id=1, source_target_pairs={{0,1},{1,0},{2,3},{3,2},{4,5},{5,4},{6,7},{7,6},{8,9},{9,8},{10,11... | collective-permute-start | bytes 104 | tf_op jit(solution)/shard_map/ppermute | solution.py:240
  22.8 45.1 %slice-start = ((s8[12582912]{0:T(1024)(128)(4,1)}), s8[4194304]{0:T(1024)(128)(4,1)S(1)}, s32[]{:S(2)}) async-start(s8[12582912]{0:T(1024)(128)(4,1)} %bitcast.11), calls=%async_computation | async-start | bytes 8388608
  24.1 43.8 %slice-start.1 = ((s8[12582912]{0:T(1024)(128)(4,1)}), s8[4194304]{0:T(1024)(128)(4,1)S(1)}, s32[]{:S(2)}) async-start(s8[12582912]{0:T(1024)(128)(4,1)} %bitcast.11), calls=%async_computation.1 | async-start | bytes 8388608
  24.1 43.8 %slice-start.2 = ((s8[12582912]{0:T(1024)(128)(4,1)}), s8[4194304]{0:T(1024)(128)(4,1)S(1)}, s32[]{:S(2)}) async-start(s8[12582912]{0:T(1024)(128)(4,1)} %bitcast.11), calls=%async_computation.2 | async-start | bytes 8388608
  24.1 15.8 %collective-permute-start.3 = (bf16[2,16,9216]{2,1,0:T(8,128)(2,1)S(1)}, bf16[2,16,9216]{2,1,0:T(8,128)(2,1)S(1)}, u32[]{:S(2)}, u32[]{:S(2)}) collective-permute-start(bf16[2,16,9216]{2,1,0:T(8,128)(2,1)S(1)} %get-tuple-element.28), channel_id=1, source_target_pairs={{0,4},{1,5},{2,6},{3,7},{4,0},{5,1},{6,2},{7,3},{8,12},{9,13},{10,... | collective-permute-start | bytes 1769480 | tf_op jit(solution)/shard_map/ppermute | solution.py:240
  24.7 15.4 %collective-permute-start.4 = (bf16[2,16,9216]{2,1,0:T(8,128)(2,1)S(1)}, bf16[2,16,9216]{2,1,0:T(8,128)(2,1)S(1)}, u32[]{:S(2)}, u32[]{:S(2)}) collective-permute-start(bf16[2,16,9216]{2,1,0:T(8,128)(2,1)S(1)} %get-tuple-element.29), channel_id=1, source_target_pairs={{0,2},{1,3},{2,0},{3,1},{4,6},{5,7},{6,4},{7,5},{8,10},{9,11},{10,... | collective-permute-start | bytes 1769480 | tf_op jit(solution)/shard_map/ppermute | solution.py:240
  25.2 14.9 %collective-permute-start.5 = (bf16[2,16,9216]{2,1,0:T(8,128)(2,1)}, bf16[2,16,9216]{2,1,0:T(8,128)(2,1)S(1)}, u32[]{:S(2)}, u32[]{:S(2)}) collective-permute-start(bf16[2,16,9216]{2,1,0:T(8,128)(2,1)} %collective-permute-done.refs_1_.rest_3_), channel_id=1, source_target_pairs={{4,8},{5,9},{6,10},{7,11},{8,4},{9,5},{10,6},{11,7},{20,24},{21,25... | collective-permute-start | bytes 1769480 | tf_op jit(solution)/shard_map/ppermute | solution.py:240
  40.3 12.4 %collective-permute-start.7 = (bf16[1,16,9216]{2,1,0:T(8,128)(2,1)S(1)}, bf16[1,16,9216]{2,1,0:T(8,128)(2,1)S(1)}, u32[]{:S(2)}, u32[]{:S(2)}) collective-permute-start(bf16[1,16,9216]{2,1,0:T(8,128)(2,1)S(1)} %get-tuple-element.50), channel_id=1, source_target_pairs={{4,0},{5,1},{6,2},{7,3},{8,12},{9,13},{10,14},{11,15},{20,16},{21,... | collective-permute-start | bytes 884744 | tf_op jit(solution)/shard_map/ppermute | solution.py:240
  42.9 25.0 %collective-permute-start.13 = (bf16[5,16,9216]{2,1,0:T(8,128)(2,1)S(1)}, bf16[5,16,9216]{2,1,0:T(8,128)(2,1)S(1)}, u32[]{:S(2)}, u32[]{:S(2)}) collective-permute-start(bf16[5,16,9216]{2,1,0:T(8,128)(2,1)S(1)} %pick0_1_2_3_4.1), channel_id=1, source_target_pairs={{0,1},{1,0},{2,3},{3,2},{4,5},{5,4},{6,7},{7,6},{8,9},{9,8},{10,11... | collective-permute-start | bytes 4423688 | tf_op jit(solution)/shard_map/ppermute | solution.py:240
  43.0 14.0 %collective-permute-start.10 = (bf16[1,16,9216]{2,1,0:T(8,128)(2,1)S(1)}, bf16[1,16,9216]{2,1,0:T(8,128)(2,1)S(1)}, u32[]{:S(2)}, u32[]{:S(2)}) collective-permute-start(bf16[1,16,9216]{2,1,0:T(8,128)(2,1)S(1)} %get-tuple-element.47), channel_id=1, source_target_pairs={{0,2},{1,3},{2,0},{3,1},{4,6},{5,7},{6,4},{7,5},{8,10},{9,11},{10,... | collective-permute-start | bytes 884744 | tf_op jit(solution)/shard_map/ppermute | solution.py:240
  43.6 14.7 %collective-permute-start.8 = (bf16[1,16,9216]{2,1,0:T(8,128)(2,1)S(1)}, bf16[1,16,9216]{2,1,0:T(8,128)(2,1)S(1)}, u32[]{:S(2)}, u32[]{:S(2)}) collective-permute-start(bf16[1,16,9216]{2,1,0:T(8,128)(2,1)S(1)} %get-tuple-element.49), channel_id=1, source_target_pairs={{4,0},{5,1},{6,2},{7,3},{8,12},{9,13},{10,14},{11,15},{20,16},{21,... | collective-permute-start | bytes 884744 | tf_op jit(solution)/shard_map/ppermute | solution.py:240
  44.8 14.3 %collective-permute-start.9 = (bf16[1,16,9216]{2,1,0:T(8,128)(2,1)S(1)}, bf16[1,16,9216]{2,1,0:T(8,128)(2,1)S(1)}, u32[]{:S(2)}, u32[]{:S(2)}) collective-permute-start(bf16[1,16,9216]{2,1,0:T(8,128)(2,1)S(1)} %get-tuple-element.48), channel_id=1, source_target_pairs={{0,2},{1,3},{2,0},{3,1},{4,6},{5,7},{6,4},{7,5},{8,10},{9,11},{10,... | collective-permute-start | bytes 884744 | tf_op jit(solution)/shard_map/ppermute | solution.py:240
  52.7 12.4 %collective-permute-start.11 = (bf16[1,16,9216]{2,1,0:T(8,128)(2,1)S(1)}, bf16[1,16,9216]{2,1,0:T(8,128)(2,1)S(1)}, u32[]{:S(2)}, u32[]{:S(2)}) collective-permute-start(bf16[1,16,9216]{2,1,0:T(8,128)(2,1)S(1)} %collective-permute-done.7.refs_0_.rest_8_), channel_id=1, source_target_pairs={{0,2},{1,3},{2,0},{3,1},{12,14},{13,15},{14,12},{15,13},{16,18},{1... | collective-permute-start | bytes 884744 | tf_op jit(solution)/shard_map/ppermute | solution.py:240
  57.0 8.6 %collective-permute-start.12 = (bf16[1,16,9216]{2,1,0:T(8,128)(2,1)S(1)}, bf16[1,16,9216]{2,1,0:T(8,128)(2,1)S(1)}, u32[]{:S(2)}, u32[]{:S(2)}) collective-permute-start(bf16[1,16,9216]{2,1,0:T(8,128)(2,1)S(1)} %collective-permute-done.10.refs_4_.refs_3_.rest_12_), channel_id=1, source_target_pairs={{4,0},{5,1},{6,2},{7,3},{8,12},{9,13},{10,14},{11,15},{20,16},{21,... | collective-permute-start | bytes 884744 | tf_op jit(solution)/shard_map/ppermute | solution.py:240
  59.8 8.0 %collective-permute-start.14 = (bf16[2,16,9216]{2,1,0:T(8,128)(2,1)S(1)}, bf16[2,16,9216]{2,1,0:T(8,128)(2,1)S(1)}, u32[]{:S(2)}, u32[]{:S(2)}) collective-permute-start(bf16[2,16,9216]{2,1,0:T(8,128)(2,1)S(1)} %pick5_6.1), channel_id=1, source_target_pairs={{0,1},{1,0},{2,3},{3,2},{4,5},{5,4},{6,7},{7,6},{8,9},{9,8},{10,11... | collective-permute-start | bytes 1769480 | tf_op jit(solution)/shard_map/ppermute | solution.py:240
  66.2 1.6 %collective-permute-start.15 = (bf16[1,16,9216]{2,1,0:T(8,128)(2,1)S(1)}, bf16[1,16,9216]{2,1,0:T(8,128)(2,1)S(1)}, u32[]{:S(2)}, u32[]{:S(2)}) collective-permute-start(bf16[1,16,9216]{2,1,0:T(8,128)(2,1)S(1)} %pick7.1), channel_id=1, source_target_pairs={{0,1},{1,0},{2,3},{3,2},{4,5},{5,4},{6,7},{7,6},{8,9},{9,8},{10,11... | collective-permute-start | bytes 884744 | tf_op jit(solution)/shard_map/ppermute | solution.py:240

commit v5 on v4

--- a/solution.py
+++ b/solution.py
@@ -92,12 +92,15 @@
     pieces = len(bases)
     entries = [entry for batch in batches for entry in batch] + given
     arrays, spots = listed(entries)
+    parts = 2 * pieces
+    wide = key_width // parts
     owners = [(i, k, len(batch) > 2) for i, batch in enumerate(batches) for k in range(len(batch))]
     owners += [(len(batches) + i, None, False) for i in range(len(given))]
     places = [(i, buf, row, k, levels) for (i, k, levels), (buf, row) in zip(owners, spots)]
 
     def kernel(choice, tokens, mask, *rest):
-        base_refs, bufs, (out, table) = rest[:pieces], rest[pieces:-2], rest[-2:]
+        base_refs, bufs = rest[:pieces], rest[pieces:-4]
+        out, table, done, left = rest[-4:]
         for i, buf, row, k, levels in places:
             at = pl.ds(rank * i, rank)
             if k is None:
@@ -120,14 +123,21 @@
         shrink = shrink * mask[...].astype(jnp.float32)
         high = shrink.astype(jnp.bfloat16)
         low = (shrink - high.astype(jnp.float32)).astype(jnp.bfloat16)
-        start = 0
-        for base in base_refs:
-            wide = base.shape[1]
+        copies = []
+        for i in range(parts):
+            start = wide * i
+            each = parts // pieces
+            base = base_refs[i // each][:, pl.ds(wide * (i % each), wide)]
             cols = pl.ds(width + start, wide)
             part = jnp.dot(high, table[:, cols], preferred_element_type=jnp.float32)
             part += jnp.dot(low, table[:, cols], preferred_element_type=jnp.float32)
-            out[:, pl.ds(start, wide)] = (base[...] + part).astype(out.dtype)
-            start += wide
+            done[i] = (base + part).astype(out.dtype)
+            copies.append(
+                pltpu.make_async_copy(done.at[i], out.at[:, pl.ds(start, wide)], left.at[i])
+            )
+            copies[-1].start()
+        for copy in copies:
+            copy.wait()
 
     vmem = pl.BlockSpec(memory_space=pltpu.VMEM)
     pin = lambda a: pltpu.with_memory_space_constraint(a, pltpu.VMEM)
@@ -137,9 +147,11 @@
         in_specs=[pl.BlockSpec(memory_space=pltpu.SMEM)]
         + [vmem] * (2 + pieces)
         + [vmem] * len(arrays),
-        out_specs=vmem,
+        out_specs=pl.BlockSpec(memory_space=pl.ANY),
         scratch_shapes=[
             pltpu.VMEM((rank * count, whole), jnp.bfloat16),
+            pltpu.VMEM((parts, rows, wide), jnp.bfloat16),
+            pltpu.SemaphoreType.DMA((parts,)),
         ],
         compiler_params=pltpu.CompilerParams(vmem_limit_bytes=24 << 20),
         cost_estimate=pl.CostEstimate(

time: 76.8 us -> 76.6 us (level)
  no operation moved by 1% of the time
where the time goes in v5:
time: 76.6 us; the launch traced here: 76.3 us
  Pallas kernels  30.2 us (39%)
  waiting for transfers between devices  21.7 us (28%)
  starting transfers between devices  20.6 us (27%)
  other arithmetic  2.2 us (3%)
  local copies, waits for them, and re-layouts  1.15 us (2%)
    ppermute x16, waiting for transfers between devices, gridded(): send = lambda a, p: lax.ppermute(a, 'store', p)  21.7 us
    ppermute x16, starting transfers between devices, gridded(): send = lambda a, p: lax.ppermute(a, 'store', p)  20.6 us
    pallas_call x2, Pallas kernels, base_part(): pl.pallas_call(kernel, out_shape=jax.ShapeDtypeStruct((rows, wide), jnp.f...  18.3 us
    pallas_call x1, Pallas kernels, finish(): pl.pallas_call(kernel, out_shape=jax.ShapeDtypeStruct((rows, key_width),...  8.26 us
    pallas_call x3, Pallas kernels, picked(): pl.pallas_call(kernel, out_shape=jax.ShapeDtypeStruct((len(ids), rank, wh...  2.49 us
  transfers between devices with their start and end apart: 16, of which 8 were waited for; matrix products, arithmetic and copies ran while one was open for 3% of the time, Pallas kernels for 27%

profile of v5, /device:TPU:0, one launch (start us, length us, event | category | flops | bytes accessed | tf_op | source)
XLA Modules:
  0.0 76.3 jit_solution(3733098201986247375)
XLA Ops:
  0.0 1.1 %join.1.refs_0_.rest_2_ = bf16[2,16,9216]{2,1,0:T(8,128)(2,1)S(1)} custom-call(bf16[2,16,8192]{2,1,0:T(8,128)(2,1)} %shrink.1, bf16[2,16,1024]{2,1,0:T(8,128)(2,1)} %expand.1), custom_call_target="tpu_custom_call" | custom-call | tf_op jit(solution)/shard_map/join/pallas_call | solution.py:181
  1.1 3.0 %collective-permute-start.2 = (bf16[2,16,9216]{2,1,0:T(8,128)(2,1)S(1)}, bf16[2,16,9216]{2,1,0:T(8,128)(2,1)S(1)}, u32[]{:S(2)}, u32[]{:S(2)}) collective-permute-start(bf16[2,16,9216]{2,1,0:T(8,128)(2,1)S(1)} %join.1.refs_0_.rest_2_), channel_id=1, source_target_pairs={{0,2},{1,3},{2,0},{3,1},{4,6},{5,7},{6,4},{7,5},{8,10},{9,11},{10,... | collective-permute-start | bytes 1769480 | tf_op jit(solution)/shard_map/ppermute | solution.py:252
  4.1 0.7 collective-permute-start.1
  4.8 4.4 %collective-permute-start = (bf16[2,16,9216]{2,1,0:T(8,128)(2,1)S(1)}, bf16[2,16,9216]{2,1,0:T(8,128)(2,1)}, u32[]{:S(2)}, u32[]{:S(2)}) collective-permute-start(bf16[2,16,9216]{2,1,0:T(8,128)(2,1)S(1)} %join.1.refs_0_.rest_2_), channel_id=1, source_target_pairs={{0,4},{1,5},{2,6},{3,7},{4,0},{5,1},{6,2},{7,3},{8,12},{9,13},{10,... | collective-permute-start | bytes 1769480 | tf_op jit(solution)/shard_map/ppermute | solution.py:252
  9.4 0.7 copy-done
  10.1 8.9 %base0.1.rest_0_ = f32[768,512]{1,0:T(8,128)S(1)} custom-call(s32[1,8]{1,0:T(1,128)S(1)} %copy-done, bf16[768,8192]{1,0:T(8,128)(2,1)} %tokens.5, bf16[8192,1024]{1,0:T(8,128)(2,1)} %weight.3), custom_call_target="tpu_custom_call" | custom-call | flops 6442450944 | bytes 8388608 | tf_op jit(solution)/shard_map/base0/pallas_call | solution.py:68
  19.0 3.1 %collective-permute-done.refs_1_.rest_3_ = bf16[2,16,9216]{2,1,0:T(8,128)(2,1)} collective-permute-done((bf16[2,16,9216]{2,1,0:T(8,128)(2,1)S(1)}, bf16[2,16,9216]{2,1,0:T(8,128)(2,1)}, u32[]{:S(2)}, u32[]{:S(2)}) %collective-permute-start) | collective-permute-done | bytes 589856 | tf_op jit(solution)/shard_map/ppermute | solution.py:252
  22.1 0.2 select_reduce_fusion.3
  22.8 1.3 %broadcast_select_fusion.1 = (bf16[2,16,9216]{2,1,0:T(8,128)(2,1)S(1)}, bf16[2,16,9216]{2,1,0:T(8,128)(2,1)S(1)}) fusion(bf16[2,16,9216]{2,1,0:T(8,128)(2,1)S(1)} %collective-permute-done.1.refs_5_.rest_7_, bf16[2,16,9216]{2,1,0:T(8,128)(2,1)} %collective-permute-done.refs_1_.rest_3_, pred[]{:T(512)S(6)} %or.3, ...), kind=kLoop, calls=%fused_computation.2 | loop fusion | flops 589824 | bytes 2949121 | tf_op jit(solution)/shard_map/jit(_where)/select_n | solution.py:263
  24.1 0.6 collective-permute-start.3
  24.7 0.5 collective-permute-start.4
  25.2 0.8 %collective-permute-start.5 = (bf16[2,16,9216]{2,1,0:T(8,128)(2,1)}, bf16[2,16,9216]{2,1,0:T(8,128)(2,1)S(1)}, u32[]{:S(2)}, u32[]{:S(2)}) collective-permute-start(bf16[2,16,9216]{2,1,0:T(8,128)(2,1)} %collective-permute-done.refs_1_.rest_3_), channel_id=1, source_target_pairs={{4,8},{5,9},{6,10},{7,11},{8,4},{9,5},{10,6},{11,7},{20,24},{21,25... | collective-permute-start | bytes 1769480 | tf_op jit(solution)/shard_map/ppermute | solution.py:252
  26.1 9.4 %base512.1.rest_1_ = f32[768,512]{1,0:T(8,128)S(1)} custom-call(s32[1,8]{1,0:T(1,128)S(1)} %copy-done.1, bf16[768,8192]{1,0:T(8,128)(2,1)} %tokens.5, bf16[8192,1024]{1,0:T(8,128)(2,1)} %weight.3), custom_call_target="tpu_custom_call" | custom-call | flops 6442450944 | bytes 8388608 | tf_op jit(solution)/shard_map/base512/pallas_call | solution.py:68
  35.5 0.2 compare_convert_fusion.mask
  35.7 0.2 select_reduce_fusion
  36.0 3.9 %collective-permute-done.3.refs_4_.rest_6_ = bf16[2,16,9216]{2,1,0:T(8,128)(2,1)S(1)} collective-permute-done((bf16[2,16,9216]{2,1,0:T(8,128)(2,1)S(1)}, bf16[2,16,9216]{2,1,0:T(8,128)(2,1)S(1)}, u32[]{:S(2)}, u32[]{:S(2)}) %collective-permute-start.3) | collective-permute-done | bytes 589856 | tf_op jit(solution)/shard_map/ppermute | solution.py:252
  39.9 0.3 collective-permute-done.4.refs_3_.refs_5_.rest_5_
  40.3 1.3 %collective-permute-start.7 = (bf16[1,16,9216]{2,1,0:T(8,128)(2,1)S(1)}, bf16[1,16,9216]{2,1,0:T(8,128)(2,1)S(1)}, u32[]{:S(2)}, u32[]{:S(2)}) collective-permute-start(bf16[1,16,9216]{2,1,0:T(8,128)(2,1)S(1)} %get-tuple-element.50), channel_id=1, source_target_pairs={{4,0},{5,1},{6,2},{7,3},{8,12},{9,13},{10,14},{11,15},{20,16},{21,... | collective-permute-start | bytes 884744 | tf_op jit(solution)/shard_map/ppermute | solution.py:252
  41.6 1.3 %pick0_1_2_3_4.1 = bf16[5,16,9216]{2,1,0:T(8,128)(2,1)S(1)} custom-call(s32[9]{0:T(128)S(1)} %get-tuple-element.42.choice, bf16[2,16,9216]{2,1,0:T(8,128)(2,1)S(1)} %join.1.refs_0_.rest_2_, bf16[2,16,9216]{2,1,0:T(8,128)(2,1)} %collective-permute-done.refs_1_.rest_3_, bf16[2,16,9216]{2,1,0:T(8,128)(2,1)S(1)} %collective-permute-done.2.refs_2_.rest_4_, ...), custom_call_target="tpu_custom_call" | custom-call | tf_op jit(solution)/shard_map/pick0_1_2_3_4/pallas_call | solution.py:224
  43.0 0.6 collective-permute-start.10
  43.6 1.3 %collective-permute-start.8 = (bf16[1,16,9216]{2,1,0:T(8,128)(2,1)S(1)}, bf16[1,16,9216]{2,1,0:T(8,128)(2,1)S(1)}, u32[]{:S(2)}, u32[]{:S(2)}) collective-permute-start(bf16[1,16,9216]{2,1,0:T(8,128)(2,1)S(1)} %get-tuple-element.49), channel_id=1, source_target_pairs={{4,0},{5,1},{6,2},{7,3},{8,12},{9,13},{10,14},{11,15},{20,16},{21,... | collective-permute-start | bytes 884744 | tf_op jit(solution)/shard_map/ppermute | solution.py:252
  44.8 1.6 %collective-permute-start.9 = (bf16[1,16,9216]{2,1,0:T(8,128)(2,1)S(1)}, bf16[1,16,9216]{2,1,0:T(8,128)(2,1)S(1)}, u32[]{:S(2)}, u32[]{:S(2)}) collective-permute-start(bf16[1,16,9216]{2,1,0:T(8,128)(2,1)S(1)} %get-tuple-element.48), channel_id=1, source_target_pairs={{0,2},{1,3},{2,0},{3,1},{4,6},{5,7},{6,4},{7,5},{8,10},{9,11},{10,... | collective-permute-start | bytes 884744 | tf_op jit(solution)/shard_map/ppermute | solution.py:252
  46.4 6.3 %collective-permute-done.7.refs_0_.rest_8_ = bf16[1,16,9216]{2,1,0:T(8,128)(2,1)S(1)} collective-permute-done((bf16[1,16,9216]{2,1,0:T(8,128)(2,1)S(1)}, bf16[1,16,9216]{2,1,0:T(8,128)(2,1)S(1)}, u32[]{:S(2)}, u32[]{:S(2)}) %collective-permute-start.7) | collective-permute-done | bytes 294944 | tf_op jit(solution)/shard_map/ppermute | solution.py:252
  52.7 4.3 %collective-permute-start.11 = (bf16[1,16,9216]{2,1,0:T(8,128)(2,1)S(1)}, bf16[1,16,9216]{2,1,0:T(8,128)(2,1)S(1)}, u32[]{:S(2)}, u32[]{:S(2)}) collective-permute-start(bf16[1,16,9216]{2,1,0:T(8,128)(2,1)S(1)} %collective-permute-done.7.refs_0_.rest_8_), channel_id=1, source_target_pairs={{0,2},{1,3},{2,0},{3,1},{12,14},{13,15},{14,12},{15,13},{16,18},{1... | collective-permute-start | bytes 884744 | tf_op jit(solution)/shard_map/ppermute | solution.py:252
  57.0 1.3 %collective-permute-start.12 = (bf16[1,16,9216]{2,1,0:T(8,128)(2,1)S(1)}, bf16[1,16,9216]{2,1,0:T(8,128)(2,1)S(1)}, u32[]{:S(2)}, u32[]{:S(2)}) collective-permute-start(bf16[1,16,9216]{2,1,0:T(8,128)(2,1)S(1)} %collective-permute-done.10.refs_4_.refs_3_.rest_12_), channel_id=1, source_target_pairs={{4,0},{5,1},{6,2},{7,3},{8,12},{9,13},{10,14},{11,15},{20,16},{21,... | collective-permute-start | bytes 884744 | tf_op jit(solution)/shard_map/ppermute | solution.py:252
  58.3 0.9 %collective-permute-done.9.refs_3_.refs_2_.rest_11_ = bf16[1,16,9216]{2,1,0:T(8,128)(2,1)S(1)} collective-permute-done((bf16[1,16,9216]{2,1,0:T(8,128)(2,1)S(1)}, bf16[1,16,9216]{2,1,0:T(8,128)(2,1)S(1)}, u32[]{:S(2)}, u32[]{:S(2)}) %collective-permute-start.9) | collective-permute-done | bytes 294944 | tf_op jit(solution)/shard_map/ppermute | solution.py:252
  59.2 0.6 pick5_6.1
  59.9 5.2 %collective-permute-done.11.refs_0_.rest_13_ = bf16[1,16,9216]{2,1,0:T(8,128)(2,1)S(1)} collective-permute-done((bf16[1,16,9216]{2,1,0:T(8,128)(2,1)S(1)}, bf16[1,16,9216]{2,1,0:T(8,128)(2,1)S(1)}, u32[]{:S(2)}, u32[]{:S(2)}) %collective-permute-start.11) | collective-permute-done | bytes 294944 | tf_op jit(solution)/shard_map/ppermute | solution.py:252
  65.1 0.5 collective-permute-done.12.refs_1_.rest_14_
  65.6 0.6 pick7.1
  66.3 1.6 %collective-permute-done.15.rest_17_ = bf16[1,16,9216]{2,1,0:T(8,128)(2,1)S(1)} collective-permute-done((bf16[1,16,9216]{2,1,0:T(8,128)(2,1)S(1)}, bf16[1,16,9216]{2,1,0:T(8,128)(2,1)S(1)}, u32[]{:S(2)}, u32[]{:S(2)}) %collective-permute-start.15) | collective-permute-done | bytes 294944 | tf_op jit(solution)/shard_map/ppermute | solution.py:252
  67.9 8.3 %shrink_expand.1 = bf16[768,1024]{1,0:T(8,128)(2,1)} custom-call(s32[9]{0:T(128)S(1)} %get-tuple-element.35.choice, bf16[768,8192]{1,0:T(8,128)(2,1)S(1)} %bitcast.12, bf16[768,256]{1,0:T(8,128)(2,1)S(1)} %compare_convert_fusion.mask, f32[768,512]{1,0:T(8,128)S(1)} %base0.1.rest_0_, f32[768,512]{1,0:T(8,128)S(1)} %base512.1.rest_1_, ...), custom_call_target="tpu_custom_call" | custom-call | flops 3221225472 | bytes 4718592 | tf_op jit(solution)/shard_map/shrink_expand/pallas_call | solution.py:144
  (40 shorter events, 1.1 us)
Async XLA Ops:
  1.1 17.9 %collective-permute-start.2 = (bf16[2,16,9216]{2,1,0:T(8,128)(2,1)S(1)}, bf16[2,16,9216]{2,1,0:T(8,128)(2,1)S(1)}, u32[]{:S(2)}, u32[]{:S(2)}) collective-permute-start(bf16[2,16,9216]{2,1,0:T(8,128)(2,1)S(1)} %join.1.refs_0_.rest_2_), channel_id=1, source_target_pairs={{0,2},{1,3},{2,0},{3,1},{4,6},{5,7},{6,4},{7,5},{8,10},{9,11},{10,... | collective-permute-start | bytes 1769480 | tf_op jit(solution)/shard_map/ppermute | solution.py:252
  4.1 14.9 %collective-permute-start.1 = (bf16[2,16,9216]{2,1,0:T(8,128)(2,1)S(1)}, bf16[2,16,9216]{2,1,0:T(8,128)(2,1)S(1)}, u32[]{:S(2)}, u32[]{:S(2)}) collective-permute-start(bf16[2,16,9216]{2,1,0:T(8,128)(2,1)S(1)} %join.1.refs_0_.rest_2_), channel_id=1, source_target_pairs={{4,8},{5,9},{6,10},{7,11},{8,4},{9,5},{10,6},{11,7},{20,24},{21,25... | collective-permute-start | bytes 1769480 | tf_op jit(solution)/shard_map/ppermute | solution.py:252
  4.8 17.3 %collective-permute-start = (bf16[2,16,9216]{2,1,0:T(8,128)(2,1)S(1)}, bf16[2,16,9216]{2,1,0:T(8,128)(2,1)}, u32[]{:S(2)}, u32[]{:S(2)}) collective-permute-start(bf16[2,16,9216]{2,1,0:T(8,128)(2,1)S(1)} %join.1.refs_0_.rest_2_), channel_id=1, source_target_pairs={{0,4},{1,5},{2,6},{3,7},{4,0},{5,1},{6,2},{7,3},{8,12},{9,13},{10,... | collective-permute-start | bytes 1769480 | tf_op jit(solution)/shard_map/ppermute | solution.py:252
  9.4 0.7 copy-start
  10.1 12.0 %copy-start.3 = (s32[32]{0:T(128)S(1)}, s32[32]{0:T(128)}, u32[]{:S(2)}) copy-start(s32[32]{0:T(128)} %param.11) | copy-start | bytes 388
  10.1 12.6 %copy-start.2 = (s32[1,48]{1,0:T(1,128)S(1)}, s32[1,48]{1,0:T(1,128)}, u32[]{:S(2)}) copy-start(s32[1,48]{1,0:T(1,128)} %param.13) | copy-start | bytes 580
  19.0 7.1 %copy-start.1 = (s32[1,8]{1,0:T(1,128)S(1)}, s32[1,8]{1,0:T(1,128)}, u32[]{:S(2)}) copy-start(s32[1,8]{1,0:T(1,128)} %after.2) | copy-start | bytes 100
  22.3 13.4 %collective-permute-start.6 = (s32[8]{0:T(128)S(1)}, s32[8]{0:T(128)S(1)}, u32[]{:S(2)}, u32[]{:S(2)}) collective-permute-start(s32[8]{0:T(128)S(1)} %select_reduce_fusion.3), channel_id=1, source_target_pairs={{0,1},{1,0},{2,3},{3,2},{4,5},{5,4},{6,7},{7,6},{8,9},{9,8},{10,11... | collective-permute-start | bytes 104 | tf_op jit(solution)/shard_map/ppermute | solution.py:252
  22.8 45.1 %slice-start = ((s8[12582912]{0:T(1024)(128)(4,1)}), s8[4194304]{0:T(1024)(128)(4,1)S(1)}, s32[]{:S(2)}) async-start(s8[12582912]{0:T(1024)(128)(4,1)} %bitcast.11), calls=%async_computation | async-start | bytes 8388608
  24.1 43.8 %slice-start.1 = ((s8[12582912]{0:T(1024)(128)(4,1)}), s8[4194304]{0:T(1024)(128)(4,1)S(1)}, s32[]{:S(2)}) async-start(s8[12582912]{0:T(1024)(128)(4,1)} %bitcast.11), calls=%async_computation.1 | async-start | bytes 8388608
  24.1 43.8 %slice-start.2 = ((s8[12582912]{0:T(1024)(128)(4,1)}), s8[4194304]{0:T(1024)(128)(4,1)S(1)}, s32[]{:S(2)}) async-start(s8[12582912]{0:T(1024)(128)(4,1)} %bitcast.11), calls=%async_computation.2 | async-start | bytes 8388608
  24.1 15.8 %collective-permute-start.3 = (bf16[2,16,9216]{2,1,0:T(8,128)(2,1)S(1)}, bf16[2,16,9216]{2,1,0:T(8,128)(2,1)S(1)}, u32[]{:S(2)}, u32[]{:S(2)}) collective-permute-start(bf16[2,16,9216]{2,1,0:T(8,128)(2,1)S(1)} %get-tuple-element.28), channel_id=1, source_target_pairs={{0,4},{1,5},{2,6},{3,7},{4,0},{5,1},{6,2},{7,3},{8,12},{9,13},{10,... | collective-permute-start | bytes 1769480 | tf_op jit(solution)/shard_map/ppermute | solution.py:252
  24.7 15.4 %collective-permute-start.4 = (bf16[2,16,9216]{2,1,0:T(8,128)(2,1)S(1)}, bf16[2,16,9216]{2,1,0:T(8,128)(2,1)S(1)}, u32[]{:S(2)}, u32[]{:S(2)}) collective-permute-start(bf16[2,16,9216]{2,1,0:T(8,128)(2,1)S(1)} %get-tuple-element.29), channel_id=1, source_target_pairs={{0,2},{1,3},{2,0},{3,1},{4,6},{5,7},{6,4},{7,5},{8,10},{9,11},{10,... | collective-permute-start | bytes 1769480 | tf_op jit(solution)/shard_map/ppermute | solution.py:252
  25.2 14.9 %collective-permute-start.5 = (bf16[2,16,9216]{2,1,0:T(8,128)(2,1)}, bf16[2,16,9216]{2,1,0:T(8,128)(2,1)S(1)}, u32[]{:S(2)}, u32[]{:S(2)}) collective-permute-start(bf16[2,16,9216]{2,1,0:T(8,128)(2,1)} %collective-permute-done.refs_1_.rest_3_), channel_id=1, source_target_pairs={{4,8},{5,9},{6,10},{7,11},{8,4},{9,5},{10,6},{11,7},{20,24},{21,25... | collective-permute-start | bytes 1769480 | tf_op jit(solution)/shard_map/ppermute | solution.py:252
  40.3 12.4 %collective-permute-start.7 = (bf16[1,16,9216]{2,1,0:T(8,128)(2,1)S(1)}, bf16[1,16,9216]{2,1,0:T(8,128)(2,1)S(1)}, u32[]{:S(2)}, u32[]{:S(2)}) collective-permute-start(bf16[1,16,9216]{2,1,0:T(8,128)(2,1)S(1)} %get-tuple-element.50), channel_id=1, source_target_pairs={{4,0},{5,1},{6,2},{7,3},{8,12},{9,13},{10,14},{11,15},{20,16},{21,... | collective-permute-start | bytes 884744 | tf_op jit(solution)/shard_map/ppermute | solution.py:252
  42.9 25.0 %collective-permute-start.13 = (bf16[5,16,9216]{2,1,0:T(8,128)(2,1)S(1)}, bf16[5,16,9216]{2,1,0:T(8,128)(2,1)S(1)}, u32[]{:S(2)}, u32[]{:S(2)}) collective-permute-start(bf16[5,16,9216]{2,1,0:T(8,128)(2,1)S(1)} %pick0_1_2_3_4.1), channel_id=1, source_target_pairs={{0,1},{1,0},{2,3},{3,2},{4,5},{5,4},{6,7},{7,6},{8,9},{9,8},{10,11... | collective-permute-start | bytes 4423688 | tf_op jit(solution)/shard_map/ppermute | solution.py:252
  43.0 14.0 %collective-permute-start.10 = (bf16[1,16,9216]{2,1,0:T(8,128)(2,1)S(1)}, bf16[1,16,9216]{2,1,0:T(8,128)(2,1)S(1)}, u32[]{:S(2)}, u32[]{:S(2)}) collective-permute-start(bf16[1,16,9216]{2,1,0:T(8,128)(2,1)S(1)} %get-tuple-element.47), channel_id=1, source_target_pairs={{0,2},{1,3},{2,0},{3,1},{4,6},{5,7},{6,4},{7,5},{8,10},{9,11},{10,... | collective-permute-start | bytes 884744 | tf_op jit(solution)/shard_map/ppermute | solution.py:252
  43.6 14.7 %collective-permute-start.8 = (bf16[1,16,9216]{2,1,0:T(8,128)(2,1)S(1)}, bf16[1,16,9216]{2,1,0:T(8,128)(2,1)S(1)}, u32[]{:S(2)}, u32[]{:S(2)}) collective-permute-start(bf16[1,16,9216]{2,1,0:T(8,128)(2,1)S(1)} %get-tuple-element.49), channel_id=1, source_target_pairs={{4,0},{5,1},{6,2},{7,3},{8,12},{9,13},{10,14},{11,15},{20,16},{21,... | collective-permute-start | bytes 884744 | tf_op jit(solution)/shard_map/ppermute | solution.py:252
  44.8 14.3 %collective-permute-start.9 = (bf16[1,16,9216]{2,1,0:T(8,128)(2,1)S(1)}, bf16[1,16,9216]{2,1,0:T(8,128)(2,1)S(1)}, u32[]{:S(2)}, u32[]{:S(2)}) collective-permute-start(bf16[1,16,9216]{2,1,0:T(8,128)(2,1)S(1)} %get-tuple-element.48), channel_id=1, source_target_pairs={{0,2},{1,3},{2,0},{3,1},{4,6},{5,7},{6,4},{7,5},{8,10},{9,11},{10,... | collective-permute-start | bytes 884744 | tf_op jit(solution)/shard_map/ppermute | solution.py:252
  52.7 12.4 %collective-permute-start.11 = (bf16[1,16,9216]{2,1,0:T(8,128)(2,1)S(1)}, bf16[1,16,9216]{2,1,0:T(8,128)(2,1)S(1)}, u32[]{:S(2)}, u32[]{:S(2)}) collective-permute-start(bf16[1,16,9216]{2,1,0:T(8,128)(2,1)S(1)} %collective-permute-done.7.refs_0_.rest_8_), channel_id=1, source_target_pairs={{0,2},{1,3},{2,0},{3,1},{12,14},{13,15},{14,12},{15,13},{16,18},{1... | collective-permute-start | bytes 884744 | tf_op jit(solution)/shard_map/ppermute | solution.py:252
  57.0 8.6 %collective-permute-start.12 = (bf16[1,16,9216]{2,1,0:T(8,128)(2,1)S(1)}, bf16[1,16,9216]{2,1,0:T(8,128)(2,1)S(1)}, u32[]{:S(2)}, u32[]{:S(2)}) collective-permute-start(bf16[1,16,9216]{2,1,0:T(8,128)(2,1)S(1)} %collective-permute-done.10.refs_4_.refs_3_.rest_12_), channel_id=1, source_target_pairs={{4,0},{5,1},{6,2},{7,3},{8,12},{9,13},{10,14},{11,15},{20,16},{21,... | collective-permute-start | bytes 884744 | tf_op jit(solution)/shard_map/ppermute | solution.py:252
  59.8 8.0 %collective-permute-start.14 = (bf16[2,16,9216]{2,1,0:T(8,128)(2,1)S(1)}, bf16[2,16,9216]{2,1,0:T(8,128)(2,1)S(1)}, u32[]{:S(2)}, u32[]{:S(2)}) collective-permute-start(bf16[2,16,9216]{2,1,0:T(8,128)(2,1)S(1)} %pick5_6.1), channel_id=1, source_target_pairs={{0,1},{1,0},{2,3},{3,2},{4,5},{5,4},{6,7},{7,6},{8,9},{9,8},{10,11... | collective-permute-start | bytes 1769480 | tf_op jit(solution)/shard_map/ppermute | solution.py:252
  66.2 1.6 %collective-permute-start.15 = (bf16[1,16,9216]{2,1,0:T(8,128)(2,1)S(1)}, bf16[1,16,9216]{2,1,0:T(8,128)(2,1)S(1)}, u32[]{:S(2)}, u32[]{:S(2)}) collective-permute-start(bf16[1,16,9216]{2,1,0:T(8,128)(2,1)S(1)} %pick7.1), channel_id=1, source_target_pairs={{0,1},{1,0},{2,3},{3,2},{4,5},{5,4},{6,7},{7,6},{8,9},{9,8},{10,11... | collective-permute-start | bytes 884744 | tf_op jit(solution)/shard_map/ppermute | solution.py:252

commit v6 on v5

--- a/solution.py
+++ b/solution.py
@@ -80,7 +80,7 @@
             flops=2 * rows * width * wide, bytes_accessed=2 * width * wide, transcendentals=0
         ),
         name=f"base{start}",
-    )(after, *(pltpu.with_memory_space_constraint(a, pltpu.HBM) for a in (tokens, weight)))
+    )(*(pltpu.with_memory_space_constraint(a, pltpu.HBM) for a in (after, tokens, weight)))
 
 
 def finish(choice, tokens, mask, bases, batches, given):

time: 76.6 us -> 76.6 us (level)
  no operation moved by 1% of the time
where the time goes in v6:
time: 76.6 us; the launch traced here: 76.3 us
  Pallas kernels  30.2 us (39%)
  waiting for transfers between devices  22.4 us (29%)
  starting transfers between devices  20.6 us (27%)
  other arithmetic  2.2 us (3%)
    ppermute x16, waiting for transfers between devices, gridded(): send = lambda a, p: lax.ppermute(a, 'store', p)  22.4 us
    ppermute x16, starting transfers between devices, gridded(): send = lambda a, p: lax.ppermute(a, 'store', p)  20.6 us
    pallas_call x2, Pallas kernels, base_part(): pl.pallas_call(kernel, out_shape=jax.ShapeDtypeStruct((rows, wide), jnp.f...  18.4 us
    pallas_call x1, Pallas kernels, finish(): pl.pallas_call(kernel, out_shape=jax.ShapeDtypeStruct((rows, key_width),...  8.26 us
    pallas_call x3, Pallas kernels, picked(): pl.pallas_call(kernel, out_shape=jax.ShapeDtypeStruct((len(ids), rank, wh...  2.49 us
  transfers between devices with their start and end apart: 16, of which 8 were waited for; matrix products, arithmetic and copies ran while one was open for 3% of the time, Pallas kernels for 27%

profile of v6, /device:TPU:0, one launch (start us, length us, event | category | flops | bytes accessed | tf_op | source)
XLA Modules:
  0.0 76.3 jit_solution(16871205148242348320)
XLA Ops:
  0.0 1.1 %join.1.refs_0_.rest_2_ = bf16[2,16,9216]{2,1,0:T(8,128)(2,1)S(1)} custom-call(bf16[2,16,8192]{2,1,0:T(8,128)(2,1)} %shrink.1, bf16[2,16,1024]{2,1,0:T(8,128)(2,1)} %expand.1), custom_call_target="tpu_custom_call" | custom-call | tf_op jit(solution)/shard_map/join/pallas_call | solution.py:181
  1.1 3.0 %collective-permute-start.2 = (bf16[2,16,9216]{2,1,0:T(8,128)(2,1)S(1)}, bf16[2,16,9216]{2,1,0:T(8,128)(2,1)S(1)}, u32[]{:S(2)}, u32[]{:S(2)}) collective-permute-start(bf16[2,16,9216]{2,1,0:T(8,128)(2,1)S(1)} %join.1.refs_0_.rest_2_), channel_id=1, source_target_pairs={{0,2},{1,3},{2,0},{3,1},{4,6},{5,7},{6,4},{7,5},{8,10},{9,11},{10,... | collective-permute-start | bytes 1769480 | tf_op jit(solution)/shard_map/ppermute | solution.py:252
  4.1 0.7 collective-permute-start.1
  4.8 4.4 %collective-permute-start = (bf16[2,16,9216]{2,1,0:T(8,128)(2,1)S(1)}, bf16[2,16,9216]{2,1,0:T(8,128)(2,1)}, u32[]{:S(2)}, u32[]{:S(2)}) collective-permute-start(bf16[2,16,9216]{2,1,0:T(8,128)(2,1)S(1)} %join.1.refs_0_.rest_2_), channel_id=1, source_target_pairs={{0,4},{1,5},{2,6},{3,7},{4,0},{5,1},{6,2},{7,3},{8,12},{9,13},{10,... | collective-permute-start | bytes 1769480 | tf_op jit(solution)/shard_map/ppermute | solution.py:252
  9.4 8.9 %base0.1.rest_0_ = f32[768,512]{1,0:T(8,128)S(1)} custom-call(s32[1,8]{1,0:T(1,128)} %after.2, bf16[768,8192]{1,0:T(8,128)(2,1)} %tokens.5, bf16[8192,1024]{1,0:T(8,128)(2,1)} %weight.3), custom_call_target="tpu_custom_call" | custom-call | flops 6442450944 | bytes 8388608 | tf_op jit(solution)/shard_map/base0/pallas_call | solution.py:68
  18.4 3.7 %collective-permute-done.refs_1_.rest_3_ = bf16[2,16,9216]{2,1,0:T(8,128)(2,1)} collective-permute-done((bf16[2,16,9216]{2,1,0:T(8,128)(2,1)S(1)}, bf16[2,16,9216]{2,1,0:T(8,128)(2,1)}, u32[]{:S(2)}, u32[]{:S(2)}) %collective-permute-start) | collective-permute-done | bytes 589856 | tf_op jit(solution)/shard_map/ppermute | solution.py:252
  22.1 0.2 select_reduce_fusion.3
  22.4 0.1 select_reduce_fusion.2
  22.8 1.3 %broadcast_select_fusion.1 = (bf16[2,16,9216]{2,1,0:T(8,128)(2,1)S(1)}, bf16[2,16,9216]{2,1,0:T(8,128)(2,1)S(1)}) fusion(bf16[2,16,9216]{2,1,0:T(8,128)(2,1)S(1)} %collective-permute-done.1.refs_5_.rest_7_, bf16[2,16,9216]{2,1,0:T(8,128)(2,1)} %collective-permute-done.refs_1_.rest_3_, pred[]{:T(512)S(6)} %or.3, ...), kind=kLoop, calls=%fused_computation.2 | loop fusion | flops 589824 | bytes 2949121 | tf_op jit(solution)/shard_map/jit(_where)/select_n | solution.py:263
  24.1 0.6 collective-permute-start.3
  24.7 0.5 collective-permute-start.4
  25.2 0.8 %collective-permute-start.5 = (bf16[2,16,9216]{2,1,0:T(8,128)(2,1)}, bf16[2,16,9216]{2,1,0:T(8,128)(2,1)S(1)}, u32[]{:S(2)}, u32[]{:S(2)}) collective-permute-start(bf16[2,16,9216]{2,1,0:T(8,128)(2,1)} %collective-permute-done.refs_1_.rest_3_), channel_id=1, source_target_pairs={{4,8},{5,9},{6,10},{7,11},{8,4},{9,5},{10,6},{11,7},{20,24},{21,25... | collective-permute-start | bytes 1769480 | tf_op jit(solution)/shard_map/ppermute | solution.py:252
  26.1 9.4 %base512.1.rest_1_ = f32[768,512]{1,0:T(8,128)S(1)} custom-call(s32[1,8]{1,0:T(1,128)} %after.2, bf16[768,8192]{1,0:T(8,128)(2,1)} %tokens.5, bf16[8192,1024]{1,0:T(8,128)(2,1)} %weight.3), custom_call_target="tpu_custom_call" | custom-call | flops 6442450944 | bytes 8388608 | tf_op jit(solution)/shard_map/base512/pallas_call | solution.py:68
  35.5 0.2 compare_convert_fusion.mask
  35.7 0.2 select_reduce_fusion
  36.0 4.0 %collective-permute-done.3.refs_4_.rest_6_ = bf16[2,16,9216]{2,1,0:T(8,128)(2,1)S(1)} collective-permute-done((bf16[2,16,9216]{2,1,0:T(8,128)(2,1)S(1)}, bf16[2,16,9216]{2,1,0:T(8,128)(2,1)S(1)}, u32[]{:S(2)}, u32[]{:S(2)}) %collective-permute-start.3) | collective-permute-done | bytes 589856 | tf_op jit(solution)/shard_map/ppermute | solution.py:252
  39.9 0.3 collective-permute-done.4.refs_3_.refs_5_.rest_5_
  40.3 1.3 %collective-permute-start.7 = (bf16[1,16,9216]{2,1,0:T(8,128)(2,1)S(1)}, bf16[1,16,9216]{2,1,0:T(8,128)(2,1)S(1)}, u32[]{:S(2)}, u32[]{:S(2)}) collective-permute-start(bf16[1,16,9216]{2,1,0:T(8,128)(2,1)S(1)} %get-tuple-element.50), channel_id=1, source_target_pairs={{4,0},{5,1},{6,2},{7,3},{8,12},{9,13},{10,14},{11,15},{20,16},{21,... | collective-permute-start | bytes 884744 | tf_op jit(solution)/shard_map/ppermute | solution.py:252
  41.6 1.3 %pick0_1_2_3_4.1 = bf16[5,16,9216]{2,1,0:T(8,128)(2,1)S(1)} custom-call(s32[9]{0:T(128)S(1)} %get-tuple-element.42.choice, bf16[2,16,9216]{2,1,0:T(8,128)(2,1)S(1)} %join.1.refs_0_.rest_2_, bf16[2,16,9216]{2,1,0:T(8,128)(2,1)} %collective-permute-done.refs_1_.rest_3_, bf16[2,16,9216]{2,1,0:T(8,128)(2,1)S(1)} %collective-permute-done.2.refs_2_.rest_4_, ...), custom_call_target="tpu_custom_call" | custom-call | tf_op jit(solution)/shard_map/pick0_1_2_3_4/pallas_call | solution.py:224
  43.0 0.6 collective-permute-start.10
  43.6 1.3 %collective-permute-start.8 = (bf16[1,16,9216]{2,1,0:T(8,128)(2,1)S(1)}, bf16[1,16,9216]{2,1,0:T(8,128)(2,1)S(1)}, u32[]{:S(2)}, u32[]{:S(2)}) collective-permute-start(bf16[1,16,9216]{2,1,0:T(8,128)(2,1)S(1)} %get-tuple-element.49), channel_id=1, source_target_pairs={{4,0},{5,1},{6,2},{7,3},{8,12},{9,13},{10,14},{11,15},{20,16},{21,... | collective-permute-start | bytes 884744 | tf_op jit(solution)/shard_map/ppermute | solution.py:252
  44.9 1.6 %collective-permute-start.9 = (bf16[1,16,9216]{2,1,0:T(8,128)(2,1)S(1)}, bf16[1,16,9216]{2,1,0:T(8,128)(2,1)S(1)}, u32[]{:S(2)}, u32[]{:S(2)}) collective-permute-start(bf16[1,16,9216]{2,1,0:T(8,128)(2,1)S(1)} %get-tuple-element.48), channel_id=1, source_target_pairs={{0,2},{1,3},{2,0},{3,1},{4,6},{5,7},{6,4},{7,5},{8,10},{9,11},{10,... | collective-permute-start | bytes 884744 | tf_op jit(solution)/shard_map/ppermute | solution.py:252
  46.4 6.3 %collective-permute-done.7.refs_0_.rest_8_ = bf16[1,16,9216]{2,1,0:T(8,128)(2,1)S(1)} collective-permute-done((bf16[1,16,9216]{2,1,0:T(8,128)(2,1)S(1)}, bf16[1,16,9216]{2,1,0:T(8,128)(2,1)S(1)}, u32[]{:S(2)}, u32[]{:S(2)}) %collective-permute-start.7) | collective-permute-done | bytes 294944 | tf_op jit(solution)/shard_map/ppermute | solution.py:252
  52.7 4.3 %collective-permute-start.11 = (bf16[1,16,9216]{2,1,0:T(8,128)(2,1)S(1)}, bf16[1,16,9216]{2,1,0:T(8,128)(2,1)S(1)}, u32[]{:S(2)}, u32[]{:S(2)}) collective-permute-start(bf16[1,16,9216]{2,1,0:T(8,128)(2,1)S(1)} %collective-permute-done.7.refs_0_.rest_8_), channel_id=1, source_target_pairs={{0,2},{1,3},{2,0},{3,1},{12,14},{13,15},{14,12},{15,13},{16,18},{1... | collective-permute-start | bytes 884744 | tf_op jit(solution)/shard_map/ppermute | solution.py:252
  57.0 1.3 %collective-permute-start.12 = (bf16[1,16,9216]{2,1,0:T(8,128)(2,1)S(1)}, bf16[1,16,9216]{2,1,0:T(8,128)(2,1)S(1)}, u32[]{:S(2)}, u32[]{:S(2)}) collective-permute-start(bf16[1,16,9216]{2,1,0:T(8,128)(2,1)S(1)} %collective-permute-done.10.refs_4_.refs_3_.rest_12_), channel_id=1, source_target_pairs={{4,0},{5,1},{6,2},{7,3},{8,12},{9,13},{10,14},{11,15},{20,16},{21,... | collective-permute-start | bytes 884744 | tf_op jit(solution)/shard_map/ppermute | solution.py:252
  58.3 0.9 %collective-permute-done.9.refs_3_.refs_2_.rest_11_ = bf16[1,16,9216]{2,1,0:T(8,128)(2,1)S(1)} collective-permute-done((bf16[1,16,9216]{2,1,0:T(8,128)(2,1)S(1)}, bf16[1,16,9216]{2,1,0:T(8,128)(2,1)S(1)}, u32[]{:S(2)}, u32[]{:S(2)}) %collective-permute-start.9) | collective-permute-done | bytes 294944 | tf_op jit(solution)/shard_map/ppermute | solution.py:252
  59.2 0.6 pick5_6.1
  59.9 5.2 %collective-permute-done.11.refs_0_.rest_13_ = bf16[1,16,9216]{2,1,0:T(8,128)(2,1)S(1)} collective-permute-done((bf16[1,16,9216]{2,1,0:T(8,128)(2,1)S(1)}, bf16[1,16,9216]{2,1,0:T(8,128)(2,1)S(1)}, u32[]{:S(2)}, u32[]{:S(2)}) %collective-permute-start.11) | collective-permute-done | bytes 294944 | tf_op jit(solution)/shard_map/ppermute | solution.py:252
  65.1 0.5 collective-permute-done.12.refs_1_.rest_14_
  65.6 0.6 pick7.1
  66.3 1.6 %collective-permute-done.15.rest_17_ = bf16[1,16,9216]{2,1,0:T(8,128)(2,1)S(1)} collective-permute-done((bf16[1,16,9216]{2,1,0:T(8,128)(2,1)S(1)}, bf16[1,16,9216]{2,1,0:T(8,128)(2,1)S(1)}, u32[]{:S(2)}, u32[]{:S(2)}) %collective-permute-start.15) | collective-permute-done | bytes 294944 | tf_op jit(solution)/shard_map/ppermute | solution.py:252
  67.9 8.3 %shrink_expand.1 = bf16[768,1024]{1,0:T(8,128)(2,1)} custom-call(s32[9]{0:T(128)S(1)} %get-tuple-element.35.choice, bf16[768,8192]{1,0:T(8,128)(2,1)S(1)} %bitcast.12, bf16[768,256]{1,0:T(8,128)(2,1)S(1)} %compare_convert_fusion.mask, f32[768,512]{1,0:T(8,128)S(1)} %base0.1.rest_0_, f32[768,512]{1,0:T(8,128)S(1)} %base512.1.rest_1_, ...), custom_call_target="tpu_custom_call" | custom-call | flops 3221225472 | bytes 4718592 | tf_op jit(solution)/shard_map/shrink_expand/pallas_call | solution.py:144
  (38 shorter events, 1.1 us)
Async XLA Ops:
  1.1 17.3 %collective-permute-start.2 = (bf16[2,16,9216]{2,1,0:T(8,128)(2,1)S(1)}, bf16[2,16,9216]{2,1,0:T(8,128)(2,1)S(1)}, u32[]{:S(2)}, u32[]{:S(2)}) collective-permute-start(bf16[2,16,9216]{2,1,0:T(8,128)(2,1)S(1)} %join.1.refs_0_.rest_2_), channel_id=1, source_target_pairs={{0,2},{1,3},{2,0},{3,1},{4,6},{5,7},{6,4},{7,5},{8,10},{9,11},{10,... | collective-permute-start | bytes 1769480 | tf_op jit(solution)/shard_map/ppermute | solution.py:252
  4.1 14.2 %collective-permute-start.1 = (bf16[2,16,9216]{2,1,0:T(8,128)(2,1)S(1)}, bf16[2,16,9216]{2,1,0:T(8,128)(2,1)S(1)}, u32[]{:S(2)}, u32[]{:S(2)}) collective-permute-start(bf16[2,16,9216]{2,1,0:T(8,128)(2,1)S(1)} %join.1.refs_0_.rest_2_), channel_id=1, source_target_pairs={{4,8},{5,9},{6,10},{7,11},{8,4},{9,5},{10,6},{11,7},{20,24},{21,25... | collective-permute-start | bytes 1769480 | tf_op jit(solution)/shard_map/ppermute | solution.py:252
  4.8 17.3 %collective-permute-start = (bf16[2,16,9216]{2,1,0:T(8,128)(2,1)S(1)}, bf16[2,16,9216]{2,1,0:T(8,128)(2,1)}, u32[]{:S(2)}, u32[]{:S(2)}) collective-permute-start(bf16[2,16,9216]{2,1,0:T(8,128)(2,1)S(1)} %join.1.refs_0_.rest_2_), channel_id=1, source_target_pairs={{0,4},{1,5},{2,6},{3,7},{4,0},{5,1},{6,2},{7,3},{8,12},{9,13},{10,... | collective-permute-start | bytes 1769480 | tf_op jit(solution)/shard_map/ppermute | solution.py:252
  9.4 12.7 %copy-start = (s32[1,8]{1,0:T(1,128)S(1)}, s32[1,8]{1,0:T(1,128)}, u32[]{:S(2)}) copy-start(s32[1,8]{1,0:T(1,128)} %after.2) | copy-start | bytes 100
  9.4 12.7 %copy-start.2 = (s32[32]{0:T(128)S(1)}, s32[32]{0:T(128)}, u32[]{:S(2)}) copy-start(s32[32]{0:T(128)} %param.11) | copy-start | bytes 388
  9.4 13.2 %copy-start.1 = (s32[1,48]{1,0:T(1,128)S(1)}, s32[1,48]{1,0:T(1,128)}, u32[]{:S(2)}) copy-start(s32[1,48]{1,0:T(1,128)} %param.13) | copy-start | bytes 580
  22.3 13.4 %collective-permute-start.6 = (s32[8]{0:T(128)S(1)}, s32[8]{0:T(128)S(1)}, u32[]{:S(2)}, u32[]{:S(2)}) collective-permute-start(s32[8]{0:T(128)S(1)} %select_reduce_fusion.3), channel_id=1, source_target_pairs={{0,1},{1,0},{2,3},{3,2},{4,5},{5,4},{6,7},{7,6},{8,9},{9,8},{10,11... | collective-permute-start | bytes 104 | tf_op jit(solution)/shard_map/ppermute | solution.py:252
  22.8 45.1 %slice-start = ((s8[12582912]{0:T(1024)(128)(4,1)}), s8[4194304]{0:T(1024)(128)(4,1)S(1)}, s32[]{:S(2)}) async-start(s8[12582912]{0:T(1024)(128)(4,1)} %bitcast.11), calls=%async_computation | async-start | bytes 8388608
  24.1 43.8 %slice-start.1 = ((s8[12582912]{0:T(1024)(128)(4,1)}), s8[4194304]{0:T(1024)(128)(4,1)S(1)}, s32[]{:S(2)}) async-start(s8[12582912]{0:T(1024)(128)(4,1)} %bitcast.11), calls=%async_computation.1 | async-start | bytes 8388608
  24.1 43.8 %slice-start.2 = ((s8[12582912]{0:T(1024)(128)(4,1)}), s8[4194304]{0:T(1024)(128)(4,1)S(1)}, s32[]{:S(2)}) async-start(s8[12582912]{0:T(1024)(128)(4,1)} %bitcast.11), calls=%async_computation.2 | async-start | bytes 8388608
  24.1 15.8 %collective-permute-start.3 = (bf16[2,16,9216]{2,1,0:T(8,128)(2,1)S(1)}, bf16[2,16,9216]{2,1,0:T(8,128)(2,1)S(1)}, u32[]{:S(2)}, u32[]{:S(2)}) collective-permute-start(bf16[2,16,9216]{2,1,0:T(8,128)(2,1)S(1)} %get-tuple-element.28), channel_id=1, source_target_pairs={{0,4},{1,5},{2,6},{3,7},{4,0},{5,1},{6,2},{7,3},{8,12},{9,13},{10,... | collective-permute-start | bytes 1769480 | tf_op jit(solution)/shard_map/ppermute | solution.py:252
  24.7 15.4 %collective-permute-start.4 = (bf16[2,16,9216]{2,1,0:T(8,128)(2,1)S(1)}, bf16[2,16,9216]{2,1,0:T(8,128)(2,1)S(1)}, u32[]{:S(2)}, u32[]{:S(2)}) collective-permute-start(bf16[2,16,9216]{2,1,0:T(8,128)(2,1)S(1)} %get-tuple-element.29), channel_id=1, source_target_pairs={{0,2},{1,3},{2,0},{3,1},{4,6},{5,7},{6,4},{7,5},{8,10},{9,11},{10,... | collective-permute-start | bytes 1769480 | tf_op jit(solution)/shard_map/ppermute | solution.py:252
  25.2 14.9 %collective-permute-start.5 = (bf16[2,16,9216]{2,1,0:T(8,128)(2,1)}, bf16[2,16,9216]{2,1,0:T(8,128)(2,1)S(1)}, u32[]{:S(2)}, u32[]{:S(2)}) collective-permute-start(bf16[2,16,9216]{2,1,0:T(8,128)(2,1)} %collective-permute-done.refs_1_.rest_3_), channel_id=1, source_target_pairs={{4,8},{5,9},{6,10},{7,11},{8,4},{9,5},{10,6},{11,7},{20,24},{21,25... | collective-permute-start | bytes 1769480 | tf_op jit(solution)/shard_map/ppermute | solution.py:252
  40.3 12.4 %collective-permute-start.7 = (bf16[1,16,9216]{2,1,0:T(8,128)(2,1)S(1)}, bf16[1,16,9216]{2,1,0:T(8,128)(2,1)S(1)}, u32[]{:S(2)}, u32[]{:S(2)}) collective-permute-start(bf16[1,16,9216]{2,1,0:T(8,128)(2,1)S(1)} %get-tuple-element.50), channel_id=1, source_target_pairs={{4,0},{5,1},{6,2},{7,3},{8,12},{9,13},{10,14},{11,15},{20,16},{21,... | collective-permute-start | bytes 884744 | tf_op jit(solution)/shard_map/ppermute | solution.py:252
  42.9 25.0 %collective-permute-start.13 = (bf16[5,16,9216]{2,1,0:T(8,128)(2,1)S(1)}, bf16[5,16,9216]{2,1,0:T(8,128)(2,1)S(1)}, u32[]{:S(2)}, u32[]{:S(2)}) collective-permute-start(bf16[5,16,9216]{2,1,0:T(8,128)(2,1)S(1)} %pick0_1_2_3_4.1), channel_id=1, source_target_pairs={{0,1},{1,0},{2,3},{3,2},{4,5},{5,4},{6,7},{7,6},{8,9},{9,8},{10,11... | collective-permute-start | bytes 4423688 | tf_op jit(solution)/shard_map/ppermute | solution.py:252
  43.0 14.0 %collective-permute-start.10 = (bf16[1,16,9216]{2,1,0:T(8,128)(2,1)S(1)}, bf16[1,16,9216]{2,1,0:T(8,128)(2,1)S(1)}, u32[]{:S(2)}, u32[]{:S(2)}) collective-permute-start(bf16[1,16,9216]{2,1,0:T(8,128)(2,1)S(1)} %get-tuple-element.47), channel_id=1, source_target_pairs={{0,2},{1,3},{2,0},{3,1},{4,6},{5,7},{6,4},{7,5},{8,10},{9,11},{10,... | collective-permute-start | bytes 884744 | tf_op jit(solution)/shard_map/ppermute | solution.py:252
  43.6 14.7 %collective-permute-start.8 = (bf16[1,16,9216]{2,1,0:T(8,128)(2,1)S(1)}, bf16[1,16,9216]{2,1,0:T(8,128)(2,1)S(1)}, u32[]{:S(2)}, u32[]{:S(2)}) collective-permute-start(bf16[1,16,9216]{2,1,0:T(8,128)(2,1)S(1)} %get-tuple-element.49), channel_id=1, source_target_pairs={{4,0},{5,1},{6,2},{7,3},{8,12},{9,13},{10,14},{11,15},{20,16},{21,... | collective-permute-start | bytes 884744 | tf_op jit(solution)/shard_map/ppermute | solution.py:252
  44.9 14.3 %collective-permute-start.9 = (bf16[1,16,9216]{2,1,0:T(8,128)(2,1)S(1)}, bf16[1,16,9216]{2,1,0:T(8,128)(2,1)S(1)}, u32[]{:S(2)}, u32[]{:S(2)}) collective-permute-start(bf16[1,16,9216]{2,1,0:T(8,128)(2,1)S(1)} %get-tuple-element.48), channel_id=1, source_target_pairs={{0,2},{1,3},{2,0},{3,1},{4,6},{5,7},{6,4},{7,5},{8,10},{9,11},{10,... | collective-permute-start | bytes 884744 | tf_op jit(solution)/shard_map/ppermute | solution.py:252
  52.7 12.4 %collective-permute-start.11 = (bf16[1,16,9216]{2,1,0:T(8,128)(2,1)S(1)}, bf16[1,16,9216]{2,1,0:T(8,128)(2,1)S(1)}, u32[]{:S(2)}, u32[]{:S(2)}) collective-permute-start(bf16[1,16,9216]{2,1,0:T(8,128)(2,1)S(1)} %collective-permute-done.7.refs_0_.rest_8_), channel_id=1, source_target_pairs={{0,2},{1,3},{2,0},{3,1},{12,14},{13,15},{14,12},{15,13},{16,18},{1... | collective-permute-start | bytes 884744 | tf_op jit(solution)/shard_map/ppermute | solution.py:252
  57.0 8.6 %collective-permute-start.12 = (bf16[1,16,9216]{2,1,0:T(8,128)(2,1)S(1)}, bf16[1,16,9216]{2,1,0:T(8,128)(2,1)S(1)}, u32[]{:S(2)}, u32[]{:S(2)}) collective-permute-start(bf16[1,16,9216]{2,1,0:T(8,128)(2,1)S(1)} %collective-permute-done.10.refs_4_.refs_3_.rest_12_), channel_id=1, source_target_pairs={{4,0},{5,1},{6,2},{7,3},{8,12},{9,13},{10,14},{11,15},{20,16},{21,... | collective-permute-start | bytes 884744 | tf_op jit(solution)/shard_map/ppermute | solution.py:252
  59.8 8.0 %collective-permute-start.14 = (bf16[2,16,9216]{2,1,0:T(8,128)(2,1)S(1)}, bf16[2,16,9216]{2,1,0:T(8,128)(2,1)S(1)}, u32[]{:S(2)}, u32[]{:S(2)}) collective-permute-start(bf16[2,16,9216]{2,1,0:T(8,128)(2,1)S(1)} %pick5_6.1), channel_id=1, source_target_pairs={{0,1},{1,0},{2,3},{3,2},{4,5},{5,4},{6,7},{7,6},{8,9},{9,8},{10,11... | collective-permute-start | bytes 1769480 | tf_op jit(solution)/shard_map/ppermute | solution.py:252
  66.2 1.6 %collective-permute-start.15 = (bf16[1,16,9216]{2,1,0:T(8,128)(2,1)S(1)}, bf16[1,16,9216]{2,1,0:T(8,128)(2,1)S(1)}, u32[]{:S(2)}, u32[]{:S(2)}) collective-permute-start(bf16[1,16,9216]{2,1,0:T(8,128)(2,1)S(1)} %pick7.1), channel_id=1, source_target_pairs={{0,1},{1,0},{2,3},{3,2},{4,5},{5,4},{6,7},{7,6},{8,9},{9,8},{10,11... | collective-permute-start | bytes 884744 | tf_op jit(solution)/shard_map/ppermute | solution.py:252
